TPU v7x, 32 devices: a whole 2x2x4 slice. The times are simulated.
32 devices in a mesh: seq: 8 (over z, x), fsdp: 4 (over y, core).
Axes of the slice: x: 2, y: 2, z: 4, core: 2. Of those that a mesh axis runs over, the one named last changes fastest.
Arguments:
- tokens: bfloat16 [3, 4, 2048, 1024], P(None, 'fsdp', 'seq'), may hold values from -6 to 6
- memory: bfloat16 [3, 4, 256, 1024], P(None, 'fsdp', 'seq'), may hold values from -6 to 6
- cotangent: bfloat16 [3, 4, 2048, 1024], P(None, 'fsdp', 'seq'), may hold values from -6 to 6
- tile_segment: int32 [3, 4, 16], P(None, 'fsdp'), may hold values from 0 to 12, as said below
- parents: int32 [3, 4, 13], P(None, 'fsdp'), may hold values from 0 to 11, as said below
- memory_lengths: int32 [3, 4], P(None, 'fsdp'), may hold values from 64 to 256, as said below
- self_qkv: bfloat16 [1024, 3072], P(('seq', 'fsdp')), may hold values from -0.1875 to 0.1875
- self_out: bfloat16 [1024, 1024], P(('seq', 'fsdp')), may hold values from -3 to 3
- cross_q: bfloat16 [1024, 1024], P(('seq', 'fsdp')), may hold values from -0.1875 to 0.1875
- cross_kv: bfloat16 [1024, 2048], P(('seq', 'fsdp')), may hold values from -0.1875 to 0.1875
- cross_out: bfloat16 [1024, 1024], P(('seq', 'fsdp')), may hold values from -3 to 3
- ffn_in: bfloat16 [1024, 4096], P(('seq', 'fsdp')), may hold values from -0.1875 to 0.1875
- ffn_out: bfloat16 [4096, 1024], P(('seq', 'fsdp')), may hold values from -0.1875 to 0.1875
- norm_gain: bfloat16 [3, 1024], P(None, ('seq', 'fsdp')), may hold values from 0.5 to 1.5
- norm_bias: bfloat16 [3, 1024], P(None, ('seq', 'fsdp')), may hold values from -1.75 to 1.75
Outputs:
- output: bfloat16 [3, 4, 2048, 1024], P(None, 'fsdp', 'seq')
- grad_tokens: bfloat16 [3, 4, 2048, 1024], P(None, 'fsdp', 'seq')
- grad_memory: bfloat16 [3, 4, 256, 1024], P(None, 'fsdp', 'seq')
- grad_self_qkv: float32 [1024, 3072], P(('seq', 'fsdp'))
- grad_self_out: float32 [1024, 1024], P(('seq', 'fsdp'))
- grad_cross_q: float32 [1024, 1024], P(('seq', 'fsdp'))
- grad_cross_kv: float32 [1024, 2048], P(('seq', 'fsdp'))
- grad_cross_out: float32 [1024, 1024], P(('seq', 'fsdp'))
- grad_ffn_in: float32 [1024, 4096], P(('seq', 'fsdp'))
- grad_ffn_out: float32 [4096, 1024], P(('seq', 'fsdp'))
- grad_norm_gain: float32 [3, 1024], P(None, ('seq', 'fsdp'))
- grad_norm_bias: float32 [3, 1024], P(None, ('seq', 'fsdp'))
Inputs may be any that keep to these rules, and one draw needn't show every extreme that they name: `tile_segment`: 0 on the first 4 tiles (the trunk), 1 on tile 16 // 4, then never falling and rising by at most one from tile to tile; in some sequence every later tile starts a new segment. `parents`: the parent of segment s >= 1 is an earlier segment; the parent of segment 0 is 0. `memory_lengths`: some sequence of every draw has all 256 rows valid.
All inputs are finite; a program needn't handle non-finite values.
Results may differ from a plain program's by a relative error of at most 0.02.
Values may be sent and summed in bfloat16 or wider, within the bound.
A program may use at most 200 MiB of HBM per device.

v0:
```python
import jax
import jax.numpy as jnp
from jax import lax
from jax.sharding import PartitionSpec as P

H = 16
HD = 64
TILE = 128


scale_factor = 0.125
residual_weight = 36.0**0.25
norm_epsilon = 1e-05
masked_score = -1e30


def layer_norm(incoming, gain_row, bias_row):
    row_mean = jnp.mean(incoming, -1, keepdims=True)
    centred = incoming - row_mean
    variance = jnp.mean(centred * centred, -1, keepdims=True)
    return centred * lax.rsqrt(variance + norm_epsilon) * gain_row + bias_row


def smooth_gelu(incoming):
    return jax.nn.gelu(incoming, approximate=True)


def outer_sum(left_side, right_side):
    return lax.dot_general(
        left_side, right_side, (((0,), (0,)), ((), ())), preferred_element_type=jnp.float32
    )


def back_project(gradient, weight):
    return lax.dot_general(
        gradient, weight, (((1,), (1,)), ((), ())), preferred_element_type=jnp.float32
    )


def ancestors(parent_ids):
    segment_ids = jnp.arange(parent_ids.shape[0], dtype=jnp.int32)
    start_table = (segment_ids[:, None] == segment_ids[None, :]).astype(jnp.float32)

    def advance(position, loop_state):
        current, ancestry = loop_state
        current = parent_ids[current]
        found = (current[:, None] == segment_ids[None, :]).astype(jnp.float32)
        return (current, jnp.maximum(ancestry, found))

    final_state = lax.fori_loop(0, parent_ids.shape[0], advance, (segment_ids, start_table))
    return final_state[1]


def tree_mask(tile_segments, parent_ids, first_row, row_count, key_count):
    token_segment = jnp.repeat(tile_segments, TILE)
    ancestry = ancestors(parent_ids)
    segment_table = (
        token_segment[:, None] == jnp.arange(parent_ids.shape[0], dtype=jnp.int32)[None, :]
    ).astype(jnp.float32)
    query_table = lax.dynamic_slice_in_dim(segment_table, first_row, row_count, 0)
    query_ancestry = jnp.dot(query_table, ancestry)
    related = lax.dot_general(query_ancestry, segment_table, (((1,), (1,)), ((), ()))) > 0.5
    query_place = first_row + jnp.arange(row_count, dtype=jnp.int32)
    key_place = jnp.arange(key_count, dtype=jnp.int32)
    return jnp.logical_and(related, key_place[None, :] <= query_place[:, None])


def head_split(array):
    return array.reshape(array.shape[0], 4, array.shape[1] // 4).transpose(1, 0, 2)


def head_join(array):
    return array.transpose(1, 0, 2).reshape(array.shape[1], array.shape[0] * array.shape[2])


def attend_forward(queries, key_rows, value_rows, allowed):
    row_count = queries.shape[0]
    head_count = H // 4

    def one_group(group_items):
        query_part, key_part, value_part = group_items
        query_heads = query_part.reshape(row_count, head_count, HD)
        key_heads = key_part.reshape(key_part.shape[0], head_count, HD)
        value_heads = value_part.reshape(value_part.shape[0], head_count, HD)
        scores = (
            jnp.einsum("qhd,khd->hqk", query_heads, key_heads, preferred_element_type=jnp.float32)
            * scale_factor
        )
        scores = jnp.where(allowed[None], scores, masked_score)
        row_max = jnp.max(scores, -1, keepdims=True)
        exp_scores = jnp.where(allowed[None], jnp.exp(scores - row_max), 0.0)
        row_total = jnp.sum(exp_scores, -1, keepdims=True)
        soft_max = (exp_scores / row_total).astype(jnp.bfloat16)
        mixed = jnp.einsum(
            "hqk,khd->qhd", soft_max, value_heads, preferred_element_type=jnp.float32
        )
        return (mixed.reshape(row_count, head_count * HD), (row_max + jnp.log(row_total))[..., 0])

    group_parts = lax.map(
        one_group, (head_split(queries), head_split(key_rows), head_split(value_rows))
    )
    return (head_join(group_parts[0]), group_parts[1])


def attend_backward(queries, key_rows, value_rows, allowed, log_total, grad_out):
    row_count = queries.shape[0]
    head_count = H // 4

    def one_group(group_items):
        query_part, key_part, value_part, total_part, grad_part = group_items
        key_count = key_part.shape[0]
        query_heads = query_part.reshape(row_count, head_count, HD)
        key_heads = key_part.reshape(key_count, head_count, HD)
        value_heads = value_part.reshape(key_count, head_count, HD)
        grad_heads = grad_part.reshape(row_count, head_count, HD)
        scores = (
            jnp.einsum("qhd,khd->hqk", query_heads, key_heads, preferred_element_type=jnp.float32)
            * scale_factor
        )
        soft_max = jnp.where(allowed[None], jnp.exp(scores - total_part[..., None]), 0.0)
        grad_probs = jnp.einsum(
            "qhd,khd->hqk", grad_heads, value_heads, preferred_element_type=jnp.float32
        )
        row_delta = jnp.sum(soft_max * grad_probs, -1, keepdims=True)
        grad_scores = (soft_max * (grad_probs - row_delta)).astype(jnp.bfloat16)
        grad_query = (
            jnp.einsum("hqk,khd->qhd", grad_scores, key_heads, preferred_element_type=jnp.float32)
            * scale_factor
        )
        results = (grad_query.reshape(row_count, head_count * HD), row_delta[..., 0])
        grad_key = (
            jnp.einsum("hqk,qhd->khd", grad_scores, query_heads, preferred_element_type=jnp.float32)
            * scale_factor
        )
        grad_value = jnp.einsum(
            "hqk,qhd->khd",
            soft_max.astype(jnp.bfloat16),
            grad_heads,
            preferred_element_type=jnp.float32,
        )
        results = results + (
            grad_key.reshape(key_count, head_count * HD),
            grad_value.reshape(key_count, head_count * HD),
        )
        return results

    group_parts = lax.map(
        one_group,
        (
            head_split(queries),
            head_split(key_rows),
            head_split(value_rows),
            log_total,
            head_split(grad_out),
        ),
    )
    return (
        head_join(group_parts[0]),
        group_parts[1],
        head_join(group_parts[2]),
        head_join(group_parts[3]),
    )


def per_device(
    tokens,
    memory,
    cotangent,
    tile_segment,
    parents,
    memory_lengths,
    self_qkv,
    self_out,
    cross_q,
    cross_kv,
    cross_out,
    ffn_in,
    ffn_out,
    norm_gain,
    norm_bias,
):
    micro_count = tokens.shape[0]
    row_count = tokens.shape[2]
    width = tokens.shape[3]
    device_count = lax.axis_size(("seq", "fsdp"))
    first_row = lax.axis_index("seq") * row_count
    row_shards = (self_qkv, self_out, cross_q, cross_kv, cross_out, ffn_in, ffn_out)
    totals = tuple(
        (
            jnp.zeros((shard.shape[0] * device_count, shard.shape[1]), jnp.float32)
            for shard in row_shards
        )
    )
    totals = totals + (jnp.zeros((3, width), jnp.float32), jnp.zeros((3, width), jnp.float32))
    outputs = []
    grad_token_list = []
    grad_memory_list = []
    for micro_index in range(micro_count):
        gathered = (
            lax.all_gather(self_qkv, ("seq", "fsdp"), axis=0, tiled=True),
            lax.all_gather(self_out, ("seq", "fsdp"), axis=0, tiled=True),
            lax.all_gather(cross_q, ("seq", "fsdp"), axis=0, tiled=True),
            lax.all_gather(cross_kv, ("seq", "fsdp"), axis=0, tiled=True),
            lax.all_gather(cross_out, ("seq", "fsdp"), axis=0, tiled=True),
            lax.all_gather(ffn_in, ("seq", "fsdp"), axis=0, tiled=True),
            lax.all_gather(ffn_out, ("seq", "fsdp"), axis=0, tiled=True),
            lax.all_gather(norm_gain, ("seq", "fsdp"), axis=1, tiled=True),
            lax.all_gather(norm_bias, ("seq", "fsdp"), axis=1, tiled=True),
        )
        (
            joint_weight,
            self_output,
            cross_weight,
            pair_weight,
            cross_output,
            upward_weight,
            down_weight,
            gain_low,
            bias_low,
        ) = gathered
        gain_rows = gain_low.astype(jnp.float32)
        bias_rows = bias_low.astype(jnp.float32)
        token_rows = tokens[micro_index, 0]
        memory_rows = memory[micro_index, 0]
        projected = jnp.dot(token_rows, joint_weight, preferred_element_type=jnp.float32).astype(
            jnp.bfloat16
        )
        memory_pairs = jnp.dot(memory_rows, pair_weight, preferred_element_type=jnp.float32).astype(
            jnp.bfloat16
        )
        sequence_pairs, gathered_memory = (
            lax.all_gather(projected[:, width:], "seq", axis=0, tiled=True),
            lax.all_gather(memory_pairs, "seq", axis=0, tiled=True),
        )
        query_rows = projected[:, :width]
        key_rows = sequence_pairs[:, :width]
        value_rows = sequence_pairs[:, width:]
        memory_keys = gathered_memory[:, :width]
        memory_values = gathered_memory[:, width:]
        sequence_length = key_rows.shape[0]
        allowed = tree_mask(
            tile_segment[micro_index, 0],
            parents[micro_index, 0],
            first_row,
            row_count,
            sequence_length,
        )
        memory_valid = (
            jnp.arange(memory_keys.shape[0], dtype=jnp.int32) < memory_lengths[micro_index, 0]
        )
        memory_allowed = jnp.broadcast_to(memory_valid[None, :], (row_count, memory_keys.shape[0]))
        attended_full, self_total = attend_forward(query_rows, key_rows, value_rows, allowed)
        attended = attended_full.astype(jnp.bfloat16)
        mixed_first = residual_weight * token_rows.astype(jnp.float32) + jnp.dot(
            attended, self_output, preferred_element_type=jnp.float32
        )
        hidden_first = layer_norm(mixed_first, gain_rows[0], bias_rows[0])
        hidden_first_low = hidden_first.astype(jnp.bfloat16)
        cross_query = jnp.dot(
            hidden_first_low, cross_weight, preferred_element_type=jnp.float32
        ).astype(jnp.bfloat16)
        cross_full, cross_total = attend_forward(
            cross_query, memory_keys, memory_values, memory_allowed
        )
        cross_attended = cross_full.astype(jnp.bfloat16)
        mixed_second = residual_weight * hidden_first + jnp.dot(
            cross_attended, cross_output, preferred_element_type=jnp.float32
        )
        hidden_second = layer_norm(mixed_second, gain_rows[1], bias_rows[1])
        hidden_second_low = hidden_second.astype(jnp.bfloat16)
        pre_active = jnp.dot(hidden_second_low, upward_weight, preferred_element_type=jnp.float32)
        active = smooth_gelu(pre_active).astype(jnp.bfloat16)
        mixed_third = residual_weight * hidden_second + jnp.dot(
            active, down_weight, preferred_element_type=jnp.float32
        )
        outputs.append(layer_norm(mixed_third, gain_rows[2], bias_rows[2]).astype(jnp.bfloat16))
        gathered = (
            lax.all_gather(self_qkv, ("seq", "fsdp"), axis=0, tiled=True),
            lax.all_gather(self_out, ("seq", "fsdp"), axis=0, tiled=True),
            lax.all_gather(cross_q, ("seq", "fsdp"), axis=0, tiled=True),
            lax.all_gather(cross_kv, ("seq", "fsdp"), axis=0, tiled=True),
            lax.all_gather(cross_out, ("seq", "fsdp"), axis=0, tiled=True),
            lax.all_gather(ffn_in, ("seq", "fsdp"), axis=0, tiled=True),
            lax.all_gather(ffn_out, ("seq", "fsdp"), axis=0, tiled=True),
            lax.all_gather(norm_gain, ("seq", "fsdp"), axis=1, tiled=True),
            lax.all_gather(norm_bias, ("seq", "fsdp"), axis=1, tiled=True),
        )
        (
            joint_weight,
            self_output,
            cross_weight,
            pair_weight,
            cross_output,
            upward_weight,
            down_weight,
            gain_low,
            bias_low,
        ) = gathered
        gain_rows = gain_low.astype(jnp.float32)
        bias_rows = bias_low.astype(jnp.float32)
        upstream = cotangent[micro_index, 0].astype(jnp.float32)
        third_back = jax.vjp(layer_norm, mixed_third, gain_rows[2], bias_rows[2])[1]
        grad_third, gain_third, bias_third = third_back(upstream)
        branch_third = grad_third.astype(jnp.bfloat16)
        grad_down = outer_sum(active, branch_third)
        grad_active = back_project(branch_third, down_weight)
        gelu_back = jax.vjp(smooth_gelu, pre_active)[1]
        grad_inner = gelu_back(grad_active)[0].astype(jnp.bfloat16)
        grad_upward = outer_sum(hidden_second_low, grad_inner)
        grad_hidden_second = residual_weight * grad_third + back_project(grad_inner, upward_weight)
        second_back = jax.vjp(layer_norm, mixed_second, gain_rows[1], bias_rows[1])[1]
        grad_second, gain_second, bias_second = second_back(grad_hidden_second)
        branch_second = grad_second.astype(jnp.bfloat16)
        grad_cross_output = outer_sum(cross_attended, branch_second)
        grad_cross_attended = back_project(branch_second, cross_output).astype(jnp.bfloat16)
        grad_cross_query, cross_delta, grad_memory_keys, grad_memory_values = attend_backward(
            cross_query,
            memory_keys,
            memory_values,
            memory_allowed,
            cross_total,
            grad_cross_attended,
        )
        grad_cross_low = grad_cross_query.astype(jnp.bfloat16)
        grad_cross_weight = outer_sum(hidden_first_low, grad_cross_low)
        grad_hidden_first = residual_weight * grad_second + back_project(
            grad_cross_low, cross_weight
        )
        first_back = jax.vjp(layer_norm, mixed_first, gain_rows[0], bias_rows[0])[1]
        grad_first, gain_first, bias_first = first_back(grad_hidden_first)
        branch_first = grad_first.astype(jnp.bfloat16)
        grad_self_output = outer_sum(attended, branch_first)
        grad_attended = back_project(branch_first, self_output).astype(jnp.bfloat16)
        memory_partial = jnp.concatenate([grad_memory_keys, grad_memory_values], 1)
        grad_query, self_delta, grad_key, grad_value = attend_backward(
            query_rows, key_rows, value_rows, allowed, self_total, grad_attended
        )
        own_pairs, own_memory_pairs = (
            lax.psum_scatter(
                jnp.concatenate([grad_key, grad_value], 1).astype(jnp.bfloat16),
                "seq",
                scatter_dimension=0,
                tiled=True,
            ).astype(jnp.float32),
            lax.psum_scatter(
                memory_partial.astype(jnp.bfloat16), "seq", scatter_dimension=0, tiled=True
            ).astype(jnp.float32),
        )
        grad_projected = jnp.concatenate(
            [grad_query.astype(jnp.bfloat16), own_pairs.astype(jnp.bfloat16)], 1
        )
        grad_joint = outer_sum(token_rows, grad_projected)
        grad_token_list.append(
            (residual_weight * grad_first + back_project(grad_projected, joint_weight)).astype(
                jnp.bfloat16
            )
        )
        grad_pairs_low = own_memory_pairs.astype(jnp.bfloat16)
        grad_pair_weight = outer_sum(memory_rows, grad_pairs_low)
        grad_memory_list.append(back_project(grad_pairs_low, pair_weight).astype(jnp.bfloat16))
        gain_grads = jnp.stack([gain_first, gain_second, gain_third])
        bias_grads = jnp.stack([bias_first, bias_second, bias_third])
        micro_grads = (
            grad_joint,
            grad_self_output,
            grad_cross_weight,
            grad_pair_weight,
            grad_cross_output,
            grad_upward,
            grad_down,
            gain_grads,
            bias_grads,
        )
        totals = tuple((total + extra for total, extra in zip(totals, micro_grads)))
    owned = (
        lax.psum_scatter(totals[0], ("seq", "fsdp"), scatter_dimension=0, tiled=True),
        lax.psum_scatter(totals[1], ("seq", "fsdp"), scatter_dimension=0, tiled=True),
        lax.psum_scatter(totals[2], ("seq", "fsdp"), scatter_dimension=0, tiled=True),
        lax.psum_scatter(totals[3], ("seq", "fsdp"), scatter_dimension=0, tiled=True),
        lax.psum_scatter(totals[4], ("seq", "fsdp"), scatter_dimension=0, tiled=True),
        lax.psum_scatter(totals[5], ("seq", "fsdp"), scatter_dimension=0, tiled=True),
        lax.psum_scatter(totals[6], ("seq", "fsdp"), scatter_dimension=0, tiled=True),
        lax.psum_scatter(totals[7], ("seq", "fsdp"), scatter_dimension=1, tiled=True),
        lax.psum_scatter(totals[8], ("seq", "fsdp"), scatter_dimension=1, tiled=True),
    )
    output = jnp.stack(outputs)[:, None]
    grad_tokens = jnp.stack(grad_token_list)[:, None]
    grad_memory = jnp.stack(grad_memory_list)[:, None]
    return (
        output,
        grad_tokens,
        grad_memory,
        owned[0],
        owned[1],
        owned[2],
        owned[3],
        owned[4],
        owned[5],
        owned[6],
        owned[7],
        owned[8],
    )


def solution(mesh):
    in_specs = (
        P(None, "fsdp", "seq", None),
        P(None, "fsdp", "seq", None),
        P(None, "fsdp", "seq", None),
        P(None, "fsdp", None),
        P(None, "fsdp", None),
        P(None, "fsdp"),
        P(("seq", "fsdp"), None),
        P(("seq", "fsdp"), None),
        P(("seq", "fsdp"), None),
        P(("seq", "fsdp"), None),
        P(("seq", "fsdp"), None),
        P(("seq", "fsdp"), None),
        P(("seq", "fsdp"), None),
        P(None, ("seq", "fsdp")),
        P(None, ("seq", "fsdp")),
    )
    out_specs = (
        P(None, "fsdp", "seq", None),
        P(None, "fsdp", "seq", None),
        P(None, "fsdp", "seq", None),
        P(("seq", "fsdp"), None),
        P(("seq", "fsdp"), None),
        P(("seq", "fsdp"), None),
        P(("seq", "fsdp"), None),
        P(("seq", "fsdp"), None),
        P(("seq", "fsdp"), None),
        P(("seq", "fsdp"), None),
        P(None, ("seq", "fsdp")),
        P(None, ("seq", "fsdp")),
    )
    return jax.shard_map(
        per_device, mesh=mesh, in_specs=in_specs, out_specs=out_specs, check_vma=False
    )
```

profile of v0, /device:TPU:0, one launch (start us, length us, event | category | flops | bytes accessed | tf_op | source)
XLA Modules:
  0.0 3318.9 jit_solution(16396951790918094970)
XLA Ops:
  8.7 66.9 %all-gather.22.cloned.1.call-done = bf16[1024,2048]{1,0:T(8,128)(2,1)} async-done(((bf16[32,2048]{1,0:T(8,128)(2,1)}), bf16[1024,2048]{1,0:T(8,128)(2,1)}) %all-gather.22.cloned.1.call-update) | async-done | bytes 4194320 | tf_op jit(solution)/shard_map/all_gather | solution.py:203
  87.2 59.4 %all-gather.16.cloned.1.call-done = bf16[1024,3072]{1,0:T(8,128)(2,1)} async-done(((bf16[32,3072]{1,0:T(8,128)(2,1)}), bf16[1024,3072]{1,0:T(8,128)(2,1)}) %all-gather.16.cloned.1.call-update) | async-done | bytes 6291472 | tf_op jit(solution)/shard_map/all_gather | solution.py:200
  174.5 10.0 while.207
  184.4 10.0 while.211
  194.4 10.0 while.209
  204.5 39.0 %all-gather = bf16[32,32,3]{1,2,0:T(4,128)(2,1)S(1)} all-gather(bf16[1,32,3]{1,2,0:T(4,128)(2,1)S(1)} %bitcast.1127), channel_id=1, replica_groups=mesh['seq'=8,'fsdp'=4] {'seq','fsdp'}, dimensions={0}, use_global_device_ids=true | all-gather | bytes 6336 | tf_op jit(solution)/shard_map/all_gather | solution.py:207
  244.2 36.9 %all-gather.1 = bf16[32,32,3]{1,2,0:T(4,128)(2,1)S(1)} all-gather(bf16[1,32,3]{1,2,0:T(4,128)(2,1)S(1)} %bitcast.1128), channel_id=1, replica_groups=mesh['seq'=8,'fsdp'=4] {'seq','fsdp'}, dimensions={0}, use_global_device_ids=true | all-gather | bytes 6336 | tf_op jit(solution)/shard_map/all_gather | solution.py:208
  303.4 93.4 %all-gather.38.cloned.1.call-done = bf16[2048,2048]{1,0:T(8,128)(2,1)} async-done(((bf16[256,2048]{1,0:T(8,128)(2,1)}), bf16[2048,2048]{1,0:T(8,128)(2,1)}) %all-gather.38.cloned.1.call-update) | async-done | bytes 8388624 | tf_op jit(solution)/shard_map/all_gather | solution.py:232
  403.1 6.7 copy.223
  409.8 112.3 %all-gather.34.cloned.1.call-done = bf16[2048,2048]{1,0:T(8,128)(2,1)} async-done(((bf16[256,2048]{1,0:T(8,128)(2,1)}), bf16[2048,2048]{1,0:T(8,128)(2,1)}) %all-gather.34.cloned.1.call-update) | async-done | bytes 8388624 | tf_op jit(solution)/shard_map/all_gather | solution.py:232
  528.0 6.6 copy.217
  534.6 112.8 %all-gather.18.cloned.1.call-done = bf16[2048,2048]{1,0:T(8,128)(2,1)} async-done(((bf16[256,2048]{1,0:T(8,128)(2,1)}), bf16[2048,2048]{1,0:T(8,128)(2,1)}) %all-gather.18.cloned.1.call-update) | async-done | bytes 8388624 | tf_op jit(solution)/shard_map/all_gather | solution.py:232
  653.3 6.6 copy.211
  666.4 36.5 %while.201 = (s32[]{:T(128)}, bf16[4,256,256]{1,2,0:T(8,128)(2,1)S(1)}, f32[4,4,256]{2,1,0:T(4,128)S(1)}, bf16[4,2048,256]{1,2,0:T(8,128)(2,1)}, pred[256,2048]{...) while((s32[]{:T(128)}, ...), condition=%wide.region_5.6_spmd, body=%wide.region_2.5_spmd.sunk | while | flops 566230016 | bytes 33849452 | solution.py:99
  707.7 55.2 %all-gather.26.cloned.1.call-done = bf16[1024,1024]{1,0:T(8,128)(2,1)} async-done(((bf16[32,1024]{1,0:T(8,128)(2,1)}), bf16[1024,1024]{1,0:T(8,128)(2,1)}) %all-gather.26.cloned.1.call-update) | async-done | bytes 2097168 | tf_op jit(solution)/shard_map/all_gather | solution.py:202
  771.9 49.1 %all-gather.28.cloned.1.call-done = bf16[1024,1024]{1,0:T(8,128)(2,1)} async-done(((bf16[32,1024]{1,0:T(8,128)(2,1)}), bf16[1024,1024]{1,0:T(8,128)(2,1)}) %all-gather.28.cloned.1.call-update) | async-done | bytes 2097168 | tf_op jit(solution)/shard_map/all_gather | solution.py:204
  823.8 76.4 %all-gather.30.cloned.1.call-done = bf16[1024,4096]{1,0:T(8,128)(2,1)} async-done(((bf16[32,4096]{1,0:T(8,128)(2,1)}), bf16[1024,4096]{1,0:T(8,128)(2,1)}) %all-gather.30.cloned.1.call-update) | async-done | bytes 8388624 | tf_op jit(solution)/shard_map/all_gather | solution.py:205
  900.2 7.8 fusion.228
  908.0 71.3 %all-gather.32.cloned.1.call-done = bf16[4096,1024]{1,0:T(8,128)(2,1)} async-done(((bf16[128,1024]{1,0:T(8,128)(2,1)}), bf16[4096,1024]{1,0:T(8,128)(2,1)}) %all-gather.32.cloned.1.call-update) | async-done | bytes 8388624 | tf_op jit(solution)/shard_map/all_gather | solution.py:206
  979.2 7.5 fusion.256
  987.7 6.6 copy.215
  995.0 42.8 %while.202 = (s32[]{:T(128)}, bf16[4,256,256]{1,2,0:T(8,128)(2,1)S(1)}, f32[4,4,256]{2,1,0:T(4,128)}, bf16[4,2048,256]{1,2,0:T(8,128)(2,1)}, pred[256,2048]{1,0:...) while((s32[]{:T(128)}, ...), condition=%wide.region_21.22_spmd, body=%wide.region_18.21_spmd.sunk | while | flops 566230016 | bytes 33849452 | solution.py:99
  1046.1 14.2 while.210
  1073.9 6.6 copy.221
  1081.4 42.7 %while.203 = (s32[]{:T(128)}, bf16[4,256,256]{1,2,0:T(8,128)(2,1)}, f32[4,4,256]{2,1,0:T(4,128)S(1)}, bf16[4,2048,256]{1,2,0:T(8,128)(2,1)}, pred[256,2048]{1,0:...) while((s32[]{:T(128)}, bf16[4,256,256]{1,2,0:T(8,128)(2,1)}, ...), condition=%wide.region_37.38_spmd, body=%wide.region_34.37_spmd.sunk | while | flops 566230016 | bytes 33849452 | solution.py:99
  1132.1 14.4 while.212
  1164.0 9.0 fusion.101
  1173.0 6.6 convolution_add_fusion.12
  1179.6 8.0 fusion.94
  1187.6 6.8 convolution_add_fusion.13
  1194.5 8.1 fusion.87
  1202.7 7.6 multiply_reduce_fusion.10
  1219.8 27.5 while.215
  1260.9 30.5 while.214
  1298.5 30.2 while.213
  1354.8 77.8 %while.204 = (s32[]{:T(128)}, bf16[4,256,256]{1,2,0:T(8,128)(2,1)}, bf16[4,2048,256]{1,2,0:T(8,128)(2,1)}, bf16[4,2048,256]{1,2,0:T(8,128)(2,1)}, bf16[4,2048,25...) while((s32[]{:T(128)}, bf16[4,256,256]{1,2,0:T(8,128)(2,1)}, ...), condition=%wide.region_59.60_spmd, body=%wide.region_57.59_spmd.sunk | while | flops 1374813184 | bytes 79589520 | solution.py:147
  1441.4 8.5 pad_maximum_fusion
  1455.1 71.3 %while.205 = (s32[]{:T(128)}, bf16[4,256,256]{1,2,0:T(8,128)(2,1)S(1)}, bf16[4,2048,256]{1,2,0:T(8,128)(2,1)}, bf16[4,2048,256]{1,2,0:T(8,128)(2,1)}, bf16[4,204...) while((s32[]{:T(128)}, ...), condition=%wide.region_72.73_spmd, body=%wide.region_70.72_spmd.sunk | while | flops 1374813184 | bytes 79589520 | solution.py:147
  1526.4 8.6 pad_maximum_fusion.1
  1540.2 75.1 %while.206 = (s32[]{:T(128)}, bf16[4,256,256]{1,2,0:T(8,128)(2,1)S(1)}, bf16[4,2048,256]{1,2,0:T(8,128)(2,1)}, bf16[4,2048,256]{1,2,0:T(8,128)(2,1)}, bf16[4,204...) while((s32[]{:T(128)}, ...), condition=%wide.region_85.86_spmd, body=%wide.region_83.85_spmd.sunk | while | flops 1374813184 | bytes 79589520 | solution.py:147
  1615.3 8.6 pad_maximum_fusion.2
  1665.6 10.5 add_bitcast_fusion.1
  1676.2 9.3 copy.241
  1687.0 7.7 fusion.139
  1694.7 99.5 %reduce-scatter.32.cloned.1.call-done = bf16[256,2048]{0,1:T(8,128)(2,1)} async-done(((bf16[2048,2048]{0,1:T(8,128)(2,1)}), bf16[256,2048]{0,1:T(8,128)(2,1)}) %reduce-scatter.32.cloned.1.call-update) | async-done | bytes 1048592 | tf_op jit(solution)/shard_map/reduce_scatter | solution.py:339
  1794.1 7.8 fusion.138
  1801.9 144.7 %reduce-scatter.34.cloned.1.call-done = bf16[256,2048]{0,1:T(8,128)(2,1)} async-done(((bf16[2048,2048]{0,1:T(8,128)(2,1)}), bf16[256,2048]{0,1:T(8,128)(2,1)}) %reduce-scatter.34.cloned.1.call-update) | async-done | bytes 1048592 | tf_op jit(solution)/shard_map/reduce_scatter | solution.py:339
  1946.7 14.9 add_bitcast_fusion
  1961.5 12.7 copy.239
  1975.5 11.0 fusion.205
  1986.5 8.7 fusion.209
  1995.2 20.5 add_add_fusion
  2016.9 10.1 fusion.219
  2027.1 8.3 fusion.226
  2035.4 19.2 add_add_fusion.1
  2057.3 24.5 reduce-scatter.56.cloned.1.call-done
  2083.2 130.6 %reduce-scatter.58.cloned.1.call-done = f32[32,3]{1,0:T(8,128)} async-done(((f32[1024,3]{1,0:T(8,128)}), f32[32,3]{1,0:T(8,128)}) %reduce-scatter.58.cloned.1.call-update) | async-done | bytes 400
  2232.4 121.4 %reduce-scatter.38.cloned.1.call-done = f32[32,1024]{1,0:T(8,128)} async-done(((f32[1024,1024]{1,0:T(8,128)}), f32[32,1024]{1,0:T(8,128)}) %reduce-scatter.38.cloned.1.call-update) | async-done | bytes 131088 | tf_op jit(solution)/shard_map/reduce_scatter | solution.py:378
  2353.8 139.9 %reduce-scatter.40.cloned.1.call-done = f32[32,1024]{1,0:T(8,128)} async-done(((f32[1024,1024]{1,0:T(8,128)}), f32[32,1024]{1,0:T(8,128)}) %reduce-scatter.40.cloned.1.call-update) | async-done | bytes 131088 | tf_op jit(solution)/shard_map/reduce_scatter | solution.py:380
  2493.7 139.8 %reduce-scatter.36.cloned.1.call-done = f32[32,1024]{1,0:T(8,128)} async-done(((f32[1024,1024]{1,0:T(8,128)}), f32[32,1024]{1,0:T(8,128)}) %reduce-scatter.36.cloned.1.call-update) | async-done | bytes 131088 | tf_op jit(solution)/shard_map/reduce_scatter | solution.py:377
  2633.5 147.7 %reduce-scatter.54.cloned.1.call-done = f32[32,2048]{1,0:T(8,128)} async-done(((f32[1024,2048]{1,0:T(8,128)}), f32[32,2048]{1,0:T(8,128)}) %reduce-scatter.54.cloned.1.call-update) | async-done | bytes 262160
  2781.2 158.1 %reduce-scatter.52.cloned.1.call-done = f32[32,3072]{1,0:T(8,128)} async-done(((f32[1024,3072]{1,0:T(8,128)}), f32[32,3072]{1,0:T(8,128)}) %reduce-scatter.52.cloned.1.call-update) | async-done | bytes 393232
  2939.3 184.9 %reduce-scatter.44.cloned.1.call-done = f32[128,1024]{1,0:T(8,128)} async-done(((f32[4096,1024]{1,0:T(8,128)}), f32[128,1024]{1,0:T(8,128)}) %reduce-scatter.44.cloned.1.call-update) | async-done | bytes 524304 | tf_op jit(solution)/shard_map/reduce_scatter | solution.py:382
  3124.2 187.6 %reduce-scatter.42.cloned.1.call-done = f32[32,4096]{1,0:T(8,128)} async-done(((f32[1024,4096]{1,0:T(8,128)}), f32[32,4096]{1,0:T(8,128)}) %reduce-scatter.42.cloned.1.call-update) | async-done | bytes 524304 | tf_op jit(solution)/shard_map/reduce_scatter | solution.py:381
  (1321 shorter events, 789.3 us)
Async XLA Ops:
  7.2 72.3 %copy-start.101 = (bf16[3,1,32,1024]{3,2,1,0:T(8,128)(2,1)S(1)}, bf16[3,1,32,1024]{3,2,1,0:T(8,128)(2,1)}, u32[]{:S(2)}) copy-start(bf16[3,1,32,1024]{3,2,1,0:T(8,128)(2,1)} %param.46) | copy-start | bytes 589828
  7.2 68.5 %all-gather.22.cloned.1.call-start = ((), (), s32[]{:S(2)}) async-start(), calls=%async_computation.18 | async-start | bytes 4325376 | tf_op jit(solution)/shard_map/all_gather | solution.py:203
  7.9 138.6 %all-gather.16.cloned.1.call-start = ((), (), s32[]{:S(2)}) async-start(), calls=%async_computation.15 | async-start | bytes 6488064 | tf_op jit(solution)/shard_map/all_gather | solution.py:200
  8.7 278.6 %all-gather.40.cloned.1.call-start = ((), (), s32[]{:S(2)}) async-start(), calls=%async_computation.27 | async-start | bytes 1179648 | tf_op jit(solution)/shard_map/all_gather | solution.py:233
  79.4 67.1 %copy-start.41 = (bf16[3,1,256,1024]{3,2,1,0:T(8,128)(2,1)S(1)}, bf16[3,1,256,1024]{3,2,1,0:T(8,128)(2,1)}, u32[]{:S(2)}) copy-start(bf16[3,1,256,1024]{3,2,1,0:T(8,128)(2,1)} %param.45) | copy-start | bytes 4718596
  79.4 211.0 %all-gather.36.cloned.1.call-start = ((), (), s32[]{:S(2)}) async-start(), calls=%async_computation.25 | async-start | bytes 1179648 | tf_op jit(solution)/shard_map/all_gather | solution.py:233
  83.3 210.2 %all-gather.24.cloned.1.call-start = ((), (), s32[]{:S(2)}) async-start(), calls=%async_computation.19 | async-start | bytes 1179648 | tf_op jit(solution)/shard_map/all_gather | solution.py:233
  87.1 309.7 %all-gather.38.cloned.1.call-start = ((), (), s32[]{:S(2)}) async-start(), calls=%async_computation.26 | async-start | bytes 9437184 | tf_op jit(solution)/shard_map/all_gather | solution.py:232
  153.4 368.7 %all-gather.34.cloned.1.call-start = ((), (), s32[]{:S(2)}) async-start(), calls=%async_computation.24 | async-start | bytes 9437184 | tf_op jit(solution)/shard_map/all_gather | solution.py:232
  160.4 487.0 %all-gather.18.cloned.1.call-start = ((), (), s32[]{:S(2)}) async-start(), calls=%async_computation.16 | async-start | bytes 9437184 | tf_op jit(solution)/shard_map/all_gather | solution.py:232
  167.3 537.5 %all-gather.20.cloned.1.call-start = ((), (), s32[]{:S(2)}) async-start(), calls=%async_computation.17 | async-start | bytes 2162688 | tf_op jit(solution)/shard_map/all_gather | solution.py:201
  168.1 594.8 %all-gather.26.cloned.1.call-start = ((), (), s32[]{:S(2)}) async-start(), calls=%async_computation.20 | async-start | bytes 2162688 | tf_op jit(solution)/shard_map/all_gather | solution.py:202
  168.7 652.4 %all-gather.28.cloned.1.call-start = ((), (), s32[]{:S(2)}) async-start(), calls=%async_computation.21 | async-start | bytes 2162688 | tf_op jit(solution)/shard_map/all_gather | solution.py:204
  169.4 730.8 %all-gather.30.cloned.1.call-start = ((), (), s32[]{:S(2)}) async-start(), calls=%async_computation.22 | async-start | bytes 8650752 | tf_op jit(solution)/shard_map/all_gather | solution.py:205
  170.0 809.3 %all-gather.32.cloned.1.call-start = ((), (), s32[]{:S(2)}) async-start(), calls=%async_computation.23 | async-start | bytes 8650752 | tf_op jit(solution)/shard_map/all_gather | solution.py:206
  170.7 1483.1 %reduce-scatter.48.cloned.1.call-start = ((), (), s32[]{:S(2)}) async-start(), calls=%async_computation.37 | async-start | bytes 1179648
  174.5 69.7 %copy-start.201 = (bf16[3,32]{1,0:T(4,128)(2,1)S(1)}, bf16[3,32]{1,0:T(4,128)(2,1)}, u32[]{:S(2)}) copy-start(bf16[3,32]{1,0:T(4,128)(2,1)} %param.59) | copy-start | bytes 580
  244.2 966.3 %copy-start.95 = (f32[1,1024]{1,0:T(1,128)}, f32[1,1024]{1,0:T(1,128)S(1)}, u32[]{:S(2)}) copy-start(f32[1,1024]{1,0:T(1,128)S(1)} %get-tuple-element.1221) | copy-start | bytes 12292
  244.2 1099.6 %copy-start.103 = (f32[1,1024]{1,0:T(1,128)}, f32[1,1024]{1,0:T(1,128)S(1)}, u32[]{:S(2)}) copy-start(f32[1,1024]{1,0:T(1,128)S(1)} %get-tuple-element.1222) | copy-start | bytes 12292
  281.8 864.7 %copy-start.106 = (f32[1,1024]{1,0:T(1,128)}, f32[1,1024]{1,0:T(1,128)S(1)}, u32[]{:S(2)}) copy-start(f32[1,1024]{1,0:T(1,128)S(1)} %get-tuple-element.1225) | copy-start | bytes 12292
  281.8 873.8 %copy-start.99 = (f32[1,1024]{1,0:T(1,128)}, f32[1,1024]{1,0:T(1,128)S(1)}, u32[]{:S(2)}) copy-start(f32[1,1024]{1,0:T(1,128)S(1)} %get-tuple-element.1224) | copy-start | bytes 12292
  702.9 59.9 %copy-start.51 = (bf16[4,256,256]{1,2,0:T(8,128)(2,1)}, bf16[4,256,256]{1,2,0:T(8,128)(2,1)S(1)}, u32[]{:S(2)}) copy-start(bf16[4,256,256]{1,2,0:T(8,128)(2,1)S(1)} %get-tuple-element.646) | copy-start | bytes 1572868
  702.9 63.1 %copy-start.4 = (pred[256,2048]{1,0:T(8,128)(4,1)}, pred[256,2048]{1,0:T(8,128)(4,1)S(1)}, u32[]{:S(2)}) copy-start(pred[256,2048]{1,0:T(8,128)(4,1)S(1)} %get-tuple-element.2489) | copy-start | bytes 1572868
  707.4 113.6 %copy-start.9 = (f32[256,1024]{1,0:T(8,128)}, f32[256,1024]{1,0:T(8,128)S(1)}, u32[]{:S(2)}) copy-start(f32[256,1024]{1,0:T(8,128)S(1)} %get-tuple-element.1256) | copy-start | bytes 3145732
  707.4 113.6 %copy-start.119 = (f32[256]{0:T(256)}, f32[256]{0:T(256)S(1)}, u32[]{:S(2)}) copy-start(f32[256]{0:T(256)S(1)} %broadcast_multiply_fusion.8) | copy-start | bytes 3076
  707.7 59.6 %copy-start.168 = (f32[256]{0:T(256)}, f32[256]{0:T(256)S(1)}, u32[]{:S(2)}) copy-start(f32[256]{0:T(256)S(1)} %multiply_reduce_fusion.26) | copy-start | bytes 3076
  707.7 113.4 %copy-start.127 = (f32[256]{0:T(256)}, f32[256]{0:T(256)S(1)}, u32[]{:S(2)}) copy-start(f32[256]{0:T(256)S(1)} %fusion.190) | copy-start | bytes 3076
  771.9 49.2 %copy-start.37 = (bf16[4,256,256]{1,2,0:T(8,128)(2,1)}, bf16[4,256,256]{1,2,0:T(8,128)(2,1)S(1)}, u32[]{:S(2)}) copy-start(bf16[4,256,256]{1,2,0:T(8,128)(2,1)S(1)} %get-tuple-element.2523) | copy-start | bytes 1572868
  771.9 49.1 %copy-start.38 = (bf16[4,256,256]{1,2,0:T(8,128)(2,1)}, bf16[4,256,256]{1,2,0:T(8,128)(2,1)S(1)}, u32[]{:S(2)}) copy-start(bf16[4,256,256]{1,2,0:T(8,128)(2,1)S(1)} %get-tuple-element.2525) | copy-start | bytes 1572868
  771.9 136.1 %copy-start.40 = (bf16[4,256,256]{1,2,0:T(8,128)(2,1)}, bf16[4,256,256]{1,2,0:T(8,128)(2,1)S(1)}, u32[]{:S(2)}) copy-start(bf16[4,256,256]{1,2,0:T(8,128)(2,1)S(1)} %get-tuple-element.2532) | copy-start | bytes 1572868
  771.9 136.1 %copy-start.58 = (bf16[4,256,256]{1,2,0:T(8,128)(2,1)}, bf16[4,256,256]{1,2,0:T(8,128)(2,1)S(1)}, u32[]{:S(2)}) copy-start(bf16[4,256,256]{1,2,0:T(8,128)(2,1)S(1)} %get-tuple-element.647) | copy-start | bytes 1572868
  771.9 136.0 %copy-start.108 = (pred[256]{0:T(512)(128)(4,1)}, pred[256]{0:T(512)(128)(4,1)S(1)}, u32[]{:S(2)}) copy-start(pred[256]{0:T(512)(128)(4,1)S(1)} %get-tuple-element.2574) | copy-start | bytes 772
  771.9 136.0 %copy-start.114 = (f32[4,4,256]{2,1,0:T(4,128)}, f32[4,4,256]{2,1,0:T(4,128)S(1)}, u32[]{:S(2)}) copy-start(f32[4,4,256]{2,1,0:T(4,128)S(1)} %get-tuple-element.2333) | copy-start | bytes 49156
  823.5 155.7 %copy-start.18 = (f32[256,1024]{1,0:T(8,128)}, f32[256,1024]{1,0:T(8,128)S(1)}, u32[]{:S(2)}) copy-start(f32[256,1024]{1,0:T(8,128)S(1)} %get-tuple-element.1258) | copy-start | bytes 3145732
  823.5 155.7 %copy-start.134 = (f32[256]{0:T(256)}, f32[256]{0:T(256)S(1)}, u32[]{:S(2)}) copy-start(f32[256]{0:T(256)S(1)} %broadcast_multiply_fusion.7) | copy-start | bytes 3076
  823.8 84.2 %copy-start.172 = (f32[256]{0:T(256)}, f32[256]{0:T(256)S(1)}, u32[]{:S(2)}) copy-start(f32[256]{0:T(256)S(1)} %multiply_reduce_fusion.25) | copy-start | bytes 3076
  823.8 155.4 %copy-start.140 = (f32[256]{0:T(256)}, f32[256]{0:T(256)S(1)}, u32[]{:S(2)}) copy-start(f32[256]{0:T(256)S(1)} %fusion.191) | copy-start | bytes 3076
  1127.3 216.4 %copy-start.7 = (f32[256,1024]{1,0:T(8,128)}, f32[256,1024]{1,0:T(8,128)S(1)}, u32[]{:S(2)}) copy-start(f32[256,1024]{1,0:T(8,128)S(1)} %get-tuple-element.1262) | copy-start | bytes 3145732
  1127.4 216.4 %copy-start.117 = (f32[256]{0:T(256)}, f32[256]{0:T(256)S(1)}, u32[]{:S(2)}) copy-start(f32[256]{0:T(256)S(1)} %broadcast_multiply_fusion.2) | copy-start | bytes 3076
  1127.6 216.1 %copy-start.125 = (f32[256]{0:T(256)}, f32[256]{0:T(256)S(1)}, u32[]{:S(2)}) copy-start(f32[256]{0:T(256)S(1)} %fusion.196) | copy-start | bytes 3076
  1149.3 61.1 %copy-start.24 = (f32[256,1024]{1,0:T(8,128)}, f32[256,1024]{1,0:T(8,128)S(1)}, u32[]{:S(2)}) copy-start(f32[256,1024]{1,0:T(8,128)S(1)} %get-tuple-element.1264) | copy-start | bytes 3145732
  1149.3 61.1 %copy-start.153 = (f32[256]{0:T(256)}, f32[256]{0:T(256)S(1)}, u32[]{:S(2)}) copy-start(f32[256]{0:T(256)S(1)} %broadcast_multiply_fusion.1) | copy-start | bytes 3076
  1149.6 60.8 %copy-start.160 = (f32[256]{0:T(256)}, f32[256]{0:T(256)S(1)}, u32[]{:S(2)}) copy-start(f32[256]{0:T(256)S(1)} %fusion.197) | copy-start | bytes 3076
  1163.9 38.7 %copy-start.67 = (f32[256,1024]{1,0:T(8,128)}, f32[256,1024]{1,0:T(8,128)S(1)}, u32[]{:S(2)}) copy-start(f32[256,1024]{1,0:T(8,128)S(1)} %get-tuple-element.1140) | copy-start | bytes 3145732
  1212.7 128.4 %copy-start.166 = (f32[256]{0:T(256)}, f32[256]{0:T(256)S(1)}, u32[]{:S(2)}) copy-start(f32[256]{0:T(256)S(1)} %negate_multiply_fusion.7) | copy-start | bytes 3076
  1212.7 125.2 %copy-start.164 = (f32[256]{0:T(256)}, f32[256]{0:T(256)S(1)}, u32[]{:S(2)}) copy-start(f32[256]{0:T(256)S(1)} %negate_multiply_fusion.4) | copy-start | bytes 3076
  1212.7 127.6 %copy-start.162 = (f32[256]{0:T(256)}, f32[256]{0:T(256)S(1)}, u32[]{:S(2)}) copy-start(f32[256]{0:T(256)S(1)} %negate_multiply_fusion.1) | copy-start | bytes 3076
  1295.9 364.2 %reduce-scatter.46.cloned.1.call-start = ((), (), s32[]{:S(2)}) async-start(), calls=%async_computation.36 | async-start | bytes 1179648
  1337.8 327.8 %reduce-scatter.50.cloned.1.call-start = ((), (), s32[]{:S(2)}) async-start(), calls=%async_computation.38 | async-start | bytes 1179648
  1348.9 337.1 %reduce-scatter.30.cloned.1.call-start = ((), (), s32[]{:S(2)}) async-start(), calls=%async_computation.28 | async-start | bytes 9437184 | tf_op jit(solution)/shard_map/reduce_scatter | solution.py:339
  1449.9 344.2 %reduce-scatter.32.cloned.1.call-start = ((), (), s32[]{:S(2)}) async-start(), calls=%async_computation.29 | async-start | bytes 9437184 | tf_op jit(solution)/shard_map/reduce_scatter | solution.py:339
  1535.0 411.6 %reduce-scatter.34.cloned.1.call-start = ((), (), s32[]{:S(2)}) async-start(), calls=%async_computation.30 | async-start | bytes 9437184 | tf_op jit(solution)/shard_map/reduce_scatter | solution.py:339
  1624.1 457.7 %reduce-scatter.56.cloned.1.call-start = ((), (), s32[]{:S(2)}) async-start(), calls=%async_computation.41 | async-start | bytes 540672
  1633.2 580.6 %reduce-scatter.58.cloned.1.call-start = ((), (), s32[]{:S(2)}) async-start(), calls=%async_computation.42 | async-start | bytes 540672
  1634.4 719.4 %reduce-scatter.38.cloned.1.call-start = ((), (), s32[]{:S(2)}) async-start(), calls=%async_computation.32 | async-start | bytes 4325376 | tf_op jit(solution)/shard_map/reduce_scatter | solution.py:378
  1641.2 852.5 %reduce-scatter.40.cloned.1.call-start = ((), (), s32[]{:S(2)}) async-start(), calls=%async_computation.33 | async-start | bytes 4325376 | tf_op jit(solution)/shard_map/reduce_scatter | solution.py:380
  1647.5 986.0 %reduce-scatter.36.cloned.1.call-start = ((), (), s32[]{:S(2)}) async-start(), calls=%async_computation.31 | async-start | bytes 4325376 | tf_op jit(solution)/shard_map/reduce_scatter | solution.py:377
  1653.8 1127.4 %reduce-scatter.54.cloned.1.call-start = ((), (), s32[]{:S(2)}) async-start(), calls=%async_computation.40 | async-start | bytes 8650752
  1685.5 1253.8 %reduce-scatter.52.cloned.1.call-start = ((), (), s32[]{:S(2)}) async-start(), calls=%async_computation.39 | async-start | bytes 12976128
  1794.1 152.5 %copy-start.76 = (bf16[4,256,256]{1,2,0:T(8,128)(2,1)S(1)}, bf16[4,256,256]{1,2,0:T(8,128)(2,1)}, u32[]{:S(2)}) copy-start(bf16[4,256,256]{1,2,0:T(8,128)(2,1)} %copy-done.75) | copy-start | bytes 1572868
  1974.3 1149.9 %reduce-scatter.44.cloned.1.call-start = ((), (), s32[]{:S(2)}) async-start(), calls=%async_computation.35 | async-start | bytes 17301504 | tf_op jit(solution)/shard_map/reduce_scatter | solution.py:382
  2015.8 1296.0 %reduce-scatter.42.cloned.1.call-start = ((), (), s32[]{:S(2)}) async-start(), calls=%async_computation.34 | async-start | bytes 17301504 | tf_op jit(solution)/shard_map/reduce_scatter | solution.py:381
  2054.6 160.5 %copy-start.105 = (bf16[32,2048]{1,0:T(8,128)(2,1)S(1)}, bf16[32,2048]{1,0:T(8,128)(2,1)}, u32[]{:S(2)}) copy-start(bf16[32,2048]{1,0:T(8,128)(2,1)} %reduce-scatter.50.cloned.1.call-done) | copy-start | bytes 393220
  2054.7 164.1 %copy-start.98 = (bf16[32,2048]{1,0:T(8,128)(2,1)S(1)}, bf16[32,2048]{1,0:T(8,128)(2,1)}, u32[]{:S(2)}) copy-start(bf16[32,2048]{1,0:T(8,128)(2,1)} %reduce-scatter.46.cloned.1.call-done) | copy-start | bytes 393220
  (175 other events, 902.1 us)
Sparse Core Ops, SparseCore 0:
  10.9 64.7 all-gather.21
  78.6 67.9 all-gather.15
  149.2 38.7 all-gather.39
  190.5 39.0 all-gather.35
  232.2 38.9 all-gather.23
  273.1 123.6 all-gather.37
  399.0 123.1 all-gather.33
  524.2 123.1 all-gather.17
  650.2 54.5 all-gather.19
  707.6 55.2 all-gather.25
  765.7 55.2 all-gather.27
  823.7 76.3 all-gather.29
  903.0 76.1 all-gather.31
  1296.0 61.9 reduce-scatter.47
  1361.7 62.3 reduce-scatter.45
  1427.4 62.3 reduce-scatter.49
  1493.7 148.6 reduce-scatter.29
  1645.9 148.1 reduce-scatter.31
  1798.2 148.4 reduce-scatter.33
  1948.7 132.9 reduce-scatter.55
  2084.1 129.5 reduce-scatter.57
  2216.6 137.0 reduce-scatter.37
  2356.6 137.0 reduce-scatter.39
  2496.4 137.0 reduce-scatter.35
  2636.4 144.7 reduce-scatter.53
  2787.6 151.6 reduce-scatter.51
  2942.1 182.0 reduce-scatter.43
  3127.2 184.5 reduce-scatter.41
where the time goes:
time: 3330 us; the launch traced here: 3320 us
  waiting for transfers between devices  2180 us (65%)
  matrix products  514 us (15%)
  local copies, waits for them, and re-layouts  397 us (12%)
  other arithmetic  125 us (4%)
  blocking collectives  75.9 us (2%)
    unnamed x35, waiting for transfers between devices  466 us
    all_gather x3, waiting for transfers between devices, per_device(): lax.all_gather(projected[:, width:], 'seq', axis=0, tiled=True)  319 us
    reduce_scatter x3, waiting for transfers between devices, per_device(): lax.psum_scatter(jnp.concatenate([grad_key, grad_value], 1).astype(jnp.bf...  244 us
    reduce_scatter x1, waiting for transfers between devices, per_device(): lax.psum_scatter(totals[5], ('seq', 'fsdp'), scatter_dimension=0, tiled=T...  188 us
    reduce_scatter x1, waiting for transfers between devices, per_device(): lax.psum_scatter(totals[6], ('seq', 'fsdp'), scatter_dimension=0, tiled=T...  185 us
    dot_general x21, matrix products, outer_sum(): lax.dot_general(left_side, right_side, (((0,), (0,)), ((), ())), preferre...  150 us
    reduce_scatter x1, waiting for transfers between devices, per_device(): lax.psum_scatter(totals[4], ('seq', 'fsdp'), scatter_dimension=0, tiled=T...  140 us
    reduce_scatter x1, waiting for transfers between devices, per_device(): lax.psum_scatter(totals[1], ('seq', 'fsdp'), scatter_dimension=0, tiled=T...  140 us
  transfers between devices with their start and end apart: 28, of which 21 were waited for; matrix products, arithmetic and copies ran while one was open for 21% of the time, Pallas kernels for 0%

commit v1 on v0

v1 whole, which is shorter than its diff:
```python
import functools

import jax
import jax.numpy as jnp
from jax import lax
from jax.experimental import pallas as pl
from jax.experimental.pallas import tpu as pltpu
from jax.sharding import PartitionSpec as P

H = 16
HD = 64
TILE = 128
BLOCK = 256

scale_factor = 0.125
residual_weight = 36.0**0.25
norm_epsilon = 1e-05
masked_score = -1e30
ALL = ("seq", "fsdp")
f32 = jnp.float32
bf16 = jnp.bfloat16


def dot_nn(a, b):
    return lax.dot_general(a, b, (((1,), (0,)), ((), ())), preferred_element_type=f32)


def dot_nt(a, b):
    return lax.dot_general(a, b, (((1,), (1,)), ((), ())), preferred_element_type=f32)


def dot_tn(a, b):
    return lax.dot_general(a, b, (((0,), (0,)), ((), ())), preferred_element_type=f32)


def norm_stats(incoming):
    row_mean = jnp.mean(incoming, -1, keepdims=True)
    centred = incoming - row_mean
    variance = jnp.mean(centred * centred, -1, keepdims=True)
    return centred, lax.rsqrt(variance + norm_epsilon)


def layer_norm(incoming, gain_row, bias_row):
    centred, inverse = norm_stats(incoming)
    return centred * inverse * gain_row + bias_row


def layer_norm_back(incoming, gain_row, upstream):
    centred, inverse = norm_stats(incoming)
    normal = centred * inverse
    grad_bias = jnp.sum(upstream, 0)
    grad_gain = jnp.sum(upstream * normal, 0)
    scaled = upstream * gain_row
    grad = inverse * (
        scaled
        - jnp.mean(scaled, -1, keepdims=True)
        - normal * jnp.mean(scaled * normal, -1, keepdims=True)
    )
    return grad, grad_gain, grad_bias


def ancestors(parent_ids):
    segment_ids = jnp.arange(parent_ids.shape[0], dtype=jnp.int32)
    hop = (parent_ids[:, None] == segment_ids[None, :]).astype(f32)
    reach = jnp.maximum(hop, (segment_ids[:, None] == segment_ids[None, :]).astype(f32))
    steps = 1
    while steps < parent_ids.shape[0]:
        reach = jnp.minimum(jnp.dot(reach, reach, precision=lax.Precision.HIGHEST), 1.0)
        steps *= 2
    return reach


def tree_bias(tile_segments, parent_ids, block):
    tiles = tile_segments.shape[0]
    onehot = (
        tile_segments[:, None] == jnp.arange(parent_ids.shape[0], dtype=jnp.int32)[None, :]
    ).astype(f32)
    high = lax.Precision.HIGHEST
    related = jnp.dot(
        jnp.dot(onehot, ancestors(parent_ids), precision=high), onehot.T, precision=high
    )
    bias = jnp.where(related > 0.5, 0.0, masked_score)
    per = block // TILE
    blocks = tiles // per
    bias = bias.reshape(blocks, per, blocks, per).transpose(2, 0, 3, 1)
    return jnp.repeat(bias, TILE, axis=3)


def head_masks(shape, heads):
    lane = lax.broadcasted_iota(jnp.int32, shape, 1)
    return [(lane >= h * HD) & (lane < (h + 1) * HD) for h in range(heads)]


def keep_head(value, mask, heads):
    return value if heads == 1 else jnp.where(mask, value, jnp.zeros_like(value))


def self_forward_kernel(heads, block, qkv_ref, bias_ref, out_ref, lse_ref, queries, values_t):
    length, width = qkv_ref.shape[2], qkv_ref.shape[3]
    blocks = length // block
    per = block // TILE
    masks = head_masks((block, width), heads)

    def prepare(i, carry):
        rows = pl.ds(pl.multiple_of(i * block, block), block)
        q = qkv_ref[0, 0, rows, :].astype(f32) * scale_factor
        for h in range(heads):
            queries[h, rows, :] = keep_head(q, masks[h], heads).astype(bf16)
        values_t[i] = jnp.transpose(qkv_ref[0, 2, rows, :].astype(f32)).astype(bf16)
        return carry

    lax.fori_loop(0, blocks, prepare, 0)
    key_place = lax.broadcasted_iota(jnp.int32, (block, block), 0)
    query_place = lax.broadcasted_iota(jnp.int32, (block, block), 1)
    causal = key_place <= query_place

    def scores_of(i, j, h):
        rows = pl.ds(pl.multiple_of(i * block, block), block)
        keys = qkv_ref[0, 1, pl.ds(pl.multiple_of(j * block, block), block), :]
        raw = dot_nt(keys, queries[h, rows, :])
        bias = bias_ref[0, j, i]
        return (raw.reshape(per, TILE, block) + bias[:, None, :]).reshape(block, block)

    def query_block(i, carry):
        state = []
        for h in range(heads):
            s = jnp.where(causal, scores_of(i, i, h), masked_score)
            m = jnp.max(s, 0, keepdims=True)
            p = jnp.exp(s - m)
            total = jnp.sum(p, 0, keepdims=True)
            acc = dot_nn(values_t[i][h * HD : (h + 1) * HD], p.astype(bf16))
            state += [m, total, acc]

        def key_block(j, state):
            fresh = []
            for h in range(heads):
                m, total, acc = state[3 * h : 3 * h + 3]
                s = scores_of(i, j, h)
                m_new = jnp.maximum(m, jnp.max(s, 0, keepdims=True))
                shrink = jnp.exp(m - m_new)
                p = jnp.exp(s - m_new)
                total = total * shrink + jnp.sum(p, 0, keepdims=True)
                acc = acc * shrink + dot_nn(values_t[j][h * HD : (h + 1) * HD], p.astype(bf16))
                fresh += [m_new, total, acc]
            return tuple(fresh)

        state = lax.fori_loop(0, i, key_block, tuple(state))
        out = jnp.concatenate(
            [state[3 * h + 2] * (1.0 / state[3 * h + 1]) for h in range(heads)], 0
        )
        out_ref[0, pl.ds(pl.multiple_of(i * block, block), block), :] = jnp.transpose(out).astype(
            bf16
        )
        lse_ref[0, i] = jnp.concatenate(
            [state[3 * h] + jnp.log(state[3 * h + 1]) for h in range(heads)], 0
        )
        return carry

    lax.fori_loop(0, blocks, query_block, 0)


def self_forward(qkv, bias):
    micro, _, length, width = qkv.shape
    heads = width // HD
    blocks = length // BLOCK
    return pl.pallas_call(
        functools.partial(self_forward_kernel, heads, BLOCK),
        grid=(micro,),
        in_specs=[
            pl.BlockSpec((1, 3, length, width), lambda m: (m, 0, 0, 0)),
            pl.BlockSpec((1,) + bias.shape[1:], lambda m: (m, 0, 0, 0, 0)),
        ],
        out_specs=[
            pl.BlockSpec((1, length, width), lambda m: (m, 0, 0)),
            pl.BlockSpec((1, blocks, heads, BLOCK), lambda m: (m, 0, 0, 0)),
        ],
        out_shape=[
            jax.ShapeDtypeStruct((micro, length, width), bf16),
            jax.ShapeDtypeStruct((micro, blocks, heads, BLOCK), f32),
        ],
        scratch_shapes=[
            pltpu.VMEM((heads, length, width), bf16),
            pltpu.VMEM((blocks, width, BLOCK), bf16),
        ],
        compiler_params=pltpu.CompilerParams(vmem_limit_bytes=48 << 20),
        name="self_forward",
    )(qkv, bias)


def self_backward_kernel(
    heads, block, qkv_ref, bias_ref, out_ref, lse_ref, gout_ref, grad_ref,
    queries, keys_h, gouts, delta, grad_q,
):
    length, width = qkv_ref.shape[2], qkv_ref.shape[3]
    blocks = length // block
    per = block // TILE
    masks = head_masks((block, width), heads)
    lane = lax.broadcasted_iota(jnp.int32, (8, width), 1)
    row = lax.broadcasted_iota(jnp.int32, (8, width), 0)
    pick = jnp.where(lane // HD == row, 1.0, 0.0)

    def prepare(i, carry):
        rows = pl.ds(pl.multiple_of(i * block, block), block)
        q = qkv_ref[0, 0, rows, :].astype(f32) * scale_factor
        k = qkv_ref[0, 1, rows, :].astype(f32)
        g = gout_ref[0, rows, :].astype(f32)
        for h in range(heads):
            queries[h, rows, :] = keep_head(q, masks[h], heads).astype(bf16)
            keys_h[h, rows, :] = keep_head(k, masks[h], heads).astype(bf16)
            gouts[h, rows, :] = keep_head(g, masks[h], heads).astype(bf16)
        products = g * out_ref[0, rows, :].astype(f32)
        delta[i] = lax.dot_general(
            pick,
            products,
            (((1,), (1,)), ((), ())),
            precision=lax.Precision.HIGHEST,
            preferred_element_type=f32,
        )
        grad_q[rows, :] = jnp.zeros((block, width), f32)
        return carry

    lax.fori_loop(0, blocks, prepare, 0)
    key_place = lax.broadcasted_iota(jnp.int32, (block, block), 0)
    query_place = lax.broadcasted_iota(jnp.int32, (block, block), 1)
    causal = key_place <= query_place

    def key_block(j, carry):
        krows = pl.ds(pl.multiple_of(j * block, block), block)
        keys = qkv_ref[0, 1, krows, :]
        values = qkv_ref[0, 2, krows, :]

        def pair(i, grad_k, grad_v, diagonal):
            rows = pl.ds(pl.multiple_of(i * block, block), block)
            bias = bias_ref[0, j, i]
            gq = grad_q[rows, :]
            for h in range(heads):
                raw = dot_nt(keys, queries[h, rows, :]).reshape(per, TILE, block)
                shift = bias - lse_ref[0, i, h : h + 1, :]
                s = (raw + shift[:, None, :]).reshape(block, block)
                if diagonal:
                    s = jnp.where(causal, s, masked_score)
                p = jnp.exp(s)
                gp = dot_nt(values, gouts[h, rows, :])
                gs = (p * (gp - delta[i, h : h + 1, :])).astype(bf16)
                grad_v = grad_v + dot_nn(p.astype(bf16), gouts[h, rows, :])
                grad_k = grad_k + dot_nn(gs, queries[h, rows, :])
                gq = gq + dot_tn(gs, keys_h[h, krows, :])
            grad_q[rows, :] = gq
            return grad_k, grad_v

        zero = jnp.zeros((block, width), f32)
        state = pair(j, zero, zero, True)
        state = lax.fori_loop(j + 1, blocks, lambda i, s: pair(i, s[0], s[1], False), state)
        grad_ref[0, 1, krows, :] = state[0].astype(bf16)
        grad_ref[0, 2, krows, :] = state[1].astype(bf16)
        return carry

    lax.fori_loop(0, blocks, key_block, 0)
    grad_ref[0, 0] = (grad_q[...] * scale_factor).astype(bf16)


def self_backward(qkv, bias, out, lse, gout):
    micro, _, length, width = qkv.shape
    heads = width // HD
    blocks = length // BLOCK
    return pl.pallas_call(
        functools.partial(self_backward_kernel, heads, BLOCK),
        grid=(micro,),
        in_specs=[
            pl.BlockSpec((1, 3, length, width), lambda m: (m, 0, 0, 0)),
            pl.BlockSpec((1,) + bias.shape[1:], lambda m: (m, 0, 0, 0, 0)),
            pl.BlockSpec((1, length, width), lambda m: (m, 0, 0)),
            pl.BlockSpec((1, blocks, heads, BLOCK), lambda m: (m, 0, 0, 0)),
            pl.BlockSpec((1, length, width), lambda m: (m, 0, 0)),
        ],
        out_specs=pl.BlockSpec((1, 3, length, width), lambda m: (m, 0, 0, 0)),
        out_shape=jax.ShapeDtypeStruct((micro, 3, length, width), bf16),
        scratch_shapes=[
            pltpu.VMEM((heads, length, width), bf16),
            pltpu.VMEM((heads, length, width), bf16),
            pltpu.VMEM((heads, length, width), bf16),
            pltpu.VMEM((blocks, 8, BLOCK), f32),
            pltpu.VMEM((length, width), f32),
        ],
        compiler_params=pltpu.CompilerParams(vmem_limit_bytes=48 << 20),
        name="self_backward",
    )(qkv, bias, out, lse, gout)


def cross_forward_kernel(lengths_ref, q_ref, k_ref, v_ref, out_ref, lse_ref):
    count, width = k_ref.shape[1], k_ref.shape[2]
    rows = q_ref.shape[1]
    heads = width // HD
    masks = head_masks((rows, width), heads)
    valid = (
        lax.broadcasted_iota(jnp.int32, (count, rows), 0) < lengths_ref[pl.program_id(0)]
    )
    q = q_ref[0].astype(f32) * scale_factor
    values_t = jnp.transpose(v_ref[0].astype(f32)).astype(bf16)
    outs, lses = [], []
    for h in range(heads):
        s = dot_nt(k_ref[0], keep_head(q, masks[h], heads).astype(bf16))
        s = jnp.where(valid, s, masked_score)
        m = jnp.max(s, 0, keepdims=True)
        p = jnp.exp(s - m)
        total = jnp.sum(p, 0, keepdims=True)
        out = dot_nn(values_t[h * HD : (h + 1) * HD], p.astype(bf16))
        outs.append(out * (1.0 / total))
        lses.append(m + jnp.log(total))
    out_ref[0] = jnp.transpose(jnp.concatenate(outs, 0)).astype(bf16)
    lse_ref[0, 0] = jnp.concatenate(lses, 0)


def cross_forward(lengths, queries, pairs):
    micro, rows, width = queries.shape
    count = pairs.shape[1]
    groups = width // 128
    return pl.pallas_call(
        cross_forward_kernel,
        grid=(micro, groups),
        in_specs=[
            pl.BlockSpec(memory_space=pltpu.SMEM),
            pl.BlockSpec((1, rows, 128), lambda m, g: (m, 0, g)),
            pl.BlockSpec((1, count, 128), lambda m, g: (m, 0, g)),
            pl.BlockSpec((1, count, 128), lambda m, g: (m, 0, g + groups)),
        ],
        out_specs=[
            pl.BlockSpec((1, rows, 128), lambda m, g: (m, 0, g)),
            pl.BlockSpec((1, 1, 2, rows), lambda m, g: (m, g, 0, 0)),
        ],
        out_shape=[
            jax.ShapeDtypeStruct((micro, rows, width), bf16),
            jax.ShapeDtypeStruct((micro, groups, 2, rows), f32),
        ],
        compiler_params=pltpu.CompilerParams(vmem_limit_bytes=32 << 20),
        name="cross_forward",
    )(lengths, queries, pairs, pairs)


def cross_backward_kernel(
    lengths_ref, q_ref, k_ref, v_ref, out_ref, lse_ref, gout_ref, gq_ref, gk_ref, gv_ref
):
    count, width = k_ref.shape[1], k_ref.shape[2]
    rows = q_ref.shape[1]
    heads = width // HD
    masks = head_masks((rows, width), heads)
    key_masks = head_masks((count, width), heads)
    valid = (
        lax.broadcasted_iota(jnp.int32, (count, rows), 0) < lengths_ref[pl.program_id(0)]
    )
    lane = lax.broadcasted_iota(jnp.int32, (8, width), 1)
    row = lax.broadcasted_iota(jnp.int32, (8, width), 0)
    pick = jnp.where(lane // HD == row, 1.0, 0.0)
    q = q_ref[0].astype(f32) * scale_factor
    g = gout_ref[0].astype(f32)
    k = k_ref[0].astype(f32)
    delta = lax.dot_general(
        pick,
        g * out_ref[0].astype(f32),
        (((1,), (1,)), ((), ())),
        precision=lax.Precision.HIGHEST,
        preferred_element_type=f32,
    )
    grad_q = jnp.zeros((rows, width), f32)
    grad_k = jnp.zeros((count, width), f32)
    grad_v = jnp.zeros((count, width), f32)
    for h in range(heads):
        qh = keep_head(q, masks[h], heads).astype(bf16)
        gh = keep_head(g, masks[h], heads).astype(bf16)
        kh = keep_head(k, key_masks[h], heads).astype(bf16)
        s = dot_nt(k_ref[0], qh) - lse_ref[0, 0, h : h + 1, :]
        p = jnp.exp(jnp.where(valid, s, masked_score))
        gp = dot_nt(v_ref[0], gh)
        gs = (p * (gp - delta[h : h + 1, :])).astype(bf16)
        grad_v += dot_nn(p.astype(bf16), gh)
        grad_k += dot_nn(gs, qh)
        grad_q += dot_tn(gs, kh)
    gq_ref[0] = (grad_q * scale_factor).astype(bf16)
    gk_ref[0] = grad_k.astype(bf16)
    gv_ref[0] = grad_v.astype(bf16)


def cross_backward(lengths, queries, pairs, out, lse, gout):
    micro, rows, width = queries.shape
    count = pairs.shape[1]
    groups = width // 128
    row_spec = pl.BlockSpec((1, rows, 128), lambda m, g: (m, 0, g))
    key_spec = pl.BlockSpec((1, count, 128), lambda m, g: (m, 0, g))
    value_spec = pl.BlockSpec((1, count, 128), lambda m, g: (m, 0, g + groups))
    lse_spec = pl.BlockSpec((1, 1, 2, rows), lambda m, g: (m, g, 0, 0))
    return pl.pallas_call(
        cross_backward_kernel,
        grid=(micro, groups),
        in_specs=[
            pl.BlockSpec(memory_space=pltpu.SMEM),
            row_spec,
            key_spec,
            value_spec,
            row_spec,
            lse_spec,
            row_spec,
        ],
        out_specs=[row_spec, key_spec, key_spec],
        out_shape=[
            jax.ShapeDtypeStruct((micro, rows, width), bf16),
            jax.ShapeDtypeStruct((micro, count, width), bf16),
            jax.ShapeDtypeStruct((micro, count, width), bf16),
        ],
        compiler_params=pltpu.CompilerParams(vmem_limit_bytes=32 << 20),
        name="cross_backward",
    )(lengths, queries, pairs, pairs, out, lse, gout)


def gelu_parts(v):
    inner = 0.7978845608028654 * (v + 0.044715 * (v * v * v))
    t = jnp.tanh(inner)
    value = 0.5 * v * (1.0 + t)
    slope = 0.5 * (1.0 + t) + 0.5 * v * (1.0 - t * t) * (
        0.7978845608028654 * (1.0 + 3.0 * 0.044715 * (v * v))
    )
    return value, slope


def per_device(
    tokens,
    memory,
    cotangent,
    tile_segment,
    parents,
    memory_lengths,
    self_qkv,
    self_out,
    cross_q,
    cross_kv,
    cross_out,
    ffn_in,
    ffn_out,
    norm_gain,
    norm_bias,
):
    micro, _, row_count, width = tokens.shape
    seq = lax.axis_size("seq")
    total_rows = micro * row_count
    part = width // seq
    memory_rows = memory.shape[2]

    def gather(shard, axis=0):
        return lax.all_gather(shard, ALL, axis=axis, tiled=True)

    joint_weight = gather(self_qkv)
    norms = gather(jnp.concatenate([norm_gain, norm_bias], 0), 1).astype(f32)
    gain_rows, bias_rows = norms[:3], norms[3:]
    small = gather(jnp.concatenate([self_out, cross_q, cross_kv, cross_out, ffn_in], 1))
    memory_full = lax.all_gather(memory[:, 0], "seq", axis=1, tiled=True)
    down_weight = gather(ffn_out)
    cuts = [0]
    for shard in (self_out, cross_q, cross_kv, cross_out, ffn_in):
        cuts.append(cuts[-1] + shard.shape[1])
    self_output, cross_weight, pair_weight, cross_output, upward_weight = (
        small[:, a:b] for a, b in zip(cuts[:-1], cuts[1:])
    )

    x = tokens.reshape(total_rows, width)
    x32 = x.astype(f32)
    bias = jax.vmap(lambda t, p: tree_bias(t, p, BLOCK))(tile_segment[:, 0], parents[:, 0])
    lengths = memory_lengths[:, 0]

    def to_heads(rows, parts):
        blocks = rows.reshape(micro, row_count, parts, seq, part).transpose(0, 2, 3, 1, 4)
        swapped = lax.all_to_all(blocks, "seq", split_axis=2, concat_axis=2, tiled=True)
        return swapped.reshape(micro, parts, seq * row_count, part)

    def to_rows(heads, parts):
        blocks = heads.reshape(micro, parts, seq, row_count, part)
        swapped = lax.all_to_all(blocks, "seq", split_axis=2, concat_axis=2, tiled=True)
        return swapped.transpose(0, 3, 1, 2, 4).reshape(total_rows, parts * width)

    projected = dot_nn(x, joint_weight).astype(bf16)
    qkv = to_heads(projected, 3)
    attended_heads, self_lse = self_forward(qkv, bias)
    attended = to_rows(attended_heads, 1)

    mixed_first = residual_weight * x32 + dot_nn(attended, self_output)
    hidden_first = layer_norm(mixed_first, gain_rows[0], bias_rows[0])
    hidden_first_low = hidden_first.astype(bf16)
    cross_query = dot_nn(hidden_first_low, cross_weight).astype(bf16)
    cross_query = cross_query.reshape(micro, row_count, width)
    count = memory_full.shape[1]
    pairs = dot_nn(memory_full.reshape(micro * count, width), pair_weight).astype(bf16)
    pairs = pairs.reshape(micro, count, 2 * width)
    cross_heads, cross_lse = cross_forward(lengths, cross_query, pairs)
    cross_attended = cross_heads.reshape(total_rows, width)
    mixed_second = residual_weight * hidden_first + dot_nn(cross_attended, cross_output)
    hidden_second = layer_norm(mixed_second, gain_rows[1], bias_rows[1])
    hidden_second_low = hidden_second.astype(bf16)
    pre_active = dot_nn(hidden_second_low, upward_weight)
    active = gelu_parts(pre_active)[0].astype(bf16)
    mixed_third = residual_weight * hidden_second + dot_nn(active, down_weight)
    output = layer_norm(mixed_third, gain_rows[2], bias_rows[2]).astype(bf16)

    upstream = cotangent.reshape(total_rows, width).astype(f32)
    grad_third, gain_third, bias_third = layer_norm_back(mixed_third, gain_rows[2], upstream)
    branch_third = grad_third.astype(bf16)
    grad_down = dot_tn(active, branch_third).astype(bf16)
    grad_inner = (gelu_parts(pre_active)[1] * dot_nt(branch_third, down_weight)).astype(bf16)
    grad_upward = dot_tn(hidden_second_low, grad_inner).astype(bf16)

    def scatter(full, axis=0):
        return lax.psum_scatter(full, ALL, scatter_dimension=axis, tiled=True)

    own_down = scatter(grad_down).astype(f32)
    own_upward = scatter(grad_upward).astype(f32)

    grad_hidden_second = residual_weight * grad_third + dot_nt(grad_inner, upward_weight)
    grad_second, gain_second, bias_second = layer_norm_back(
        mixed_second, gain_rows[1], grad_hidden_second
    )
    branch_second = grad_second.astype(bf16)
    grad_cross_output = dot_tn(cross_attended, branch_second).astype(bf16)
    grad_cross_attended = dot_nt(branch_second, cross_output).astype(bf16)
    grad_cross_low, grad_keys, grad_values = cross_backward(
        lengths,
        cross_query,
        pairs,
        cross_heads,
        cross_lse,
        grad_cross_attended.reshape(micro, row_count, width),
    )
    memory_partial = jnp.concatenate([grad_keys, grad_values], 2)
    own_pairs = lax.psum_scatter(memory_partial, "seq", scatter_dimension=1, tiled=True)
    grad_cross_low = grad_cross_low.reshape(total_rows, width)
    grad_cross_weight = dot_tn(hidden_first_low, grad_cross_low).astype(bf16)
    grad_hidden_first = residual_weight * grad_second + dot_nt(grad_cross_low, cross_weight)
    grad_first, gain_first, bias_first = layer_norm_back(
        mixed_first, gain_rows[0], grad_hidden_first
    )
    branch_first = grad_first.astype(bf16)
    grad_self_output = dot_tn(attended, branch_first).astype(bf16)
    grad_attended = dot_nt(branch_first, self_output).astype(bf16)
    gout = to_heads(grad_attended, 1)
    own_three = scatter(
        jnp.concatenate([grad_self_output, grad_cross_weight, grad_cross_output], 1)
    ).astype(f32)
    grad_qkv = self_backward(qkv, bias, attended_heads, self_lse, gout[:, 0])
    grad_projected = to_rows(grad_qkv, 3)
    grad_joint = dot_tn(x, grad_projected).astype(bf16)
    grad_tokens = (residual_weight * grad_first + dot_nt(grad_projected, joint_weight)).astype(bf16)
    grad_pairs_low = own_pairs.reshape(micro * memory_rows, 2 * width)
    grad_pair_weight = dot_tn(memory.reshape(micro * memory_rows, width), grad_pairs_low)
    grad_memory = dot_nt(grad_pairs_low, pair_weight).astype(bf16)
    own_last = scatter(
        jnp.concatenate([grad_joint, grad_pair_weight.astype(bf16)], 1)
    ).astype(f32)
    norm_grads = jnp.stack(
        [gain_first, gain_second, gain_third, bias_first, bias_second, bias_third]
    )
    own_norms = scatter(norm_grads, 1)
    return (
        output.reshape(tokens.shape),
        grad_tokens.reshape(tokens.shape),
        grad_memory.reshape(memory.shape),
        own_last[:, : 3 * width],
        own_three[:, :width],
        own_three[:, width : 2 * width],
        own_last[:, 3 * width :],
        own_three[:, 2 * width :],
        own_upward,
        own_down,
        own_norms[:3],
        own_norms[3:],
    )


def solution(mesh):
    rows = P(None, "fsdp", "seq", None)
    weight = P(ALL, None)
    in_specs = (
        rows,
        rows,
        rows,
        P(None, "fsdp", None),
        P(None, "fsdp", None),
        P(None, "fsdp"),
    ) + (weight,) * 7 + (P(None, ALL),) * 2
    out_specs = (rows, rows, rows) + (weight,) * 7 + (P(None, ALL),) * 2
    return jax.shard_map(
        per_device, mesh=mesh, in_specs=in_specs, out_specs=out_specs, check_vma=False
    )
```

time: 3330 us -> 1400 us (0.42)
  waiting for transfers between devices: 2180 us -> 741 us
  matrix products: 514 us -> 165 us
  local copies, waits for them, and re-layouts: 397 us -> 88.6 us
  Pallas kernels: 0 us -> 221 us
  other arithmetic: 125 us -> 37.8 us
  blocking collectives: 75.9 us -> 116 us
    reduce_scatter x8 -> x3, waiting for transfers between devices: 1020 us -> 240 us  [the longest x2 240 us: scatter(): return lax.psum_scatter(full, ALL, scatter_dimension=axis, tiled=True)]
    all_gather x13 -> x4, waiting for transfers between devices: 699 us -> 69.3 us  [the longest x3 69.3 us: gather(): return lax.all_gather(shard, ALL, axis=axis, tiled=True)]
    dot_general x234 -> x27, matrix products: 514 us -> 165 us  [the longest x7 61.4 us: dot_nt(): lax.dot_general(a, b, (((1,), (1,)), ((), ())), preferred_element_type=f32)]
    unnamed x35 -> x13, waiting for transfers between devices: 466 us -> 151 us
    all_to_all x0 -> x3, waiting for transfers between devices: none -> 280 us  [the longest x1 156 us: to_heads(): lax.all_to_all(blocks, 'seq', split_axis=2, concat_axis=2, tiled=True)]
    pallas_call x0 -> x4, Pallas kernels: none -> 221 us  [the longest x1 94.7 us: self_backward(): pl.pallas_call(functools.partial(self_backward_kernel, heads, BLOCK), gri...]
    dynamic_slice x144 -> x0, local copies, waits for them, and re-layouts: 137 us -> none  [attend_forward(): lax.map(one_group, (head_split(queries), head_split(key_rows), head_split...]
    reshape x24 -> x7, local copies, waits for them, and re-layouts: 65.4 us -> 19 us  [the longest x1 8.36 us: to_rows(): return swapped.transpose(0, 3, 1, 2, 4).reshape(total_rows, parts * width)]
  transfers between devices with their start and end apart: 28 -> 13, of which waited for: 21 -> 6; matrix products, arithmetic and copies ran while one was open for 21% -> 15% of each run, Pallas kernels for 0% -> 14%
where the time goes in v1:
time: 1400 us
  waiting for transfers between devices  741 us (53%)
  Pallas kernels  221 us (16%)
  matrix products  165 us (12%)
  blocking collectives  116 us (8%)
  local copies, waits for them, and re-layouts  88.6 us (6%)
  other arithmetic  37.8 us (3%)
  between operations  15 us (1%)
    reduce_scatter x2, waiting for transfers between devices, scatter(): return lax.psum_scatter(full, ALL, scatter_dimension=axis, tiled=True)  240 us
    all_to_all x1, waiting for transfers between devices, to_heads(): lax.all_to_all(blocks, 'seq', split_axis=2, concat_axis=2, tiled=True)  156 us
    unnamed x13, waiting for transfers between devices  151 us
    all_to_all x2, waiting for transfers between devices, to_rows(): lax.all_to_all(blocks, 'seq', split_axis=2, concat_axis=2, tiled=True)  124 us
    pallas_call x1, Pallas kernels, self_backward(): pl.pallas_call(functools.partial(self_backward_kernel, heads, BLOCK), gri...  94.7 us
    pallas_call x1, Pallas kernels, self_forward(): pl.pallas_call(functools.partial(self_forward_kernel, heads, BLOCK), grid...  83.3 us
    all_gather x1, blocking collectives, gather(): return lax.all_gather(shard, ALL, axis=axis, tiled=True)  69.4 us
    all_gather x3, waiting for transfers between devices, gather(): return lax.all_gather(shard, ALL, axis=axis, tiled=True)  69.3 us
  transfers between devices with their start and end apart: 13, of which 6 were waited for; matrix products, arithmetic and copies ran while one was open for 15% of the time, Pallas kernels for 14%

profile of v1, /device:TPU:0, one launch (start us, length us, event | category | flops | bytes accessed | tf_op | source)
XLA Modules:
  0.0 1397.2 jit_solution(12390929386454027935)
XLA Ops:
  14.0 69.3 %all-gather.7.cloned.1.call-done = bf16[1024,3072]{1,0:T(8,128)(2,1)} async-done(((bf16[32,3072]{1,0:T(8,128)(2,1)}), bf16[1024,3072]{1,0:T(8,128)(2,1)}) %all-gather.7.cloned.1.call-update) | async-done | bytes 6291472 | tf_op jit(solution)/shard_map/all_gather | solution.py:448
  83.2 7.6 fusion.30
  90.8 1.4 copy.116
  92.2 3.4 copy.134
  95.6 4.8 all-to-all-start
  102.3 1.3 copy.90
  104.6 156.2 %all-to-all-done = bf16[3,3,8,256,128]{4,3,1,0,2:T(8,128)(2,1)} async-done(((bf16[3,3,8,256,128]{4,3,1,0,2:T(8,128)(2,1)}), bf16[3,3,8,256,128]{4,3,1,0,2:T(8,128)(2,1)}, u32[]{:S(2)}, u32[]{:S(2)}) %all-to-all-start) | async-done | bytes 4718624 | tf_op jit(solution)/shard_map/all_to_all | solution.py:470
  260.7 5.1 copy.89
  265.8 83.3 %self_forward.1 = (bf16[3,2048,128]{2,1,0:T(8,128)(2,1)S(1)}, f32[3,8,2,256]{3,2,1,0:T(2,128)S(1)}) custom-call(bf16[3,3,2048,128]{3,2,1,0:T(8,128)(2,1)} %bitcast.144, f32[3,8,8,2,256]{4,3,2,1,0:T(2,128)S(1)} %reshape.182.bias_ref), custom_call_target="tpu_custom_call" | custom-call | tf_op jit(solution)/shard_map/self_forward/pallas_call | solution.py:166
  349.1 1.3 copy.91
  350.4 1.1 copy-done
  351.6 3.6 all-to-all-start.1
  355.2 69.4 %all-gather.1 = bf16[32,32,6]{1,2,0:T(8,128)(2,1)S(1)} all-gather(bf16[1,32,6]{1,2,0:T(8,128)(2,1)S(1)} %maximum_bitcast_fusion), channel_id=1, replica_groups=mesh['seq'=8,'fsdp'=4] {'seq','fsdp'}, dimensions={0}, use_global_device_ids=true | all-gather | bytes 12672 | tf_op jit(solution)/shard_map/all_gather | solution.py:448
  426.6 4.5 fusion.92
  431.6 1.1 copy-done.18
  432.7 4.7 fusion.52
  437.4 6.2 fusion.18
  443.6 21.8 %cross_forward.1 = (bf16[3,256,1024]{2,1,0:T(8,128)(2,1)S(1)}, f32[3,8,2,256]{3,2,1,0:T(2,128)S(1)}) custom-call(s32[3]{0:T(128)S(1)} %bitcast.140, bf16[3,256,1024]{2,1,0:T(8,128)(2,1)S(1)} %bitcast.135, bf16[3,256,2048]{2,1,0:T(8,128)(2,1)S(1)} %bitcast.129, bf16[3,256,2048]{2,1,0:T(8,128)(2,1)S(1)} %bitcast.130), custom_call_target="tpu_custom_call" | custom-call | tf_op jit(solution)/shard_map/cross_forward/pallas_call | solution.py:318
  465.4 4.2 fusion.93
  470.1 1.1 copy-done.15
  471.3 13.0 fusion.12
  484.2 14.0 %fusion.94 = (f32[768]{0:T(1024)S(1)}, f32[768,1024]{1,0:T(8,128)S(1)}) fusion(bf16[4096,1024]{1,0:T(8,128)(2,1)} %all-gather.11.cloned.1.call-done, f32[768,4096]{1,0:T(8,128)} %fusion.12, f32[1024]{0:T(1024)S(1)} %bitcast.183, f32[1024]{0:T(1024)S(1)} %bitcast.167, f32[768]{0:T(1024)S(1)} %add_rsqrt_fusion.1, f32[768,1024]{1,0:T(8,128)} %copy-done.15, ...), kind=kOutput, calls=%fused_computation.142 | convolution fusion | flops 6476266496 | bytes 27280384 | tf_op jit(solution)/shard_map/dot_general | solution.py:25
  499.7 1.1 fusion.27
  500.8 2.3 fusion.24
  503.2 20.1 %fusion.9 = bf16[768,4096]{1,0:T(8,128)(2,1)} fusion(f32[768,4096]{1,0:T(8,128)} %fusion.12, bf16[4096,1024]{1,0:T(8,128)(2,1)} %all-gather.11.cloned.1.call-done, f32[768,1024]{1,0:T(8,128)S(1)} %get-tuple-element.98), kind=kOutput, calls=%fused_computation.11 | convolution fusion | flops 6499860480 | bytes 30408704 | tf_op jit(solution)/shard_map/dot_general | solution.py:29
  523.3 12.2 multiply_reduce_fusion
  536.7 4.6 fusion.55
  541.3 20.8 %cross_backward.1 = (bf16[3,256,1024]{2,1,0:T(8,128)(2,1)S(1)}, bf16[3,256,1024]{2,1,0:T(8,128)(2,1)S(1)}, bf16[3,256,1024]{2,1,0:T(8,128)(2,1)S(1)}) custom-call(s32[3]{0:T(128)S(1)} %bitcast.141, bf16[3,256,1024]{2,1,0:T(8,128)(2,1)S(1)} %bitcast.136, bf16[3,256,2048]{2,1,0:T(8,128)(2,1)S(1)} %bitcast.131, bf16[3,256,2048]{2,1,0:T(8,128)(2,1)S(1)} %bitcast.132, ...), custom_call_target="tpu_custom_call" | custom-call | tf_op jit(solution)/shard_map/cross_backward/pallas_call | solution.py:391
  562.1 1.1 copy-done.10
  563.2 2.0 pad_maximum_fusion.2
  565.3 1.3 copy-done.11
  566.6 6.8 multiply_reduce_fusion.1
  574.6 3.8 subtract_multiply_fusion
  579.1 3.2 convolution_convert_fusion.3
  582.3 3.2 convolution_convert_fusion.5
  585.5 3.3 convolution_convert_fusion.4
  588.9 6.1 pad_maximum_fusion.1
  595.0 8.7 copy.108
  603.7 1.9 copy-done.24
  605.6 13.8 convolution_convert_fusion
  619.5 1.8 copy-done.17
  621.3 12.1 convolution_convert_fusion.1
  633.5 1.9 copy-done.22
  635.3 3.4 fusion.62
  639.6 46.3 %all_to_all.20 = bf16[3,1,8,256,128]{4,3,0,1,2:T(8,128)(2,1)S(1)} all-to-all(bf16[3,1,8,256,128]{4,3,0,1,2:T(8,128)(2,1)S(1)} %bitcast.151), channel_id=1, replica_groups=mesh['seq'=8,'fsdp'=4] {'seq'}, dimensions={2} | all-to-all | bytes 3145728 | tf_op jit(solution)/shard_map/all_to_all | solution.py:470
  686.1 94.7 %self_backward.1 = bf16[3,3,2048,128]{3,2,1,0:T(8,128)(2,1)} custom-call(bf16[3,3,2048,128]{3,2,1,0:T(8,128)(2,1)} %bitcast.145, f32[3,8,8,2,256]{4,3,2,1,0:T(2,128)S(1)} %copy-done.5, bf16[3,2048,128]{2,1,0:T(8,128)(2,1)S(1)} %copy-done.1, f32[3,8,2,256]{3,2,1,0:T(2,128)S(1)} %get-tuple-element.23.lse_ref, bf16[3,2048,128]{2,1,0:T(8,128)(2,1)S(1)} %bitcast.134), custom_call_target="tpu_custom_call" | custom-call | tf_op jit(solution)/shard_map/self_backward/pallas_call | solution.py:266
  780.8 5.0 copy.96
  785.8 4.8 all-to-all-start.3
  791.0 4.4 convert_bitcast_fusion.1
  795.4 124.3 %all-to-all-done.3 = bf16[3,3,8,256,128]{4,3,1,0,2:T(8,128)(2,1)} async-done(((bf16[3,3,8,256,128]{4,3,1,0,2:T(8,128)(2,1)}), bf16[3,3,8,256,128]{4,3,1,0,2:T(8,128)(2,1)}, u32[]{:S(2)}, u32[]{:S(2)}) %all-to-all-start.3) | async-done | bytes 4718624 | tf_op jit(solution)/shard_map/all_to_all | solution.py:475
  919.7 7.5 copy.97
  927.1 8.4 reshape.194
  935.5 7.8 convert_bitcast_fusion
  943.4 15.7 %pad_maximum_fusion = bf16[1024,5120]{0,1:T(8,128)(2,1)} fusion(bf16[1024,2048]{0,1:T(8,128)(2,1)S(1)} %copy-done.12, bf16[1024,3072]{0,1:T(8,128)(2,1)S(1)} %convert_bitcast_fusion), kind=kLoop, calls=%fused_computation.13 | loop fusion | flops 20971520 | bytes 20971520 | tf_op jit(solution)/shard_map/concatenate | solution.py:552
  959.1 13.8 copy.106
  975.1 4.3 fusion.67
  979.4 1.3 copy.109
  983.3 9.9 add_convert_fusion
  993.3 95.1 %reduce-scatter.17.cloned.1.call-done = bf16[128,1024]{1,0:T(8,128)(2,1)} async-done(((bf16[4096,1024]{1,0:T(8,128)(2,1)}), bf16[128,1024]{1,0:T(8,128)(2,1)}) %reduce-scatter.17.cloned.1.call-update) | async-done | bytes 262160 | tf_op jit(solution)/shard_map/reduce_scatter | solution.py:509
  1088.3 1.8 convert_element_type.149
  1090.1 145.0 %reduce-scatter.15.cloned.1.call-done = bf16[32,4096]{1,0:T(8,128)(2,1)} async-done(((bf16[1024,4096]{1,0:T(8,128)(2,1)}), bf16[32,4096]{1,0:T(8,128)(2,1)}) %reduce-scatter.15.cloned.1.call-update) | async-done | bytes 262160 | tf_op jit(solution)/shard_map/reduce_scatter | solution.py:509
  1235.1 1.8 convert_element_type.147
  1236.9 149.3 %reduce-scatter.19.cloned.1.call-done = bf16[32,5120]{1,0:T(8,128)(2,1)} async-done(((bf16[1024,5120]{1,0:T(8,128)(2,1)}), bf16[32,5120]{1,0:T(8,128)(2,1)}) %reduce-scatter.19.cloned.1.call-update) | async-done | bytes 327696
  1389.0 1.2 copy.101
  (151 shorter events, 26.1 us)
Async XLA Ops:
  7.2 76.1 %all-gather.7.cloned.1.call-start = ((), (), s32[]{:S(2)}) async-start(), calls=%async_computation.10 | async-start | bytes 6488064 | tf_op jit(solution)/shard_map/all_gather | solution.py:448
  7.9 418.7 %all-gather.9.cloned.1.call-start = ((), (), s32[]{:S(2)}) async-start(), calls=%async_computation.11 | async-start | bytes 19464192 | tf_op jit(solution)/shard_map/all_gather | solution.py:448
  12.4 0.8 copy-start.32
  13.2 424.2 %all-gather.13.cloned.1.call-start = ((), (), s32[]{:S(2)}) async-start(), calls=%async_computation.16 | async-start | bytes 1769472 | tf_op jit(solution)/shard_map/all_gather | solution.py:454
  95.6 5.4 copy-start.33
  95.6 5.4 copy-start.34
  95.6 165.1 %all-to-all-start = ((bf16[3,3,8,256,128]{4,3,1,0,2:T(8,128)(2,1)}), bf16[3,3,8,256,128]{4,3,1,0,2:T(8,128)(2,1)}, u32[]{:S(2)}, u32[]{:S(2)}) async-start(bf16[3,3,8,256,128]{4,3,1,0,2:T(8,128)(2,1)} %bitcast.146), calls=%async_computation | async-start | bytes 9437184 | tf_op jit(solution)/shard_map/all_to_all | solution.py:470
  100.4 383.8 %all-gather.11.cloned.1.call-start = ((), (), s32[]{:S(2)}) async-start(), calls=%async_computation.12 | async-start | bytes 8650752 | tf_op jit(solution)/shard_map/all_gather | solution.py:448
  104.5 161.3 %copy-start.4 = (f32[3,8,8,2,256]{4,3,2,1,0:T(2,128)}, f32[3,8,8,2,256]{4,3,2,1,0:T(2,128)S(1)}, u32[]{:S(2)}) copy-start(f32[3,8,8,2,256]{4,3,2,1,0:T(2,128)S(1)} %reshape.182.bias_ref) | copy-start | bytes 1179652
  349.1 6.1 copy-start.35
  349.1 6.1 copy-start.36
  349.1 75.6 %copy-start.13 = (bf16[3,1,256,1024]{3,2,1,0:T(8,128)(2,1)S(1)}, bf16[3,1,256,1024]{3,2,1,0:T(8,128)(2,1)}, u32[]{:S(2)}) copy-start(bf16[3,1,256,1024]{3,2,1,0:T(8,128)(2,1)} %param.17) | copy-start | bytes 4718596
  350.4 1.1 copy-start
  351.6 74.0 %all-to-all-start.1 = ((bf16[3,1,8,256,128]{4,3,0,1,2:T(8,128)(2,1)}), bf16[3,1,8,256,128]{4,3,0,1,2:T(8,128)(2,1)S(1)}, u32[]{:S(2)}, u32[]{:S(2)}) async-start(bf16[3,1,8,256,128]{4,3,0,1,2:T(8,128)(2,1)} %copy.91), calls=%async_computation.1 | async-start | bytes 3145728 | tf_op jit(solution)/shard_map/all_to_all | solution.py:475
  355.1 435.9 %reduce-scatter.13.cloned.1.call-start = ((), (), s32[]{:S(2)}) async-start(), calls=%async_computation.13 | async-start | bytes 3538944 | tf_op jit(solution)/shard_map/reduce_scatter | solution.py:530
  426.6 4.5 copy-start.27
  431.1 1.6 copy-start.18
  437.4 6.2 copy-start.2
  437.4 6.2 copy-start.9
  443.6 21.8 %copy-start.19 = (f32[768,1024]{1,0:T(8,128)S(1)}, f32[768,1024]{1,0:T(8,128)}, u32[]{:S(2)}) copy-start(f32[768,1024]{1,0:T(8,128)} %copy-done.18) | copy-start | bytes 9437188
  465.4 4.2 copy-start.6
  469.6 1.6 copy-start.15
  498.3 1.4 copy-start.14
  503.2 20.1 %copy-start.23 = (f32[768,1024]{1,0:T(8,128)}, f32[768,1024]{1,0:T(8,128)S(1)}, u32[]{:S(2)}) copy-start(f32[768,1024]{1,0:T(8,128)S(1)} %get-tuple-element.98) | copy-start | bytes 9437188
  503.2 20.1 %copy-start.16 = (f32[768,1024]{1,0:T(8,128)S(1)}, f32[768,1024]{1,0:T(8,128)}, u32[]{:S(2)}) copy-start(f32[768,1024]{1,0:T(8,128)} %copy-done.15) | copy-start | bytes 9437188
  536.6 4.6 copy-start.25
  536.6 4.6 copy-start.3
  536.7 4.6 copy-start.7
  562.1 1.1 copy-start.10
  565.2 1.4 copy-start.11
  565.3 407.7 %reduce-scatter.23.cloned.1.call-start = ((), (), s32[]{:S(2)}) async-start(), calls=%async_computation.19 | async-start | bytes 540672
  574.5 3.8 copy-start.8
  574.5 4.5 copy-start.26
  579.1 3.2 copy-start.21
  579.1 3.2 copy-start.28
  582.3 3.2 copy-start.20
  588.8 390.6 %reduce-scatter.21.cloned.1.call-start = ((), (), s32[]{:S(2)}) async-start(), calls=%async_computation.18 | async-start | bytes 6488064
  603.6 2.0 copy-start.24
  603.7 484.6 %reduce-scatter.17.cloned.1.call-start = ((), (), s32[]{:S(2)}) async-start(), calls=%async_computation.15 | async-start | bytes 8650752 | tf_op jit(solution)/shard_map/reduce_scatter | solution.py:509
  619.4 1.9 copy-start.17
  619.5 615.7 %reduce-scatter.15.cloned.1.call-start = ((), (), s32[]{:S(2)}) async-start(), calls=%async_computation.14 | async-start | bytes 8650752 | tf_op jit(solution)/shard_map/reduce_scatter | solution.py:509
  633.4 1.9 copy-start.22
  639.6 46.4 %copy-start.1 = (bf16[3,2048,128]{2,1,0:T(8,128)(2,1)S(1)}, bf16[3,2048,128]{2,1,0:T(8,128)(2,1)}, u32[]{:S(2)}) copy-start(bf16[3,2048,128]{2,1,0:T(8,128)(2,1)} %copy-done) | copy-start | bytes 4718596
  639.6 46.4 %copy-start.5 = (f32[3,8,8,2,256]{4,3,2,1,0:T(2,128)S(1)}, f32[3,8,8,2,256]{4,3,2,1,0:T(2,128)}, u32[]{:S(2)}) copy-start(f32[3,8,8,2,256]{4,3,2,1,0:T(2,128)} %copy-done.4) | copy-start | bytes 1179652
  785.8 5.3 copy-start.31
  785.8 133.9 %all-to-all-start.3 = ((bf16[3,3,8,256,128]{4,3,1,0,2:T(8,128)(2,1)}), bf16[3,3,8,256,128]{4,3,1,0,2:T(8,128)(2,1)}, u32[]{:S(2)}, u32[]{:S(2)}) async-start(bf16[3,3,8,256,128]{4,3,1,0,2:T(8,128)(2,1)} %copy.96), calls=%async_computation.3 | async-start | bytes 9437184 | tf_op jit(solution)/shard_map/all_to_all | solution.py:475
  790.5 595.6 %reduce-scatter.19.cloned.1.call-start = ((), (), s32[]{:S(2)}) async-start(), calls=%async_computation.17 | async-start | bytes 10813440
  927.1 8.4 copy-start.37
  935.5 7.8 copy-start.12
  972.9 2.2 copy-start.29
  1386.2 2.4 copy-start.30
Sparse Core Ops, SparseCore 0:
  10.9 72.2 all-gather.6
  86.7 204.5 all-gather.8
  293.5 43.0 all-gather.12
  339.3 96.1 all-gather.10
  565.4 77.9 reduce-scatter.12
  646.0 134.5 reduce-scatter.22
  787.2 150.4 reduce-scatter.20
  940.0 148.2 reduce-scatter.16
  1090.6 144.4 reduce-scatter.14
  1237.3 148.8 reduce-scatter.18

commit v2 on v1

--- a/solution.py
+++ b/solution.py
@@ -19,6 +19,7 @@
 ALL = ("seq", "fsdp")
 f32 = jnp.float32
 bf16 = jnp.bfloat16
+MESH = pl.DeviceIdType.MESH
 
 
 def dot_nn(a, b):
@@ -95,196 +96,379 @@
     return value if heads == 1 else jnp.where(mask, value, jnp.zeros_like(value))
 
 
-def self_forward_kernel(heads, block, qkv_ref, bias_ref, out_ref, lse_ref, queries, values_t):
-    length, width = qkv_ref.shape[2], qkv_ref.shape[3]
+def greet(peers):
+    barrier = pltpu.get_barrier_semaphore()
+    for peer in peers:
+        pl.semaphore_signal(barrier, inc=1, device_id=peer, device_id_type=MESH)
+    pl.semaphore_wait(barrier, len(peers))
+
+
+def peer_at(step):
+    count = lax.axis_size("seq")
+    return lax.rem(lax.axis_index("seq") + step, count)
+
+
+def rows_at(i, count):
+    return pl.ds(pl.multiple_of(i * count, count), count)
+
+
+def cut_heads(rows_ref, m, parts, blocks_ref):
+    seq, part = blocks_ref.shape[2], blocks_ref.shape[4]
+    for p in range(parts):
+        for s in range(seq):
+            first = (p * seq + s) * part
+            blocks_ref[m, p, s] = rows_ref[m, :, first : first + part]
+
+
+def join_heads(blocks_ref, m, parts, rows_ref):
+    seq, part = blocks_ref.shape[2], blocks_ref.shape[4]
+    for p in range(parts):
+        for s in range(seq):
+            first = (p * seq + s) * part
+            rows_ref[m, :, first : first + part] = blocks_ref[m, p, s]
+
+
+def to_peer(source_ref, target_ref, send, receive, m, step):
+    rows = source_ref.shape[3]
+    return pltpu.make_async_remote_copy(
+        src_ref=source_ref.at[m, :, peer_at(step)],
+        dst_ref=target_ref.at[m, :, rows_at(lax.axis_index("seq"), rows)],
+        send_sem=send.at[m, step],
+        recv_sem=receive.at[m, step],
+        device_id={"seq": peer_at(step)},
+        device_id_type=MESH,
+    )
+
+
+def to_self(source_ref, target_ref, sem, m):
+    rows = source_ref.shape[3]
+    me = lax.axis_index("seq")
+    return pltpu.make_async_copy(
+        source_ref.at[m, :, me], target_ref.at[m, :, rows_at(me, rows)], sem.at[m, 0]
+    )
+
+
+def send_blocks(source_ref, target_ref, send, receive, m):
+    for step in range(1, lax.axis_size("seq")):
+        to_peer(source_ref, target_ref, send, receive, m, step).start()
+    to_self(source_ref, target_ref, send, m).start()
+
+
+def take_blocks(source_ref, target_ref, send, receive, m):
+    for step in range(1, lax.axis_size("seq")):
+        to_peer(source_ref, target_ref, send, receive, m, step).wait_recv()
+    to_self(source_ref, target_ref, send, m).wait()
+
+
+def home_copy(source_ref, target_ref, send, receive, m, place):
+    rows = target_ref.shape[3]
+    me = lax.axis_index("seq")
+    count = lax.axis_size("seq")
+    step = lax.rem(place - me + count, count)
+    return pltpu.make_async_remote_copy(
+        src_ref=source_ref.at[m, :, rows_at(place, rows)],
+        dst_ref=target_ref.at[m, :, me],
+        send_sem=send.at[m, step],
+        recv_sem=receive.at[m, step],
+        device_id={"seq": place},
+        device_id_type=MESH,
+    )
+
+
+def home_self(source_ref, target_ref, sem, m):
+    rows = target_ref.shape[3]
+    me = lax.axis_index("seq")
+    return pltpu.make_async_copy(
+        source_ref.at[m, :, rows_at(me, rows)], target_ref.at[m, :, me], sem.at[m, 0]
+    )
+
+
+def send_home(source_ref, target_ref, send, receive, m, place):
+    me = lax.axis_index("seq")
+
+    @pl.when(place != me)
+    def _():
+        home_copy(source_ref, target_ref, send, receive, m, place).start()
+
+    @pl.when(place == me)
+    def _():
+        home_self(source_ref, target_ref, send, m).start()
+
+
+def take_home(source_ref, target_ref, send, receive, m):
+    for step in range(1, lax.axis_size("seq")):
+        home_copy(source_ref, target_ref, send, receive, m, peer_at(step)).wait()
+    home_self(source_ref, target_ref, send, m).wait()
+
+
+def self_forward_kernel(
+    heads, block, rows_ref, bias_ref, qkv_ref, out_ref, lse_ref, attended_ref,
+    cut, back, queries, values_t, send_in, take_in, send_out, take_out,
+):
+    micro, _, length, width = qkv_ref.shape
+    seq = lax.axis_size("seq")
     blocks = length // block
     per = block // TILE
+    place_rows = length // seq
     masks = head_masks((block, width), heads)
-
-    def prepare(i, carry):
-        rows = pl.ds(pl.multiple_of(i * block, block), block)
-        q = qkv_ref[0, 0, rows, :].astype(f32) * scale_factor
-        for h in range(heads):
-            queries[h, rows, :] = keep_head(q, masks[h], heads).astype(bf16)
-        values_t[i] = jnp.transpose(qkv_ref[0, 2, rows, :].astype(f32)).astype(bf16)
+    greet([{"seq": peer_at(step)} for step in range(1, seq)])
+
+    def launch(m, carry):
+        cut_heads(rows_ref, m, 3, cut)
+
+        @pl.when(m < 2)
+        def _():
+            send_blocks(cut, qkv_ref, send_in, take_in, m)
+
         return carry
 
-    lax.fori_loop(0, blocks, prepare, 0)
+    lax.fori_loop(0, micro, launch, 0)
     key_place = lax.broadcasted_iota(jnp.int32, (block, block), 0)
     query_place = lax.broadcasted_iota(jnp.int32, (block, block), 1)
     causal = key_place <= query_place
 
-    def scores_of(i, j, h):
-        rows = pl.ds(pl.multiple_of(i * block, block), block)
-        keys = qkv_ref[0, 1, pl.ds(pl.multiple_of(j * block, block), block), :]
-        raw = dot_nt(keys, queries[h, rows, :])
-        bias = bias_ref[0, j, i]
-        return (raw.reshape(per, TILE, block) + bias[:, None, :]).reshape(block, block)
-
-    def query_block(i, carry):
-        state = []
-        for h in range(heads):
-            s = jnp.where(causal, scores_of(i, i, h), masked_score)
-            m = jnp.max(s, 0, keepdims=True)
-            p = jnp.exp(s - m)
-            total = jnp.sum(p, 0, keepdims=True)
-            acc = dot_nn(values_t[i][h * HD : (h + 1) * HD], p.astype(bf16))
-            state += [m, total, acc]
-
-        def key_block(j, state):
-            fresh = []
+    def one_micro(m, carry):
+        take_blocks(cut, qkv_ref, send_in, take_in, m)
+
+        @pl.when(m + 2 < micro)
+        def _():
+            send_blocks(cut, qkv_ref, send_in, take_in, m + 2)
+
+        def prepare(i, carry):
+            rows = rows_at(i, block)
+            q = qkv_ref[m, 0, rows, :].astype(f32) * scale_factor
             for h in range(heads):
-                m, total, acc = state[3 * h : 3 * h + 3]
-                s = scores_of(i, j, h)
-                m_new = jnp.maximum(m, jnp.max(s, 0, keepdims=True))
-                shrink = jnp.exp(m - m_new)
-                p = jnp.exp(s - m_new)
-                total = total * shrink + jnp.sum(p, 0, keepdims=True)
-                acc = acc * shrink + dot_nn(values_t[j][h * HD : (h + 1) * HD], p.astype(bf16))
-                fresh += [m_new, total, acc]
-            return tuple(fresh)
-
-        state = lax.fori_loop(0, i, key_block, tuple(state))
-        out = jnp.concatenate(
-            [state[3 * h + 2] * (1.0 / state[3 * h + 1]) for h in range(heads)], 0
-        )
-        out_ref[0, pl.ds(pl.multiple_of(i * block, block), block), :] = jnp.transpose(out).astype(
-            bf16
-        )
-        lse_ref[0, i] = jnp.concatenate(
-            [state[3 * h] + jnp.log(state[3 * h + 1]) for h in range(heads)], 0
-        )
+                queries[h, rows, :] = keep_head(q, masks[h], heads).astype(bf16)
+            values_t[i] = jnp.transpose(qkv_ref[m, 2, rows, :].astype(f32)).astype(bf16)
+            return carry
+
+        lax.fori_loop(0, blocks, prepare, 0)
+
+        def scores_of(i, j, h):
+            raw = dot_nt(qkv_ref[m, 1, rows_at(j, block), :], queries[h, rows_at(i, block), :])
+            bias = bias_ref[m, j, i]
+            return (raw.reshape(per, TILE, block) + bias[:, None, :]).reshape(block, block)
+
+        def query_block(i, carry):
+            state = []
+            for h in range(heads):
+                s = jnp.where(causal, scores_of(i, i, h), masked_score)
+                top = jnp.max(s, 0, keepdims=True)
+                p = jnp.exp(s - top)
+                total = jnp.sum(p, 0, keepdims=True)
+                acc = dot_nn(values_t[i][h * HD : (h + 1) * HD], p.astype(bf16))
+                state += [top, total, acc]
+
+            def key_block(j, state):
+                fresh = []
+                for h in range(heads):
+                    top, total, acc = state[3 * h : 3 * h + 3]
+                    s = scores_of(i, j, h)
+                    higher = jnp.maximum(top, jnp.max(s, 0, keepdims=True))
+                    shrink = jnp.exp(top - higher)
+                    p = jnp.exp(s - higher)
+                    total = total * shrink + jnp.sum(p, 0, keepdims=True)
+                    acc = acc * shrink + dot_nn(
+                        values_t[j][h * HD : (h + 1) * HD], p.astype(bf16)
+                    )
+                    fresh += [higher, total, acc]
+                return tuple(fresh)
+
+            state = lax.fori_loop(0, i, key_block, tuple(state))
+            out = jnp.concatenate(
+                [state[3 * h + 2] * (1.0 / state[3 * h + 1]) for h in range(heads)], 0
+            )
+            out_ref[m, 0, rows_at(i, block), :] = jnp.transpose(out).astype(bf16)
+            lse_ref[m, i] = jnp.concatenate(
+                [state[3 * h] + jnp.log(state[3 * h + 1]) for h in range(heads)], 0
+            )
+            for sub in range(block // place_rows):
+                place = i * (block // place_rows) + sub
+                send_home(out_ref, back, send_out, take_out, m, place)
+            return carry
+
+        lax.fori_loop(0, blocks, query_block, 0)
         return carry
 
-    lax.fori_loop(0, blocks, query_block, 0)
-
-
-def self_forward(qkv, bias):
-    micro, _, length, width = qkv.shape
-    heads = width // HD
+    lax.fori_loop(0, micro, one_micro, 0)
+
+    def finish(m, carry):
+        for step in range(1, seq):
+            to_peer(cut, qkv_ref, send_in, take_in, m, step).wait_send()
+        take_home(out_ref, back, send_out, take_out, m)
+        join_heads(back, m, 1, attended_ref)
+        return carry
+
+    lax.fori_loop(0, micro, finish, 0)
+
+
+def self_forward(projected, bias, seq):
+    micro, rows, width = projected.shape
+    part = width // 3 // seq
+    heads = part // HD
+    length = rows * seq
     blocks = length // BLOCK
+    whole = pl.BlockSpec(memory_space=pltpu.VMEM)
+    sems = pltpu.SemaphoreType.DMA((micro, seq))
     return pl.pallas_call(
         functools.partial(self_forward_kernel, heads, BLOCK),
-        grid=(micro,),
-        in_specs=[
-            pl.BlockSpec((1, 3, length, width), lambda m: (m, 0, 0, 0)),
-            pl.BlockSpec((1,) + bias.shape[1:], lambda m: (m, 0, 0, 0, 0)),
-        ],
-        out_specs=[
-            pl.BlockSpec((1, length, width), lambda m: (m, 0, 0)),
-            pl.BlockSpec((1, blocks, heads, BLOCK), lambda m: (m, 0, 0, 0)),
-        ],
+        in_specs=[whole, whole],
+        out_specs=[whole] * 4,
         out_shape=[
-            jax.ShapeDtypeStruct((micro, length, width), bf16),
+            jax.ShapeDtypeStruct((micro, 3, length, part), bf16),
+            jax.ShapeDtypeStruct((micro, 1, length, part), bf16),
             jax.ShapeDtypeStruct((micro, blocks, heads, BLOCK), f32),
+            jax.ShapeDtypeStruct((micro, rows, width // 3), bf16),
         ],
         scratch_shapes=[
-            pltpu.VMEM((heads, length, width), bf16),
-            pltpu.VMEM((blocks, width, BLOCK), bf16),
+            pltpu.VMEM((micro, 3, seq, rows, part), bf16),
+            pltpu.VMEM((micro, 1, seq, rows, part), bf16),
+            pltpu.VMEM((heads, length, part), bf16),
+            pltpu.VMEM((blocks, part, BLOCK), bf16),
+            sems,
+            sems,
+            sems,
+            sems,
         ],
-        compiler_params=pltpu.CompilerParams(vmem_limit_bytes=48 << 20),
+        compiler_params=pltpu.CompilerParams(
+            vmem_limit_bytes=50 << 20, collective_id=1, has_side_effects=True
+        ),
         name="self_forward",
-    )(qkv, bias)
+    )(projected, bias)
 
 
 def self_backward_kernel(
-    heads, block, qkv_ref, bias_ref, out_ref, lse_ref, gout_ref, grad_ref,
-    queries, keys_h, gouts, delta, grad_q,
+    heads, block, rows_ref, qkv_ref, bias_ref, out_ref, lse_ref, grad_ref,
+    cut, gout, grads, back, queries, keys_h, gouts, delta, grad_q,
+    send_in, take_in, send_out, take_out,
 ):
-    length, width = qkv_ref.shape[2], qkv_ref.shape[3]
+    micro, _, length, width = qkv_ref.shape
+    seq = lax.axis_size("seq")
     blocks = length // block
     per = block // TILE
+    place_rows = length // seq
     masks = head_masks((block, width), heads)
     lane = lax.broadcasted_iota(jnp.int32, (8, width), 1)
-    row = lax.broadcasted_iota(jnp.int32, (8, width), 0)
-    pick = jnp.where(lane // HD == row, 1.0, 0.0)
-
-    def prepare(i, carry):
-        rows = pl.ds(pl.multiple_of(i * block, block), block)
-        q = qkv_ref[0, 0, rows, :].astype(f32) * scale_factor
-        k = qkv_ref[0, 1, rows, :].astype(f32)
-        g = gout_ref[0, rows, :].astype(f32)
-        for h in range(heads):
-            queries[h, rows, :] = keep_head(q, masks[h], heads).astype(bf16)
-            keys_h[h, rows, :] = keep_head(k, masks[h], heads).astype(bf16)
-            gouts[h, rows, :] = keep_head(g, masks[h], heads).astype(bf16)
-        products = g * out_ref[0, rows, :].astype(f32)
-        delta[i] = lax.dot_general(
-            pick,
-            products,
-            (((1,), (1,)), ((), ())),
-            precision=lax.Precision.HIGHEST,
-            preferred_element_type=f32,
-        )
-        grad_q[rows, :] = jnp.zeros((block, width), f32)
+    first_lane = lax.broadcasted_iota(jnp.int32, (8, width), 0) * HD
+    pick = jnp.where((lane >= first_lane) & (lane < first_lane + HD), 1.0, 0.0)
+    greet([{"seq": peer_at(step)} for step in range(1, seq)])
+
+    def launch(m, carry):
+        cut_heads(rows_ref, m, 1, cut)
+        send_blocks(cut, gout, send_in, take_in, m)
         return carry
 
-    lax.fori_loop(0, blocks, prepare, 0)
+    lax.fori_loop(0, micro, launch, 0)
     key_place = lax.broadcasted_iota(jnp.int32, (block, block), 0)
     query_place = lax.broadcasted_iota(jnp.int32, (block, block), 1)
     causal = key_place <= query_place
 
-    def key_block(j, carry):
-        krows = pl.ds(pl.multiple_of(j * block, block), block)
-        keys = qkv_ref[0, 1, krows, :]
-        values = qkv_ref[0, 2, krows, :]
-
-        def pair(i, grad_k, grad_v, diagonal):
-            rows = pl.ds(pl.multiple_of(i * block, block), block)
-            bias = bias_ref[0, j, i]
-            gq = grad_q[rows, :]
+    def one_micro(m, carry):
+        take_blocks(cut, gout, send_in, take_in, m)
+
+        def prepare(i, carry):
+            rows = rows_at(i, block)
+            q = qkv_ref[m, 0, rows, :].astype(f32) * scale_factor
+            k = qkv_ref[m, 1, rows, :].astype(f32)
+            g = gout[m, 0, rows, :].astype(f32)
             for h in range(heads):
-                raw = dot_nt(keys, queries[h, rows, :]).reshape(per, TILE, block)
-                shift = bias - lse_ref[0, i, h : h + 1, :]
-                s = (raw + shift[:, None, :]).reshape(block, block)
-                if diagonal:
-                    s = jnp.where(causal, s, masked_score)
-                p = jnp.exp(s)
-                gp = dot_nt(values, gouts[h, rows, :])
-                gs = (p * (gp - delta[i, h : h + 1, :])).astype(bf16)
-                grad_v = grad_v + dot_nn(p.astype(bf16), gouts[h, rows, :])
-                grad_k = grad_k + dot_nn(gs, queries[h, rows, :])
-                gq = gq + dot_tn(gs, keys_h[h, krows, :])
-            grad_q[rows, :] = gq
-            return grad_k, grad_v
-
-        zero = jnp.zeros((block, width), f32)
-        state = pair(j, zero, zero, True)
-        state = lax.fori_loop(j + 1, blocks, lambda i, s: pair(i, s[0], s[1], False), state)
-        grad_ref[0, 1, krows, :] = state[0].astype(bf16)
-        grad_ref[0, 2, krows, :] = state[1].astype(bf16)
+                queries[h, rows, :] = keep_head(q, masks[h], heads).astype(bf16)
+                keys_h[h, rows, :] = keep_head(k, masks[h], heads).astype(bf16)
+                gouts[h, rows, :] = keep_head(g, masks[h], heads).astype(bf16)
+            delta[i] = lax.dot_general(
+                pick,
+                g * out_ref[m, 0, rows, :].astype(f32),
+                (((1,), (1,)), ((), ())),
+                precision=lax.Precision.HIGHEST,
+                preferred_element_type=f32,
+            )
+            grad_q[rows, :] = jnp.zeros((block, width), f32)
+            return carry
+
+        lax.fori_loop(0, blocks, prepare, 0)
+
+        def key_block(j, carry):
+            krows = rows_at(j, block)
+
+            def pair(i, grad_k, grad_v, diagonal):
+                rows = rows_at(i, block)
+                bias = bias_ref[m, j, i]
+                gq = grad_q[rows, :]
+                for h in range(heads):
+                    raw = dot_nt(qkv_ref[m, 1, krows, :], queries[h, rows, :])
+                    shift = bias - lse_ref[m, i, h : h + 1, :]
+                    s = (raw.reshape(per, TILE, block) + shift[:, None, :]).reshape(block, block)
+                    if diagonal:
+                        s = jnp.where(causal, s, masked_score)
+                    p = jnp.exp(s)
+                    gp = dot_nt(qkv_ref[m, 2, krows, :], gouts[h, rows, :])
+                    gs = (p * (gp - delta[i, h : h + 1, :])).astype(bf16)
+                    grad_v = grad_v + dot_nn(p.astype(bf16), gouts[h, rows, :])
+                    grad_k = grad_k + dot_nn(gs, queries[h, rows, :])
+                    gq = gq + dot_tn(gs, keys_h[h, krows, :])
+                grad_q[rows, :] = gq
+                return grad_k, grad_v
+
+            zero = jnp.zeros((block, width), f32)
+            state = pair(j, zero, zero, True)
+            state = lax.fori_loop(
+                j + 1, blocks, lambda i, s: pair(i, s[0], s[1], False), state
+            )
+            grads[m, 0, krows, :] = (grad_q[krows, :] * scale_factor).astype(bf16)
+            grads[m, 1, krows, :] = state[0].astype(bf16)
+            grads[m, 2, krows, :] = state[1].astype(bf16)
+            for sub in range(block // place_rows):
+                place = j * (block // place_rows) + sub
+                send_home(grads, back, send_out, take_out, m, place)
+            return carry
+
+        lax.fori_loop(0, blocks, key_block, 0)
         return carry
 
-    lax.fori_loop(0, blocks, key_block, 0)
-    grad_ref[0, 0] = (grad_q[...] * scale_factor).astype(bf16)
-
-
-def self_backward(qkv, bias, out, lse, gout):
-    micro, _, length, width = qkv.shape
-    heads = width // HD
+    lax.fori_loop(0, micro, one_micro, 0)
+
+    def finish(m, carry):
+        for step in range(1, seq):
+            to_peer(cut, gout, send_in, take_in, m, step).wait_send()
+        take_home(grads, back, send_out, take_out, m)
+        join_heads(back, m, 3, grad_ref)
+        return carry
+
+    lax.fori_loop(0, micro, finish, 0)
+
+
+def self_backward(grad_attended, qkv, bias, out, lse, seq):
+    micro, rows, width = grad_attended.shape
+    length, part = qkv.shape[2:]
+    heads = part // HD
     blocks = length // BLOCK
+    whole = pl.BlockSpec(memory_space=pltpu.VMEM)
+    sems = pltpu.SemaphoreType.DMA((micro, seq))
     return pl.pallas_call(
         functools.partial(self_backward_kernel, heads, BLOCK),
-        grid=(micro,),
-        in_specs=[
-            pl.BlockSpec((1, 3, length, width), lambda m: (m, 0, 0, 0)),
-            pl.BlockSpec((1,) + bias.shape[1:], lambda m: (m, 0, 0, 0, 0)),
-            pl.BlockSpec((1, length, width), lambda m: (m, 0, 0)),
-            pl.BlockSpec((1, blocks, heads, BLOCK), lambda m: (m, 0, 0, 0)),
-            pl.BlockSpec((1, length, width), lambda m: (m, 0, 0)),
+        in_specs=[whole] * 5,
+        out_specs=whole,
+        out_shape=jax.ShapeDtypeStruct((micro, rows, 3 * width), bf16),
+        scratch_shapes=[
+            pltpu.VMEM((micro, 1, seq, rows, part), bf16),
+            pltpu.VMEM((micro, 1, length, part), bf16),
+            pltpu.VMEM((micro, 3, length, part), bf16),
+            pltpu.VMEM((micro, 3, seq, rows, part), bf16),
+            pltpu.VMEM((heads, length, part), bf16),
+            pltpu.VMEM((heads, length, part), bf16),
+            pltpu.VMEM((heads, length, part), bf16),
+            pltpu.VMEM((blocks, 8, BLOCK), f32),
+            pltpu.VMEM((length, part), f32),
+            sems,
+            sems,
+            sems,
+            sems,
         ],
-        out_specs=pl.BlockSpec((1, 3, length, width), lambda m: (m, 0, 0, 0)),
-        out_shape=jax.ShapeDtypeStruct((micro, 3, length, width), bf16),
-        scratch_shapes=[
-            pltpu.VMEM((heads, length, width), bf16),
-            pltpu.VMEM((heads, length, width), bf16),
-            pltpu.VMEM((heads, length, width), bf16),
-            pltpu.VMEM((blocks, 8, BLOCK), f32),
-            pltpu.VMEM((length, width), f32),
-        ],
-        compiler_params=pltpu.CompilerParams(vmem_limit_bytes=48 << 20),
+        compiler_params=pltpu.CompilerParams(
+            vmem_limit_bytes=50 << 20, collective_id=2, has_side_effects=True
+        ),
         name="self_backward",
-    )(qkv, bias, out, lse, gout)
+    )(grad_attended, qkv, bias, out, lse)
 
 
 def cross_forward_kernel(lengths_ref, q_ref, k_ref, v_ref, out_ref, lse_ref):
@@ -350,7 +534,7 @@
     )
     lane = lax.broadcasted_iota(jnp.int32, (8, width), 1)
     row = lax.broadcasted_iota(jnp.int32, (8, width), 0)
-    pick = jnp.where(lane // HD == row, 1.0, 0.0)
+    pick = jnp.where((lane >= row * HD) & (lane < (row + 1) * HD), 1.0, 0.0)
     q = q_ref[0].astype(f32) * scale_factor
     g = gout_ref[0].astype(f32)
     k = k_ref[0].astype(f32)
@@ -441,7 +625,6 @@
     micro, _, row_count, width = tokens.shape
     seq = lax.axis_size("seq")
     total_rows = micro * row_count
-    part = width // seq
     memory_rows = memory.shape[2]
 
     def gather(shard, axis=0):
@@ -465,20 +648,11 @@
     bias = jax.vmap(lambda t, p: tree_bias(t, p, BLOCK))(tile_segment[:, 0], parents[:, 0])
     lengths = memory_lengths[:, 0]
 
-    def to_heads(rows, parts):
-        blocks = rows.reshape(micro, row_count, parts, seq, part).transpose(0, 2, 3, 1, 4)
-        swapped = lax.all_to_all(blocks, "seq", split_axis=2, concat_axis=2, tiled=True)
-        return swapped.reshape(micro, parts, seq * row_count, part)
-
-    def to_rows(heads, parts):
-        blocks = heads.reshape(micro, parts, seq, row_count, part)
-        swapped = lax.all_to_all(blocks, "seq", split_axis=2, concat_axis=2, tiled=True)
-        return swapped.transpose(0, 3, 1, 2, 4).reshape(total_rows, parts * width)
-
     projected = dot_nn(x, joint_weight).astype(bf16)
-    qkv = to_heads(projected, 3)
-    attended_heads, self_lse = self_forward(qkv, bias)
-    attended = to_rows(attended_heads, 1)
+    qkv, attended_heads, self_lse, attended = self_forward(
+        projected.reshape(micro, row_count, 3 * width), bias, seq
+    )
+    attended = attended.reshape(total_rows, width)
 
     mixed_first = residual_weight * x32 + dot_nn(attended, self_output)
     hidden_first = layer_norm(mixed_first, gain_rows[0], bias_rows[0])
@@ -537,12 +711,12 @@
     branch_first = grad_first.astype(bf16)
     grad_self_output = dot_tn(attended, branch_first).astype(bf16)
     grad_attended = dot_nt(branch_first, self_output).astype(bf16)
-    gout = to_heads(grad_attended, 1)
     own_three = scatter(
         jnp.concatenate([grad_self_output, grad_cross_weight, grad_cross_output], 1)
     ).astype(f32)
-    grad_qkv = self_backward(qkv, bias, attended_heads, self_lse, gout[:, 0])
-    grad_projected = to_rows(grad_qkv, 3)
+    grad_projected = self_backward(
+        grad_attended.reshape(micro, row_count, width), qkv, bias, attended_heads, self_lse, seq
+    ).reshape(total_rows, 3 * width)
     grad_joint = dot_tn(x, grad_projected).astype(bf16)
     grad_tokens = (residual_weight * grad_first + dot_nt(grad_projected, joint_weight)).astype(bf16)
     grad_pairs_low = own_pairs.reshape(micro * memory_rows, 2 * width)

time: 1400 us -> 1350 us (0.964)
  Pallas kernels: 221 us -> 408 us
  waiting for transfers between devices: 741 us -> 619 us
  blocking collectives: 116 us -> 43.6 us
  local copies, waits for them, and re-layouts: 88.6 us -> 56.4 us
    all_to_all x3 -> x0, waiting for transfers between devices: 280 us -> none  [the longest x1 156 us: to_heads(): lax.all_to_all(blocks, 'seq', split_axis=2, concat_axis=2, tiled=True)]
    pallas_call x2, Pallas kernels: 178 us -> 366 us  [the longest x1 230 us: self_forward(): pl.pallas_call(functools.partial(self_forward_kernel, heads, BLOCK), in_s...]
    unnamed x13, waiting for transfers between devices: 151 us -> 252 us
    reduce_scatter x2, waiting for transfers between devices: 240 us -> 292 us  [scatter(): return lax.psum_scatter(full, ALL, scatter_dimension=axis, tiled=True)]
    all_to_all x1 -> x0, blocking collectives: 46.3 us -> none  [to_heads(): lax.all_to_all(blocks, 'seq', split_axis=2, concat_axis=2, tiled=True)]
    all_gather x1, blocking collectives: 69.4 us -> 43.6 us  [gather(): return lax.all_gather(shard, ALL, axis=axis, tiled=True)]
    all_gather x1, waiting for transfers between devices: 0.01 us -> 23.6 us  [per_device(): memory_full = lax.all_gather(memory[:, 0], 'seq', axis=1, tiled=True)]
    reshape x5 -> x0, local copies, waits for them, and re-layouts: 18.4 us -> none  [the longest x1 8.36 us: to_rows(): return swapped.transpose(0, 3, 1, 2, 4).reshape(total_rows, parts * width)]
  transfers between devices with their start and end apart: 13 -> 10, of which waited for: 6 -> 7; matrix products, arithmetic and copies ran while one was open for 15% -> 14% of each run, Pallas kernels for 14% -> 29%
where the time goes in v2:
time: 1350 us
  waiting for transfers between devices  619 us (46%)
  Pallas kernels  408 us (30%)
  matrix products  167 us (12%)
  local copies, waits for them, and re-layouts  56.4 us (4%)
  blocking collectives  43.6 us (3%)
  other arithmetic  37.8 us (3%)
  between operations  15.1 us (1%)
    reduce_scatter x2, waiting for transfers between devices, scatter(): return lax.psum_scatter(full, ALL, scatter_dimension=axis, tiled=True)  292 us
    unnamed x13, waiting for transfers between devices  252 us
    pallas_call x1, Pallas kernels, self_forward(): pl.pallas_call(functools.partial(self_forward_kernel, heads, BLOCK), in_s...  230 us
    pallas_call x1, Pallas kernels, self_backward(): pl.pallas_call(functools.partial(self_backward_kernel, heads, BLOCK), in_...  136 us
    dot_general x7, matrix products, dot_nt(): lax.dot_general(a, b, (((1,), (1,)), ((), ())), preferred_element_type=f32)  62.5 us
    dot_general x7, matrix products, dot_nn(): lax.dot_general(a, b, (((1,), (0,)), ((), ())), preferred_element_type=f32)  55.8 us
    all_gather x3, waiting for transfers between devices, gather(): return lax.all_gather(shard, ALL, axis=axis, tiled=True)  51.3 us
    unnamed x87, local copies, waits for them, and re-layouts  50.9 us
  transfers between devices with their start and end apart: 10, of which 7 were waited for; matrix products, arithmetic and copies ran while one was open for 14% of the time, Pallas kernels for 29%

profile of v2, /device:TPU:0, one launch (start us, length us, event | category | flops | bytes accessed | tf_op | source)
XLA Modules:
  0.0 1347.5 jit_solution(9779364874780474779)
XLA Ops:
  8.0 0.8 constant_dynamic-update-slice_fusion.4
  9.7 0.9 constant_dynamic-update-slice_fusion.2
  10.6 0.8 constant_dynamic-update-slice_fusion.1
  11.4 1.0 constant_dynamic-update-slice_fusion
  16.7 43.6 %all-gather.1 = bf16[32,32,6]{1,2,0:T(8,128)(2,1)S(1)} all-gather(bf16[1,32,6]{1,2,0:T(8,128)(2,1)S(1)} %maximum_bitcast_fusion), channel_id=1, replica_groups=mesh['seq'=8,'fsdp'=4] {'seq','fsdp'}, dimensions={0}, use_global_device_ids=true | all-gather | bytes 12672 | tf_op jit(solution)/shard_map/all_gather | solution.py:631
  62.5 1.3 copy.56
  64.7 18.8 %all-gather.7.cloned.1.call-done = bf16[1024,3072]{1,0:T(8,128)(2,1)} async-done(((bf16[32,3072]{1,0:T(8,128)(2,1)}), bf16[1024,3072]{1,0:T(8,128)(2,1)}) %all-gather.7.cloned.1.call-update) | async-done | bytes 6291472 | tf_op jit(solution)/shard_map/all_gather | solution.py:631
  83.5 9.2 convolution_convert_fusion.2
  92.6 229.5 %self_forward.1 = (bf16[3,3,2048,128]{3,2,1,0:T(8,128)(2,1)}, bf16[3,1,2048,128]{3,2,1,0:T(8,128)(2,1)S(1)}, f32[3,8,2,256]{3,2,1,0:T(2,128)S(1)}, bf16[3,256,1024]{2,1,0:T(8,128)(2,1)S(1)}) custom-call(bf16[3,256,3072]{2,1,0:T(8,128)(2,1)} %bitcast.120, f32[3,8,8,2,256]{4,3,2,1,0:T(2,128)S(1)} %reshape.172.bias_ref), custom_call_target="tpu_custom_call" | custom-call | tf_op jit(solution)/shard_map/self_forward/pallas_call | solution.py:313
  322.2 1.1 copy-done.4
  323.3 4.5 fusion.84
  328.3 1.2 copy-done.19
  329.5 4.6 fusion.51
  334.1 23.6 %all-gather.13.cloned.1.call-done = bf16[3,1,256,1024]{3,2,1,0:T(8,128)(2,1)} async-done(((bf16[3,1,32,1024]{3,2,1,0:T(8,128)(2,1)}), bf16[3,1,256,1024]{3,2,1,0:T(8,128)(2,1)}) %all-gather.13.cloned.1.call-update) | async-done | bytes 1572880 | tf_op jit(solution)/shard_map/all_gather | solution.py:637
  357.7 6.2 fusion.18
  363.9 21.5 %cross_forward.1 = (bf16[3,256,1024]{2,1,0:T(8,128)(2,1)S(1)}, f32[3,8,2,256]{3,2,1,0:T(2,128)S(1)}) custom-call(s32[3]{0:T(128)S(1)} %bitcast.112, bf16[3,256,1024]{2,1,0:T(8,128)(2,1)S(1)} %bitcast.106, bf16[3,256,2048]{2,1,0:T(8,128)(2,1)S(1)} %bitcast.102, bf16[3,256,2048]{2,1,0:T(8,128)(2,1)S(1)} %bitcast.103), custom_call_target="tpu_custom_call" | custom-call | tf_op jit(solution)/shard_map/cross_forward/pallas_call | solution.py:502
  385.5 4.2 fusion.85
  390.2 1.1 copy-done.16
  391.3 13.1 fusion.12
  404.4 32.5 %all-gather.11.cloned.1.call-done = bf16[4096,1024]{1,0:T(8,128)(2,1)} async-done(((bf16[128,1024]{1,0:T(8,128)(2,1)}), bf16[4096,1024]{1,0:T(8,128)(2,1)}) %all-gather.11.cloned.1.call-update) | async-done | bytes 8388624 | tf_op jit(solution)/shard_map/all_gather | solution.py:631
  436.9 14.0 %fusion.86 = (f32[768]{0:T(1024)S(1)}, f32[768,1024]{1,0:T(8,128)S(1)}) fusion(bf16[4096,1024]{1,0:T(8,128)(2,1)} %all-gather.11.cloned.1.call-done, f32[768,4096]{1,0:T(8,128)} %fusion.12, f32[1024]{0:T(1024)S(1)} %bitcast.150, f32[1024]{0:T(1024)S(1)} %bitcast.134, f32[768]{0:T(1024)S(1)} %add_rsqrt_fusion.1, f32[768,1024]{1,0:T(8,128)} %copy-done.16, ...), kind=kOutput, calls=%fused_computation.134 | convolution fusion | flops 6476266496 | bytes 27280384 | tf_op jit(solution)/shard_map/dot_general | solution.py:26
  451.5 0.9 copy-done.15
  452.4 1.1 fusion.27
  453.5 2.3 fusion.24
  455.8 20.2 %fusion.9 = bf16[768,4096]{1,0:T(8,128)(2,1)} fusion(f32[768,4096]{1,0:T(8,128)} %fusion.12, bf16[4096,1024]{1,0:T(8,128)(2,1)} %all-gather.11.cloned.1.call-done, f32[768,1024]{1,0:T(8,128)S(1)} %get-tuple-element.90), kind=kOutput, calls=%fused_computation.11 | convolution fusion | flops 6499860480 | bytes 30408704 | tf_op jit(solution)/shard_map/dot_general | solution.py:30
  476.1 12.2 multiply_reduce_fusion
  488.3 1.1 subtract_multiply_fusion.1
  489.4 4.6 fusion.54
  494.0 20.8 %cross_backward.1 = (bf16[3,256,1024]{2,1,0:T(8,128)(2,1)S(1)}, bf16[3,256,1024]{2,1,0:T(8,128)(2,1)S(1)}, bf16[3,256,1024]{2,1,0:T(8,128)(2,1)S(1)}) custom-call(s32[3]{0:T(128)S(1)} %bitcast.113, bf16[3,256,1024]{2,1,0:T(8,128)(2,1)S(1)} %bitcast.107, bf16[3,256,2048]{2,1,0:T(8,128)(2,1)S(1)} %bitcast.104, bf16[3,256,2048]{2,1,0:T(8,128)(2,1)S(1)} %bitcast.105, ...), custom_call_target="tpu_custom_call" | custom-call | tf_op jit(solution)/shard_map/cross_backward/pallas_call | solution.py:575
  514.8 1.1 copy-done.12
  516.0 2.0 pad_maximum_fusion.2
  518.1 1.3 copy-done.13
  519.4 6.8 multiply_reduce_fusion.1
  526.3 1.0 copy.70
  527.3 3.5 subtract_multiply_fusion
  531.6 3.2 convolution_convert_fusion.3
  534.9 3.2 convolution_convert_fusion.5
  538.1 3.3 convolution_convert_fusion.4
  541.5 6.0 pad_maximum_fusion.1
  547.5 8.7 copy.68
  556.3 1.8 copy-done.24
  558.1 13.8 %convolution_convert_fusion = bf16[4096,1024]{1,0:T(8,128)(2,1)} fusion(f32[768,1024]{1,0:T(8,128)S(1)} %copy-done.24, f32[768,4096]{1,0:T(8,128)} %fusion.12), kind=kOutput, calls=%fused_computation.14 | convolution fusion | flops 6475743232 | bytes 24117248 | tf_op jit(solution)/shard_map/dot_general | solution.py:34
  572.0 1.8 copy-done.18
  573.8 12.3 convolution_convert_fusion.1
  586.3 4.5 fusion.48
  590.8 136.2 %self_backward.1 = bf16[3,256,3072]{2,1,0:T(8,128)(2,1)} custom-call(bf16[3,256,1024]{2,1,0:T(8,128)(2,1)S(1)} %bitcast.108, bf16[3,3,2048,128]{3,2,1,0:T(8,128)(2,1)} %get-tuple-element.25.qkv_ref, f32[3,8,8,2,256]{4,3,2,1,0:T(2,128)S(1)} %copy-done.3, bf16[3,1,2048,128]{3,2,1,0:T(8,128)(2,1)S(1)} %copy-done.5, f32[3,8,2,256]{3,2,1,0:T(2,128)S(1)} %get-tuple-element.27.lse_ref), custom_call_target="tpu_custom_call" | custom-call | tf_op jit(solution)/shard_map/self_backward/pallas_call | solution.py:447
  727.1 9.5 convert_bitcast_fusion
  736.6 2.4 convert_bitcast_fusion.1
  739.5 15.3 %pad_maximum_fusion = bf16[1024,5120]{0,1:T(8,128)(2,1)} fusion(bf16[1024,2048]{0,1:T(8,128)(2,1)S(1)} %convert_bitcast_fusion.1, bf16[1024,3072]{0,1:T(8,128)(2,1)S(1)} %copy-done.22), kind=kLoop, calls=%fused_computation.13 | loop fusion | flops 20971520 | bytes 20971520 | tf_op jit(solution)/shard_map/concatenate | solution.py:726
  754.8 13.8 %copy.66 = bf16[1024,5120]{1,0:T(8,128)(2,1)} copy(bf16[1024,5120]{0,1:T(8,128)(2,1)} %pad_maximum_fusion) | data formatting | bytes 20971520
  768.6 1.9 copy-done.26
  770.5 9.8 add_convert_fusion
  780.3 0.9 fusion.83
  782.5 4.4 fusion.59
  786.9 100.5 %reduce-scatter.21.cloned.1.call-done = bf16[32,3072]{1,0:T(8,128)(2,1)} async-done(((bf16[1024,3072]{1,0:T(8,128)(2,1)}), bf16[32,3072]{1,0:T(8,128)(2,1)}) %reduce-scatter.21.cloned.1.call-update) | async-done | bytes 196624
  887.4 1.3 copy.69
  891.3 146.9 %reduce-scatter.17.cloned.1.call-done = bf16[128,1024]{1,0:T(8,128)(2,1)} async-done(((bf16[4096,1024]{1,0:T(8,128)(2,1)}), bf16[128,1024]{1,0:T(8,128)(2,1)}) %reduce-scatter.17.cloned.1.call-update) | async-done | bytes 262160 | tf_op jit(solution)/shard_map/reduce_scatter | solution.py:683
  1038.3 1.8 convert_element_type.149
  1040.0 145.2 %reduce-scatter.15.cloned.1.call-done = bf16[32,4096]{1,0:T(8,128)(2,1)} async-done(((bf16[1024,4096]{1,0:T(8,128)(2,1)}), bf16[32,4096]{1,0:T(8,128)(2,1)}) %reduce-scatter.15.cloned.1.call-update) | async-done | bytes 262160 | tf_op jit(solution)/shard_map/reduce_scatter | solution.py:683
  1185.3 1.8 convert_element_type.147
  1187.1 149.2 %reduce-scatter.19.cloned.1.call-done = bf16[32,5120]{1,0:T(8,128)(2,1)} async-done(((bf16[1024,5120]{1,0:T(8,128)(2,1)}), bf16[32,5120]{1,0:T(8,128)(2,1)}) %reduce-scatter.19.cloned.1.call-update) | async-done | bytes 327696
  1336.3 1.0 slice.97
  1337.6 1.0 copy.64
  1339.1 1.2 copy.61
  (125 shorter events, 16.7 us)
Async XLA Ops:
  7.2 53.2 %copy-start.14 = (bf16[3,1,256,1024]{3,2,1,0:T(8,128)(2,1)S(1)}, bf16[3,1,256,1024]{3,2,1,0:T(8,128)(2,1)}, u32[]{:S(2)}) copy-start(bf16[3,1,256,1024]{3,2,1,0:T(8,128)(2,1)} %param.17) | copy-start | bytes 4718596
  7.2 76.3 %all-gather.7.cloned.1.call-start = ((), (), s32[]{:S(2)}) async-start(), calls=%async_computation.6 | async-start | bytes 6488064 | tf_op jit(solution)/shard_map/all_gather | solution.py:631
  7.9 315.4 %all-gather.9.cloned.1.call-start = ((), (), s32[]{:S(2)}) async-start(), calls=%async_computation.7 | async-start | bytes 19464192 | tf_op jit(solution)/shard_map/all_gather | solution.py:631
  12.4 0.8 copy-start.32
  13.2 344.5 %all-gather.13.cloned.1.call-start = ((), (), s32[]{:S(2)}) async-start(), calls=%async_computation.12 | async-start | bytes 1769472 | tf_op jit(solution)/shard_map/all_gather | solution.py:637
  14.0 423.0 %all-gather.11.cloned.1.call-start = ((), (), s32[]{:S(2)}) async-start(), calls=%async_computation.8 | async-start | bytes 8650752 | tf_op jit(solution)/shard_map/all_gather | solution.py:631
  14.5 722.0 %reduce-scatter.13.cloned.1.call-start = ((), (), s32[]{:S(2)}) async-start(), calls=%async_computation.9 | async-start | bytes 3538944 | tf_op jit(solution)/shard_map/reduce_scatter | solution.py:704
  64.7 28.0 %copy-start.2 = (f32[3,8,8,2,256]{4,3,2,1,0:T(2,128)}, f32[3,8,8,2,256]{4,3,2,1,0:T(2,128)S(1)}, u32[]{:S(2)}) copy-start(f32[3,8,8,2,256]{4,3,2,1,0:T(2,128)S(1)} %reshape.172.bias_ref) | copy-start | bytes 1179652
  322.2 1.2 copy-start.4
  323.3 4.5 copy-start.10
  327.8 1.6 copy-start.19
  357.7 6.2 copy-start
  357.7 6.2 copy-start.9
  363.9 21.6 %copy-start.20 = (f32[768,1024]{1,0:T(8,128)S(1)}, f32[768,1024]{1,0:T(8,128)}, u32[]{:S(2)}) copy-start(f32[768,1024]{1,0:T(8,128)} %copy-done.19) | copy-start | bytes 9437188
  385.5 4.2 copy-start.6
  389.7 1.6 copy-start.16
  451.0 1.4 copy-start.15
  455.8 20.2 %copy-start.23 = (f32[768,1024]{1,0:T(8,128)}, f32[768,1024]{1,0:T(8,128)S(1)}, u32[]{:S(2)}) copy-start(f32[768,1024]{1,0:T(8,128)S(1)} %get-tuple-element.90) | copy-start | bytes 9437188
  455.8 20.2 %copy-start.17 = (f32[768,1024]{1,0:T(8,128)S(1)}, f32[768,1024]{1,0:T(8,128)}, u32[]{:S(2)}) copy-start(f32[768,1024]{1,0:T(8,128)} %copy-done.16) | copy-start | bytes 9437188
  489.4 4.6 copy-start.27
  489.4 4.6 copy-start.1
  489.4 4.6 copy-start.7
  514.8 1.1 copy-start.12
  518.0 1.4 copy-start.13
  518.0 262.3 %reduce-scatter.23.cloned.1.call-start = ((), (), s32[]{:S(2)}) async-start(), calls=%async_computation.15 | async-start | bytes 540672
  527.3 3.5 copy-start.8
  527.3 4.3 copy-start.28
  531.6 3.2 copy-start.25
  531.6 3.2 copy-start.11
  534.9 3.2 copy-start.21
  541.5 346.0 %reduce-scatter.21.cloned.1.call-start = ((), (), s32[]{:S(2)}) async-start(), calls=%async_computation.14 | async-start | bytes 6488064
  556.2 1.9 copy-start.24
  556.2 482.0 %reduce-scatter.17.cloned.1.call-start = ((), (), s32[]{:S(2)}) async-start(), calls=%async_computation.11 | async-start | bytes 8650752 | tf_op jit(solution)/shard_map/reduce_scatter | solution.py:683
  571.9 1.9 copy-start.18
  571.9 613.3 %reduce-scatter.15.cloned.1.call-start = ((), (), s32[]{:S(2)}) async-start(), calls=%async_computation.10 | async-start | bytes 8650752 | tf_op jit(solution)/shard_map/reduce_scatter | solution.py:683
  586.2 4.6 copy-start.3
  586.2 4.6 copy-start.5
  586.2 750.1 %reduce-scatter.19.cloned.1.call-start = ((), (), s32[]{:S(2)}) async-start(), calls=%async_computation.13 | async-start | bytes 10813440
  590.8 136.3 %copy-start.33 = (bf16[3,1,256,1024]{3,2,1,0:T(8,128)(2,1)S(1)}, bf16[3,1,256,1024]{3,2,1,0:T(8,128)(2,1)}, u32[]{:S(2)}) copy-start(bf16[3,1,256,1024]{3,2,1,0:T(8,128)(2,1)} %param.15) | copy-start | bytes 4718596
  727.1 9.5 copy-start.31
  736.6 2.9 copy-start.22
  768.6 1.9 copy-start.26
  770.5 12.0 copy-start.29
  1336.3 2.4 copy-start.30
Sparse Core Ops, SparseCore 0:
  10.9 72.5 all-gather.6
  87.0 225.0 all-gather.8
  314.2 43.4 all-gather.12
  360.4 76.4 all-gather.10
  518.1 73.4 reduce-scatter.12
  594.3 152.7 reduce-scatter.22
  753.7 133.6 reduce-scatter.20
  889.7 148.4 reduce-scatter.16
  1040.6 144.6 reduce-scatter.14
  1187.4 148.8 reduce-scatter.18

commit v3 on v2

--- a/solution.py
+++ b/solution.py
@@ -471,6 +471,220 @@
     )(grad_attended, qkv, bias, out, lse)
 
 
+def scatter_places():
+    s, f = lax.axis_index("seq"), lax.axis_index("fsdp")
+    z, y = s // 2, f // 2
+    return z, s - 2 * z, y, f - 2 * y, lax.axis_size("seq") // 2, lax.axis_size("fsdp") // 2
+
+
+def scatter_peers():
+    z, x, y, c, z_size, y_size = scatter_places()
+    peers = [{"fsdp": 2 * y + 1 - c}, {"seq": 2 * z + 1 - x}]
+    peers += [{"fsdp": 2 * lax.rem(y + k, y_size) + c} for k in range(1, y_size)]
+    peers += [{"seq": 2 * lax.rem(z + k, z_size) + x} for k in range(1, z_size)]
+    return peers
+
+
+def scatter_shapes(blocks, x_first):
+    z_size, _, y_size, _, rows, columns = blocks.shape
+    if x_first:
+        first, second = (1, y_size), (y_size - 1,)
+    else:
+        first, second = (y_size - 1, 2), (1,)
+    kind = blocks.dtype
+    return [
+        pltpu.VMEM((z_size, 2, y_size, rows, columns), kind),
+        pltpu.VMEM((z_size, 2, y_size, rows, columns), kind),
+        pltpu.VMEM((z_size,) + first + (rows, columns), kind),
+        pltpu.VMEM((z_size,) + second + (rows, columns), kind),
+        pltpu.VMEM((z_size - 1, rows, columns), kind),
+    ]
+
+
+def scatter_sems(count, z_size, y_size):
+    pair = pltpu.SemaphoreType.DMA((count, z_size))
+    triple = pltpu.SemaphoreType.DMA((count, z_size, max(1, y_size - 1)))
+    return [pair, pair, pair, triple, triple, triple, triple, pair, pair]
+
+
+def add_into(target, source):
+    target[...] = target[...] + source[...]
+
+
+def scatter_steps(kinds, sources, outs, buffers, sems):
+    z, x, y, c, z_size, y_size = scatter_places()
+    local, core_s, core_r, first_s, first_r, second_s, second_r, last_s, last_r = sems
+    count = len(sources)
+
+    def to_z(t):
+        return lax.rem(z + 1 + t, z_size)
+
+    def remote(source, target, send, receive, peer):
+        return pltpu.make_async_remote_copy(
+            src_ref=source,
+            dst_ref=target,
+            send_sem=send,
+            recv_sem=receive,
+            device_id=peer,
+            device_id_type=MESH,
+        )
+
+    def own_copy(a, t):
+        return pltpu.make_async_copy(
+            sources[a].at[to_z(t), :, :, c], buffers[a][0].at[t], local.at[a, t]
+        )
+
+    def core_copy(a, t):
+        return remote(
+            sources[a].at[to_z(t), :, :, 1 - c],
+            buffers[a][1].at[t],
+            core_s.at[a, t],
+            core_r.at[a, t],
+            {"fsdp": 2 * y + 1 - c},
+        )
+
+    def x_peer():
+        return {"seq": 2 * z + 1 - x}
+
+    def y_place(k):
+        return lax.rem(y + k, y_size)
+
+    def y_peer(k):
+        return {"fsdp": 2 * y_place(k) + c}
+
+    def first_copies(a, t):
+        own, _, first, _, _ = buffers[a]
+        if kinds[a]:
+            sends = [(own.at[t, 1 - x], x_peer())]
+        else:
+            sends = [(own.at[t, :, y_place(k)], y_peer(k)) for k in range(1, y_size)]
+        return [
+            remote(source, first.at[t, k], first_s.at[a, t, k], first_r.at[a, t, k], peer)
+            for k, (source, peer) in enumerate(sends)
+        ]
+
+    def second_copies(a, t):
+        own, _, _, second, _ = buffers[a]
+        if kinds[a]:
+            sends = [(own.at[t, x, y_place(k)], y_peer(k)) for k in range(1, y_size)]
+        else:
+            sends = [(own.at[t, 1 - x, y], x_peer())]
+        return [
+            remote(source, second.at[t, k], second_s.at[a, t, k], second_r.at[a, t, k], peer)
+            for k, (source, peer) in enumerate(sends)
+        ]
+
+    def last_copy(a, t):
+        own, _, _, _, last = buffers[a]
+        return remote(
+            own.at[t, x, y],
+            last.at[t],
+            last_s.at[a, t],
+            last_r.at[a, t],
+            {"seq": 2 * to_z(t) + x},
+        )
+
+    def start_core(t):
+        for a in range(count):
+            core_copy(a, t).start()
+            own_copy(a, t).start()
+
+    def core_step(t):
+        for a in range(count):
+            core_copy(a, t).wait_recv()
+            own_copy(a, t).wait()
+            own, core = buffers[a][:2]
+
+            def add(i, carry, own=own, core=core):
+                add_into(own.at[t, i // y_size, i % y_size], core.at[t, i // y_size, i % y_size])
+                return carry
+
+            lax.fori_loop(0, 2 * y_size, add, 0)
+            for copy in first_copies(a, t):
+                copy.start()
+        if t + 2 < z_size:
+            start_core(t + 2)
+
+    def first_step(t):
+        for a in range(count):
+            own, _, first, _, _ = buffers[a]
+            for k, copy in enumerate(first_copies(a, t)):
+                copy.wait_recv()
+                for i in range(y_size if kinds[a] else 2):
+                    target = own.at[t, x, i] if kinds[a] else own.at[t, i, y]
+                    add_into(target, first.at[t, k, i])
+            for copy in second_copies(a, t):
+                copy.start()
+
+    def second_step(t):
+        for a in range(count):
+            own, _, _, second, _ = buffers[a]
+            for k, copy in enumerate(second_copies(a, t)):
+                copy.wait_recv()
+                add_into(own.at[t, x, y], second.at[t, k])
+            if t < z_size - 1:
+                last_copy(a, t).start()
+
+    def final_step():
+        for a in range(count):
+            own, _, _, _, last = buffers[a]
+            total = own[z_size - 1, x, y].astype(f32)
+            for t in range(z_size - 1):
+                last_copy(a, t).wait()
+                total = total + last[t].astype(f32)
+            outs[a][...] = total
+            for t in range(z_size):
+                core_copy(a, t).wait_send()
+                for copy in first_copies(a, t) + second_copies(a, t):
+                    copy.wait_send()
+
+    def opening():
+        start_core(0)
+        if z_size > 1:
+            start_core(1)
+
+    steps = [opening]
+    for t in range(z_size + 2):
+        if t < z_size:
+            steps.append(functools.partial(core_step, t))
+        if 0 <= t - 1 < z_size:
+            steps.append(functools.partial(first_step, t - 1))
+        if 0 <= t - 2 < z_size:
+            steps.append(functools.partial(second_step, t - 2))
+    steps.append(final_step)
+    return steps
+
+
+def scatter_kernel(kinds, *refs):
+    count = len(kinds)
+    sources, outs, rest = refs[:count], refs[count : 2 * count], refs[2 * count :]
+    buffers = [rest[5 * a : 5 * a + 5] for a in range(count)]
+    greet(scatter_peers())
+    for step in scatter_steps(kinds, sources, outs, buffers, rest[5 * count :]):
+        step()
+
+
+def scatter_grads(arrays, kinds, z_size, y_size, collective_id):
+    blocks = [
+        a.reshape(z_size, 2, y_size, 2, a.shape[0] // (4 * z_size * y_size), a.shape[1])
+        for a in arrays
+    ]
+    scratch = []
+    for block, kind in zip(blocks, kinds):
+        scratch += scatter_shapes(block, kind)
+    return pl.pallas_call(
+        functools.partial(scatter_kernel, kinds),
+        in_specs=[pl.BlockSpec(memory_space=pl.ANY)] * len(arrays),
+        out_specs=[pl.BlockSpec(memory_space=pltpu.VMEM)] * len(arrays),
+        out_shape=[jax.ShapeDtypeStruct(b.shape[4:], f32) for b in blocks],
+        scratch_shapes=scratch + scatter_sems(len(arrays), z_size, y_size),
+        compiler_params=pltpu.CompilerParams(
+            vmem_limit_bytes=60 << 20, collective_id=collective_id, has_side_effects=True
+        ),
+        name="scatter_grads",
+    )(*blocks)
+
+
 def cross_forward_kernel(lengths_ref, q_ref, k_ref, v_ref, out_ref, lse_ref):
     count, width = k_ref.shape[1], k_ref.shape[2]
     rows = q_ref.shape[1]
@@ -679,12 +893,6 @@
     grad_inner = (gelu_parts(pre_active)[1] * dot_nt(branch_third, down_weight)).astype(bf16)
     grad_upward = dot_tn(hidden_second_low, grad_inner).astype(bf16)
 
-    def scatter(full, axis=0):
-        return lax.psum_scatter(full, ALL, scatter_dimension=axis, tiled=True)
-
-    own_down = scatter(grad_down).astype(f32)
-    own_upward = scatter(grad_upward).astype(f32)
-
     grad_hidden_second = residual_weight * grad_third + dot_nt(grad_inner, upward_weight)
     grad_second, gain_second, bias_second = layer_norm_back(
         mixed_second, gain_rows[1], grad_hidden_second
@@ -711,9 +919,6 @@
     branch_first = grad_first.astype(bf16)
     grad_self_output = dot_tn(attended, branch_first).astype(bf16)
     grad_attended = dot_nt(branch_first, self_output).astype(bf16)
-    own_three = scatter(
-        jnp.concatenate([grad_self_output, grad_cross_weight, grad_cross_output], 1)
-    ).astype(f32)
     grad_projected = self_backward(
         grad_attended.reshape(micro, row_count, width), qkv, bias, attended_heads, self_lse, seq
     ).reshape(total_rows, 3 * width)
@@ -722,26 +927,40 @@
     grad_pairs_low = own_pairs.reshape(micro * memory_rows, 2 * width)
     grad_pair_weight = dot_tn(memory.reshape(micro * memory_rows, width), grad_pairs_low)
     grad_memory = dot_nt(grad_pairs_low, pair_weight).astype(bf16)
-    own_last = scatter(
-        jnp.concatenate([grad_joint, grad_pair_weight.astype(bf16)], 1)
-    ).astype(f32)
     norm_grads = jnp.stack(
         [gain_first, gain_second, gain_third, bias_first, bias_second, bias_third]
     )
-    own_norms = scatter(norm_grads, 1)
+    devices = seq * lax.axis_size("fsdp")
+    norm_blocks = norm_grads.reshape(6, devices, width // devices).transpose(1, 0, 2)
+    owned = scatter_grads(
+        [
+            grad_joint,
+            grad_self_output,
+            grad_upward,
+            grad_pair_weight.astype(bf16),
+            grad_cross_weight,
+            grad_cross_output,
+            grad_down,
+            norm_blocks.reshape(6 * devices, width // devices),
+        ],
+        (True, True, True, False, False, False, False, False),
+        seq // 2,
+        lax.axis_size("fsdp") // 2,
+        3,
+    )
     return (
         output.reshape(tokens.shape),
         grad_tokens.reshape(tokens.shape),
         grad_memory.reshape(memory.shape),
-        own_last[:, : 3 * width],
-        own_three[:, :width],
-        own_three[:, width : 2 * width],
-        own_last[:, 3 * width :],
-        own_three[:, 2 * width :],
-        own_upward,
-        own_down,
-        own_norms[:3],
-        own_norms[3:],
+        owned[0],
+        owned[1],
+        owned[4],
+        owned[3],
+        owned[5],
+        owned[2],
+        owned[6],
+        owned[7][:3],
+        owned[7][3:],
     )
 
 

time: 1350 us -> 972 us (0.72)
  waiting for transfers between devices: 619 us -> 74.4 us
  Pallas kernels: 408 us -> 616 us
  local copies, waits for them, and re-layouts: 56.4 us -> 34.1 us
  other arithmetic: 37.8 us -> 19.2 us
    reduce_scatter x2 -> x0, waiting for transfers between devices: 292 us -> none  [scatter(): return lax.psum_scatter(full, ALL, scatter_dimension=axis, tiled=True)]
    unnamed x13 -> x5, waiting for transfers between devices: 252 us -> 1.92 us
    pallas_call x0 -> x1, Pallas kernels: none -> 176 us  [scatter_grads(): pl.pallas_call(functools.partial(scatter_kernel, kinds), in_specs=[pl.Blo...]
    unnamed x87 -> x145, local copies, waits for them, and re-layouts: 50.9 us -> 19.1 us
    pallas_call x1, Pallas kernels: 136 us -> 168 us  [self_backward(): pl.pallas_call(functools.partial(self_backward_kernel, heads, BLOCK), in_...]
    concatenate x2 -> x0, other arithmetic: 21.3 us -> none  [the longest x1 15.3 us: per_device(): jnp.concatenate([grad_joint, grad_pair_weight.astype(bf16)], 1)]
  transfers between devices with their start and end apart: 10 -> 5, of which waited for: 7 -> 3; matrix products, arithmetic and copies ran while one was open for 14% -> 11% of each run, Pallas kernels for 29% -> 43%
where the time goes in v3:
time: 972 us; the launch traced here: 969 us
  Pallas kernels  616 us (63%)
  matrix products  166 us (17%)
  waiting for transfers between devices  74.4 us (8%)
  blocking collectives  43.6 us (4%)
  local copies, waits for them, and re-layouts  34.1 us (4%)
  other arithmetic  19.2 us (2%)
  between operations  14.8 us (2%)
    pallas_call x1, Pallas kernels, self_forward(): pl.pallas_call(functools.partial(self_forward_kernel, heads, BLOCK), in_s...  229 us
    pallas_call x1, Pallas kernels, scatter_grads(): pl.pallas_call(functools.partial(scatter_kernel, kinds), in_specs=[pl.Blo...  176 us
    pallas_call x1, Pallas kernels, self_backward(): pl.pallas_call(functools.partial(self_backward_kernel, heads, BLOCK), in_...  168 us
    dot_general x7, matrix products, dot_nt(): lax.dot_general(a, b, (((1,), (1,)), ((), ())), preferred_element_type=f32)  61.7 us
    dot_general x7, matrix products, dot_nn(): lax.dot_general(a, b, (((1,), (0,)), ((), ())), preferred_element_type=f32)  56.3 us
    all_gather x3, waiting for transfers between devices, gather(): return lax.all_gather(shard, ALL, axis=axis, tiled=True)  48.5 us
    dot_general x7, matrix products, dot_tn(): lax.dot_general(a, b, (((0,), (0,)), ((), ())), preferred_element_type=f32)  47.3 us
    all_gather x1, blocking collectives, gather(): return lax.all_gather(shard, ALL, axis=axis, tiled=True)  43.6 us
  transfers between devices with their start and end apart: 5, of which 3 were waited for; matrix products, arithmetic and copies ran while one was open for 11% of the time, Pallas kernels for 43%

profile of v3, /device:TPU:0, one launch (start us, length us, event | category | flops | bytes accessed | tf_op | source)
XLA Modules:
  0.0 968.5 jit_solution(9818671976972335147)
XLA Ops:
  8.0 0.8 constant_dynamic-update-slice_fusion.4
  8.8 0.8 constant_dynamic-update-slice_fusion.3
  9.7 0.9 constant_dynamic-update-slice_fusion.2
  10.6 0.8 constant_dynamic-update-slice_fusion.1
  11.4 1.0 constant_dynamic-update-slice_fusion
  12.4 0.8 copy-done.34
  14.6 0.7 copy.52
  15.3 0.7 copy.51
  16.0 0.7 maximum_bitcast_fusion
  16.7 43.6 %all-gather.1 = bf16[32,32,6]{1,2,0:T(8,128)(2,1)S(1)} all-gather(bf16[1,32,6]{1,2,0:T(8,128)(2,1)S(1)} %maximum_bitcast_fusion), channel_id=1, replica_groups=mesh['seq'=8,'fsdp'=4] {'seq','fsdp'}, dimensions={0}, use_global_device_ids=true | all-gather | bytes 12672 | tf_op jit(solution)/shard_map/all_gather | solution.py:845
  61.0 0.8 convert_reduce_fusion
  62.4 0.7 stack.26
  64.3 1.3 copy.41
  66.5 16.8 %all-gather.7.cloned.1.call-done = bf16[1024,3072]{1,0:T(8,128)(2,1)} async-done(((bf16[32,3072]{1,0:T(8,128)(2,1)}), bf16[1024,3072]{1,0:T(8,128)(2,1)}) %all-gather.7.cloned.1.call-update) | async-done | bytes 6291472 | tf_op jit(solution)/shard_map/all_gather | solution.py:845
  83.3 9.7 %convolution_convert_fusion.3 = bf16[768,3072]{1,0:T(8,128)(2,1)} fusion(bf16[768,1024]{1,0:T(8,128)(2,1)S(1)} %bitcast.159, bf16[1024,3072]{1,0:T(8,128)(2,1)} %all-gather.7.cloned.1.call-done), kind=kOutput, calls=%fused_computation.20 | convolution fusion | flops 4834197504 | bytes 12582912 | tf_op jit(solution)/shard_map/dot_general | solution.py:26
  93.0 228.7 %self_forward.1 = (bf16[3,3,2048,128]{3,2,1,0:T(8,128)(2,1)}, bf16[3,1,2048,128]{3,2,1,0:T(8,128)(2,1)S(1)}, f32[3,8,2,256]{3,2,1,0:T(2,128)S(1)}, bf16[3,256,1024]{2,1,0:T(8,128)(2,1)S(1)}) custom-call(bf16[3,256,3072]{2,1,0:T(8,128)(2,1)} %bitcast.124, f32[3,8,8,2,256]{4,3,2,1,0:T(2,128)S(1)} %reshape.206.bias_ref), custom_call_target="tpu_custom_call" | custom-call | tf_op jit(solution)/shard_map/self_forward/pallas_call | solution.py:313
  321.7 1.1 copy-done.2
  323.4 4.5 fusion.83
  328.5 1.2 copy-done.23
  329.6 4.6 fusion.51
  334.3 24.0 %all-gather.13.cloned.1.call-done = bf16[3,1,256,1024]{3,2,1,0:T(8,128)(2,1)} async-done(((bf16[3,1,32,1024]{3,2,1,0:T(8,128)(2,1)}), bf16[3,1,256,1024]{3,2,1,0:T(8,128)(2,1)}) %all-gather.13.cloned.1.call-update) | async-done | bytes 1572880 | tf_op jit(solution)/shard_map/all_gather | solution.py:851
  358.3 6.2 fusion.18
  364.5 22.1 %cross_forward.1 = (bf16[3,256,1024]{2,1,0:T(8,128)(2,1)S(1)}, f32[3,8,2,256]{3,2,1,0:T(2,128)S(1)}) custom-call(s32[3]{0:T(128)S(1)} %bitcast.112, bf16[3,256,1024]{2,1,0:T(8,128)(2,1)S(1)} %bitcast.106, bf16[3,256,2048]{2,1,0:T(8,128)(2,1)S(1)} %bitcast.102, bf16[3,256,2048]{2,1,0:T(8,128)(2,1)S(1)} %bitcast.103), custom_call_target="tpu_custom_call" | custom-call | tf_op jit(solution)/shard_map/cross_forward/pallas_call | solution.py:716
  386.7 4.2 fusion.84
  391.4 1.1 copy-done.20
  392.5 12.9 %fusion.12 = f32[768,4096]{1,0:T(8,128)} fusion(bf16[1024,9216]{1,0:T(8,128)(2,1)} %all-gather.9.cloned.1.call-done, f32[768,1024]{1,0:T(8,128)S(1)} %get-tuple-element.119, f32[1024]{0:T(1024)S(1)} %bitcast.150, f32[1024]{0:T(1024)S(1)} %bitcast.138, f32[768]{0:T(1024)S(1)} %add_rsqrt_fusion.1, f32[768]{0:T(1024)S(1)} %broadcast_multiply_fusion.7), kind=kOutput, calls=%fused_computation.17 | convolution fusion | flops 6446383104 | bytes 24131584 | tf_op jit(solution)/shard_map/dot_general | solution.py:26
  405.5 31.7 %all-gather.11.cloned.1.call-done = bf16[4096,1024]{1,0:T(8,128)(2,1)} async-done(((bf16[128,1024]{1,0:T(8,128)(2,1)}), bf16[4096,1024]{1,0:T(8,128)(2,1)}) %all-gather.11.cloned.1.call-update) | async-done | bytes 8388624 | tf_op jit(solution)/shard_map/all_gather | solution.py:845
  437.2 14.2 %fusion.85 = (f32[768]{0:T(1024)S(1)}, f32[768,1024]{1,0:T(8,128)S(1)}) fusion(bf16[4096,1024]{1,0:T(8,128)(2,1)} %all-gather.11.cloned.1.call-done, f32[768,4096]{1,0:T(8,128)} %fusion.12, f32[1024]{0:T(1024)} %bitcast.149, f32[1024]{0:T(1024)S(1)} %bitcast.139, f32[768]{0:T(1024)} %copy-done.53, f32[768,1024]{1,0:T(8,128)} %copy-done.20, ...), kind=kOutput, calls=%fused_computation.131 | convolution fusion | flops 6476266496 | bytes 27280384 | tf_op jit(solution)/shard_map/dot_general | solution.py:26
  451.9 2.1 copy-done.19
  454.0 1.7 fusion.27
  456.2 1.4 stack.23
  457.6 4.7 fusion.24
  462.3 19.8 %fusion.9 = bf16[768,4096]{1,0:T(8,128)(2,1)} fusion(f32[768,4096]{1,0:T(8,128)} %fusion.12, bf16[4096,1024]{1,0:T(8,128)(2,1)} %all-gather.11.cloned.1.call-done, f32[768,1024]{1,0:T(8,128)S(1)} %get-tuple-element.106), kind=kOutput, calls=%fused_computation.11 | convolution fusion | flops 6499860480 | bytes 30408704 | tf_op jit(solution)/shard_map/dot_general | solution.py:30
  482.1 13.9 %multiply_reduce_fusion = (f32[1024]{0:T(1024)}, f32[768]{0:T(1024)}, f32[768]{0:T(1024)}, f32[1024]{0:T(1024)}, f32[768,1024]{1,0:T(8,128)}) fusion(f32[768,1024]{1,0:T(8,128)S(1)} %copy-done.21, f32[768]{0:T(1024)S(1)} %copy-done.54, f32[768]{0:T(1024)S(1)} %broadcast_multiply_fusion.7, f32[1024]{0:T(1024)S(1)} %bitcast.140, ...), kind=kOutput, calls=%fused_computation.39 | convolution fusion | flops 6451097600 | bytes 24141824 | tf_op jit(solution)/shard_map/dot_general | solution.py:30
  496.0 1.4 stack.22
  497.4 1.4 stack.25
  498.7 0.7 broadcast_multiply_fusion.3
  499.4 3.5 subtract_multiply_fusion.1
  502.9 3.2 convolution_convert_fusion.5
  506.1 3.5 fusion.54
  509.7 21.0 %cross_backward.1 = (bf16[3,256,1024]{2,1,0:T(8,128)(2,1)S(1)}, bf16[3,256,1024]{2,1,0:T(8,128)(2,1)S(1)}, bf16[3,256,1024]{2,1,0:T(8,128)(2,1)S(1)}) custom-call(s32[3]{0:T(128)S(1)} %bitcast.113, bf16[3,256,1024]{2,1,0:T(8,128)(2,1)S(1)} %bitcast.107, bf16[3,256,2048]{2,1,0:T(8,128)(2,1)S(1)} %bitcast.104, bf16[3,256,2048]{2,1,0:T(8,128)(2,1)S(1)} %bitcast.105, ...), custom_call_target="tpu_custom_call" | custom-call | tf_op jit(solution)/shard_map/cross_backward/pallas_call | solution.py:789
  530.8 3.4 convolution_convert_fusion.6
  534.3 6.5 multiply_reduce_fusion.1
  541.3 1.4 stack.21
  542.7 1.4 stack.24
  544.1 2.8 subtract_multiply_fusion
  546.9 3.2 convolution_convert_fusion.7
  550.3 2.0 pad_maximum_fusion
  552.3 1.9 copy-done.31
  554.2 3.5 fusion.48
  557.7 168.0 %self_backward.1 = bf16[3,256,3072]{2,1,0:T(8,128)(2,1)} custom-call(bf16[3,256,1024]{2,1,0:T(8,128)(2,1)S(1)} %bitcast.108, bf16[3,3,2048,128]{3,2,1,0:T(8,128)(2,1)} %get-tuple-element.33.qkv_ref, f32[3,8,8,2,256]{4,3,2,1,0:T(2,128)S(1)} %reshape.206.bias_ref, bf16[3,1,2048,128]{3,2,1,0:T(8,128)(2,1)S(1)} %copy-done.3, f32[3,8,2,256]{3,2,1,0:T(2,128)S(1)} %copy-done.11), custom_call_target="tpu_custom_call" | custom-call | tf_op jit(solution)/shard_map/self_backward/pallas_call | solution.py:447
  725.8 1.6 stack.27
  727.3 10.1 %add_convert_fusion = bf16[768,1024]{1,0:T(8,128)(2,1)} fusion(f32[768,1024]{1,0:T(8,128)S(1)} %copy-done.31, bf16[768,3072]{1,0:T(8,128)(2,1)} %bitcast.122, bf16[1024,3072]{1,0:T(8,128)(2,1)} %all-gather.7.cloned.1.call-done), kind=kOutput, calls=%fused_computation.41 | convolution fusion | flops 4834197504 | bytes 15728640 | tf_op jit(solution)/shard_map/dot_general | solution.py:30
  737.5 12.3 %convolution_convert_fusion.1 = bf16[1024,4096]{1,0:T(8,128)(2,1)} fusion(bf16[768,4096]{1,0:T(8,128)(2,1)} %fusion.9, f32[768,1024]{1,0:T(8,128)S(1)} %copy-done.22, f32[1024]{0:T(1024)S(1)} %bitcast.151, f32[1024]{0:T(1024)S(1)} %bitcast.142, f32[768]{0:T(1024)S(1)} %copy-done.55, f32[768]{0:T(1024)S(1)} %copy-done.44), kind=kOutput, calls=%fused_computation.14 | convolution fusion | flops 6450577408 | bytes 17840128 | tf_op jit(solution)/shard_map/dot_general | solution.py:34
  749.7 7.1 convolution_convert_fusion.2
  756.8 13.9 %convolution_convert_fusion = bf16[4096,1024]{1,0:T(8,128)(2,1)} fusion(f32[768,1024]{1,0:T(8,128)S(1)} %copy-done.29, f32[768,4096]{1,0:T(8,128)} %fusion.12), kind=kOutput, calls=%fused_computation.13 | convolution fusion | flops 6475743232 | bytes 24117248 | tf_op jit(solution)/shard_map/dot_general | solution.py:34
  770.7 4.3 convolution_convert_fusion.4
  775.0 175.9 %scatter_grads.1 = (f32[32,3072]{1,0:T(8,128)}, f32[32,1024]{1,0:T(8,128)}, f32[32,4096]{1,0:T(8,128)}, f32[32,2048]{1,0:T(8,128)}, f32[32,1024]{1,0:T(8,128)}, ...) custom-call(bf16[4,2,2,2,32,3072]{5,4,3,2,1,0:T(8,128)(2,1)} %bitcast.121, ...), custom_call_target="tpu_custom_call" | custom-call | tf_op jit(solution)/shard_map/scatter_grads/pallas_call | solution.py:675
  951.0 1.3 fusion.82
  952.4 4.4 fusion.59
  956.8 0.7 copy.64
  958.8 0.7 copy.67
  960.2 0.8 copy.69
  961.0 0.8 copy.70
  (168 shorter events, 11.3 us)
Async XLA Ops:
  7.2 53.8 %copy-start.18 = (bf16[3,1,256,1024]{3,2,1,0:T(8,128)(2,1)S(1)}, bf16[3,1,256,1024]{3,2,1,0:T(8,128)(2,1)}, u32[]{:S(2)}) copy-start(bf16[3,1,256,1024]{3,2,1,0:T(8,128)(2,1)} %param.17) | copy-start | bytes 4718596
  7.2 76.1 %all-gather.7.cloned.1.call-start = ((), (), s32[]{:S(2)}) async-start(), calls=%async_computation.1 | async-start | bytes 6488064 | tf_op jit(solution)/shard_map/all_gather | solution.py:845
  7.9 315.5 %all-gather.9.cloned.1.call-start = ((), (), s32[]{:S(2)}) async-start(), calls=%async_computation.2 | async-start | bytes 19464192 | tf_op jit(solution)/shard_map/all_gather | solution.py:845
  13.2 70.1 %copy-start.64 = (bf16[3,1,256,1024]{3,2,1,0:T(8,128)(2,1)S(1)}, bf16[3,1,256,1024]{3,2,1,0:T(8,128)(2,1)}, u32[]{:S(2)}) copy-start(bf16[3,1,256,1024]{3,2,1,0:T(8,128)(2,1)} %param.15) | copy-start | bytes 4718596
  13.2 345.0 %all-gather.13.cloned.1.call-start = ((), (), s32[]{:S(2)}) async-start(), calls=%async_computation.5 | async-start | bytes 1769472 | tf_op jit(solution)/shard_map/all_gather | solution.py:851
  14.0 423.2 %all-gather.11.cloned.1.call-start = ((), (), s32[]{:S(2)}) async-start(), calls=%async_computation.3 | async-start | bytes 8650752 | tf_op jit(solution)/shard_map/all_gather | solution.py:845
  14.6 756.2 %reduce-scatter.2.cloned.1.call-start = ((), (), s32[]{:S(2)}) async-start(), calls=%async_computation.4 | async-start | bytes 3538944 | tf_op jit(solution)/shard_map/reduce_scatter | solution.py:912
  61.0 267.5 %copy-start.61 = (f32[1,1024]{1,0:T(1,128)}, f32[1,1024]{1,0:T(1,128)S(1)}, u32[]{:S(2)}) copy-start(f32[1,1024]{1,0:T(1,128)S(1)} %get-tuple-element.112) | copy-start | bytes 12292
  61.0 325.6 %copy-start.51 = (f32[1,1024]{1,0:T(1,128)}, f32[1,1024]{1,0:T(1,128)S(1)}, u32[]{:S(2)}) copy-start(f32[1,1024]{1,0:T(1,128)S(1)} %get-tuple-element.113) | copy-start | bytes 12292
  323.4 4.5 copy-start.15
  328.0 1.7 copy-start.23
  328.0 58.7 %copy-start.45 = (f32[768]{0:T(1024)}, f32[768]{0:T(1024)S(1)}, u32[]{:S(2)}) copy-start(f32[768]{0:T(1024)S(1)} %broadcast_multiply_fusion.8) | copy-start | bytes 9220
  328.5 5.8 copy-start.56
  358.3 6.2 copy-start
  358.3 6.2 copy-start.14
  364.5 22.1 %copy-start.24 = (f32[768,1024]{1,0:T(8,128)S(1)}, f32[768,1024]{1,0:T(8,128)}, u32[]{:S(2)}) copy-start(f32[768,1024]{1,0:T(8,128)} %copy-done.23) | copy-start | bytes 9437188
  364.5 22.1 %copy-start.57 = (f32[768]{0:T(1024)S(1)}, f32[768]{0:T(1024)}, u32[]{:S(2)}) copy-start(f32[768]{0:T(1024)} %copy-done.56) | copy-start | bytes 9220
  364.5 22.1 %copy-start.62 = (f32[1,1024]{1,0:T(1,128)S(1)}, f32[1,1024]{1,0:T(1,128)}, u32[]{:S(2)}) copy-start(f32[1,1024]{1,0:T(1,128)} %copy-done.61) | copy-start | bytes 12292
  386.6 4.2 copy-start.8
  386.6 4.2 copy-start.12
  390.9 1.7 copy-start.20
  390.9 108.5 %copy-start.43 = (f32[768]{0:T(1024)}, f32[768]{0:T(1024)S(1)}, u32[]{:S(2)}) copy-start(f32[768]{0:T(1024)S(1)} %broadcast_multiply_fusion.7) | copy-start | bytes 9220
  451.4 4.2 copy-start.17
  451.4 2.5 copy-start.19
  462.3 19.8 %copy-start.28 = (f32[768,1024]{1,0:T(8,128)}, f32[768,1024]{1,0:T(8,128)S(1)}, u32[]{:S(2)}) copy-start(f32[768,1024]{1,0:T(8,128)S(1)} %get-tuple-element.106) | copy-start | bytes 9437188
  462.3 19.8 %copy-start.21 = (f32[768,1024]{1,0:T(8,128)S(1)}, f32[768,1024]{1,0:T(8,128)}, u32[]{:S(2)}) copy-start(f32[768,1024]{1,0:T(8,128)} %copy-done.20) | copy-start | bytes 9437188
  462.3 19.8 %copy-start.49 = (f32[1,1024]{1,0:T(1,128)S(1)}, f32[1,1024]{1,0:T(1,128)}, u32[]{:S(2)}) copy-start(f32[1,1024]{1,0:T(1,128)} %get-tuple-element.111) | copy-start | bytes 12292
  462.3 19.8 %copy-start.54 = (f32[768]{0:T(1024)S(1)}, f32[768]{0:T(1024)}, u32[]{:S(2)}) copy-start(f32[768]{0:T(1024)} %copy-done.53) | copy-start | bytes 9220
  499.4 3.5 copy-start.9
  506.1 3.5 copy-start.1
  506.1 3.6 copy-start.13
  509.7 21.1 %copy-start.25 = (f32[768,1024]{1,0:T(8,128)S(1)}, f32[768,1024]{1,0:T(8,128)}, u32[]{:S(2)}) copy-start(f32[768,1024]{1,0:T(8,128)} %copy-done.23) | copy-start | bytes 9437188
  509.7 21.1 %copy-start.46 = (f32[768]{0:T(1024)S(1)}, f32[768]{0:T(1024)}, u32[]{:S(2)}) copy-start(f32[768]{0:T(1024)} %copy-done.45) | copy-start | bytes 9220
  509.7 21.1 %copy-start.52 = (f32[1,1024]{1,0:T(1,128)S(1)}, f32[1,1024]{1,0:T(1,128)}, u32[]{:S(2)}) copy-start(f32[1,1024]{1,0:T(1,128)} %copy-done.51) | copy-start | bytes 12292
  509.7 21.1 %copy-start.58 = (f32[768]{0:T(1024)S(1)}, f32[768]{0:T(1024)}, u32[]{:S(2)}) copy-start(f32[768]{0:T(1024)} %copy-done.56) | copy-start | bytes 9220
  509.7 21.1 %copy-start.63 = (f32[1,1024]{1,0:T(1,128)S(1)}, f32[1,1024]{1,0:T(1,128)}, u32[]{:S(2)}) copy-start(f32[1,1024]{1,0:T(1,128)} %copy-done.61) | copy-start | bytes 12292
  530.7 3.5 copy-start.4
  530.8 3.5 copy-start.6
  534.3 9.8 %copy-start.26 = (f32[768,1024]{1,0:T(8,128)S(1)}, f32[768,1024]{1,0:T(8,128)}, u32[]{:S(2)}) copy-start(f32[768,1024]{1,0:T(8,128)} %copy-done.23) | copy-start | bytes 9437188
  544.0 2.8 copy-start.16
  546.8 3.2 copy-start.30
  546.8 3.2 copy-start.5
  546.9 3.5 copy-start.7
  552.3 1.9 copy-start.31
  554.2 3.5 copy-start.3
  554.2 3.6 copy-start.11
  557.7 168.0 %copy-start.42 = (f32[1,32,32]{2,0,1:T(1,128)S(1)}, f32[1,32,32]{2,0,1:T(1,128)}, u32[]{:S(2)}) copy-start(f32[1,32,32]{2,0,1:T(1,128)} %stack.26) | copy-start | bytes 12292
  727.3 10.1 %copy-start.22 = (f32[768,1024]{1,0:T(8,128)S(1)}, f32[768,1024]{1,0:T(8,128)}, u32[]{:S(2)}) copy-start(f32[768,1024]{1,0:T(8,128)} %copy-done.20) | copy-start | bytes 9437188
  727.3 10.1 %copy-start.44 = (f32[768]{0:T(1024)S(1)}, f32[768]{0:T(1024)}, u32[]{:S(2)}) copy-start(f32[768]{0:T(1024)} %copy-done.43) | copy-start | bytes 9220
  727.3 10.1 %copy-start.50 = (f32[1,1024]{1,0:T(1,128)S(1)}, f32[1,1024]{1,0:T(1,128)}, u32[]{:S(2)}) copy-start(f32[1,1024]{1,0:T(1,128)} %get-tuple-element.111) | copy-start | bytes 12292
  727.3 10.1 %copy-start.55 = (f32[768]{0:T(1024)S(1)}, f32[768]{0:T(1024)}, u32[]{:S(2)}) copy-start(f32[768]{0:T(1024)} %copy-done.53) | copy-start | bytes 9220
  727.3 10.1 %copy-start.60 = (f32[1,1024]{1,0:T(1,128)S(1)}, f32[1,1024]{1,0:T(1,128)}, u32[]{:S(2)}) copy-start(f32[1,1024]{1,0:T(1,128)} %get-tuple-element.110) | copy-start | bytes 12292
  737.5 12.3 %copy-start.27 = (bf16[3,256,3072]{2,1,0:T(8,128)(2,1)S(1)}, bf16[3,256,3072]{2,1,0:T(8,128)(2,1)}, u32[]{:S(2)}) copy-start(bf16[3,256,3072]{2,1,0:T(8,128)(2,1)} %self_backward.1) | copy-start | bytes 14155780
  737.5 12.3 %copy-start.65 = (bf16[3,1,256,1024]{3,2,1,0:T(8,128)(2,1)S(1)}, bf16[3,1,256,1024]{3,2,1,0:T(8,128)(2,1)}, u32[]{:S(2)}) copy-start(bf16[3,1,256,1024]{3,2,1,0:T(8,128)(2,1)} %param.15) | copy-start | bytes 4718596
  749.7 7.1 copy-start.29
  756.8 13.9 %copy-start.33 = (bf16[3,1,32,1024]{3,2,1,0:T(8,128)(2,1)S(1)}, bf16[3,1,32,1024]{3,2,1,0:T(8,128)(2,1)}, u32[]{:S(2)}) copy-start(bf16[3,1,32,1024]{3,2,1,0:T(8,128)(2,1)} %param.16) | copy-start | bytes 589828
  775.0 177.3 %copy-start.32 = (bf16[3,32,2048]{2,1,0:T(8,128)(2,1)S(1)}, bf16[3,32,2048]{2,1,0:T(8,128)(2,1)}, u32[]{:S(2)}) copy-start(bf16[3,32,2048]{2,1,0:T(8,128)(2,1)} %reduce-scatter.2.cloned.1.call-done) | copy-start | bytes 1179652
  951.0 5.8 copy-start.37
  952.3 5.2 copy-start.41
  952.3 5.9 copy-start.40
  952.3 6.5 copy-start.38
  952.3 7.2 copy-start.39
  952.3 7.9 copy-start.36
  952.4 8.6 copy-start.35
  (7 other events, 8.7 us)
Sparse Core Ops, SparseCore 0:
  10.9 72.3 all-gather.6
  86.8 222.6 all-gather.8
  311.7 46.5 all-gather.12
  361.0 76.1 all-gather.10
  552.4 150.5 reduce-scatter.1

commit v4 on v2

--- a/solution.py
+++ b/solution.py
@@ -11,6 +11,7 @@
 HD = 64
 TILE = 128
 BLOCK = 256
+SCATTER_END = 75
 
 scale_factor = 0.125
 residual_weight = 36.0**0.25
@@ -199,6 +200,224 @@
     for step in range(1, lax.axis_size("seq")):
         home_copy(source_ref, target_ref, send, receive, m, peer_at(step)).wait()
     home_self(source_ref, target_ref, send, m).wait()
+
+
+def scatter_places():
+    s, f = lax.axis_index("seq"), lax.axis_index("fsdp")
+    z, y = s // 2, f // 2
+    return z, s - 2 * z, y, f - 2 * y, lax.axis_size("seq") // 2, lax.axis_size("fsdp") // 2
+
+
+def scatter_peers():
+    z, x, y, c, z_size, y_size = scatter_places()
+    peers = [{"fsdp": 2 * y + 1 - c}, {"seq": 2 * z + 1 - x}]
+    peers += [{"fsdp": 2 * lax.rem(y + k, y_size) + c} for k in range(1, y_size)]
+    peers += [{"seq": 2 * lax.rem(z + k, z_size) + x} for k in range(1, z_size)]
+    return peers
+
+
+def scatter_shapes(blocks, x_first):
+    z_size, _, y_size, _, rows, columns = blocks.shape
+    if x_first:
+        first, second = (1, y_size), (y_size - 1,)
+    else:
+        first, second = (y_size - 1, 2), (1,)
+    kind = blocks.dtype
+    return [
+        pltpu.VMEM((z_size, 2, y_size, rows, columns), kind),
+        pltpu.VMEM((z_size, 2, y_size, rows, columns), kind),
+        pltpu.VMEM((z_size,) + first + (rows, columns), kind),
+        pltpu.VMEM((z_size,) + second + (rows, columns), kind),
+        pltpu.VMEM((z_size - 1, rows, columns), kind),
+    ]
+
+
+def scatter_sems(count, z_size, y_size):
+    pair = pltpu.SemaphoreType.DMA((count, z_size))
+    triple = pltpu.SemaphoreType.DMA((count, z_size, max(1, y_size - 1)))
+    return [pair, pair, pair, triple, triple, triple, triple, pair, pair]
+
+
+def add_into(target, source):
+    target[...] = target[...] + source[...]
+
+
+def scatter_steps(kinds, sources, outs, buffers, sems):
+    z, x, y, c, z_size, y_size = scatter_places()
+    local, core_s, core_r, first_s, first_r, second_s, second_r, last_s, last_r = sems
+    count = len(sources)
+
+    def to_z(t):
+        return lax.rem(z + 1 + t, z_size)
+
+    def remote(source, target, send, receive, peer):
+        return pltpu.make_async_remote_copy(
+            src_ref=source,
+            dst_ref=target,
+            send_sem=send,
+            recv_sem=receive,
+            device_id=peer,
+            device_id_type=MESH,
+        )
+
+    def own_copy(a, t):
+        return pltpu.make_async_copy(
+            sources[a].at[to_z(t), :, :, c], buffers[a][0].at[t], local.at[a, t]
+        )
+
+    def core_copy(a, t):
+        return remote(
+            sources[a].at[to_z(t), :, :, 1 - c],
+            buffers[a][1].at[t],
+            core_s.at[a, t],
+            core_r.at[a, t],
+            {"fsdp": 2 * y + 1 - c},
+        )
+
+    def x_peer():
+        return {"seq": 2 * z + 1 - x}
+
+    def y_place(k):
+        return lax.rem(y + k, y_size)
+
+    def y_peer(k):
+        return {"fsdp": 2 * y_place(k) + c}
+
+    def first_copies(a, t):
+        own, _, first, _, _ = buffers[a]
+        if kinds[a]:
+            sends = [(own.at[t, 1 - x], x_peer())]
+        else:
+            sends = [(own.at[t, :, y_place(k)], y_peer(k)) for k in range(1, y_size)]
+        return [
+            remote(source, first.at[t, k], first_s.at[a, t, k], first_r.at[a, t, k], peer)
+            for k, (source, peer) in enumerate(sends)
+        ]
+
+    def second_copies(a, t):
+        own, _, _, second, _ = buffers[a]
+        if kinds[a]:
+            sends = [(own.at[t, x, y_place(k)], y_peer(k)) for k in range(1, y_size)]
+        else:
+            sends = [(own.at[t, 1 - x, y], x_peer())]
+        return [
+            remote(source, second.at[t, k], second_s.at[a, t, k], second_r.at[a, t, k], peer)
+            for k, (source, peer) in enumerate(sends)
+        ]
+
+    def last_copy(a, t):
+        own, _, _, _, last = buffers[a]
+        return remote(
+            own.at[t, x, y],
+            last.at[t],
+            last_s.at[a, t],
+            last_r.at[a, t],
+            {"seq": 2 * to_z(t) + x},
+        )
+
+    def start_core(t):
+        for a in range(count):
+            core_copy(a, t).start()
+            own_copy(a, t).start()
+
+    def core_step(t):
+        for a in range(count):
+            core_copy(a, t).wait_recv()
+            own_copy(a, t).wait()
+            own, core = buffers[a][:2]
+
+            def add(i, carry, own=own, core=core):
+                add_into(own.at[t, i // y_size, i % y_size], core.at[t, i // y_size, i % y_size])
+                return carry
+
+            lax.fori_loop(0, 2 * y_size, add, 0)
+            for copy in first_copies(a, t):
+                copy.start()
+        if t + 2 < z_size:
+            start_core(t + 2)
+
+    def first_step(t):
+        for a in range(count):
+            own, _, first, _, _ = buffers[a]
+            for k, copy in enumerate(first_copies(a, t)):
+                copy.wait_recv()
+                for i in range(y_size if kinds[a] else 2):
+                    target = own.at[t, x, i] if kinds[a] else own.at[t, i, y]
+                    add_into(target, first.at[t, k, i])
+            for copy in second_copies(a, t):
+                copy.start()
+
+    def second_step(t):
+        for a in range(count):
+            own, _, _, second, _ = buffers[a]
+            for k, copy in enumerate(second_copies(a, t)):
+                copy.wait_recv()
+                add_into(own.at[t, x, y], second.at[t, k])
+            if t < z_size - 1:
+                last_copy(a, t).start()
+
+    def final_step():
+        for a in range(count):
+            own, _, _, _, last = buffers[a]
+            total = own[z_size - 1, x, y].astype(f32)
+            for t in range(z_size - 1):
+                last_copy(a, t).wait()
+                total = total + last[t].astype(f32)
+            outs[a][...] = total
+            for t in range(z_size):
+                core_copy(a, t).wait_send()
+                for copy in first_copies(a, t) + second_copies(a, t):
+                    copy.wait_send()
+
+    def opening():
+        start_core(0)
+        if z_size > 1:
+            start_core(1)
+
+    steps = [opening]
+    for t in range(z_size + 2):
+        if t < z_size:
+            steps.append(functools.partial(core_step, t))
+        if 0 <= t - 1 < z_size:
+            steps.append(functools.partial(first_step, t - 1))
+        if 0 <= t - 2 < z_size:
+            steps.append(functools.partial(second_step, t - 2))
+    steps.append(final_step)
+    return steps
+
+
+def scatter_kernel(kinds, *refs):
+    count = len(kinds)
+    sources, outs, rest = refs[:count], refs[count : 2 * count], refs[2 * count :]
+    buffers = [rest[5 * a : 5 * a + 5] for a in range(count)]
+    greet(scatter_peers())
+    for step in scatter_steps(kinds, sources, outs, buffers, rest[5 * count :]):
+        step()
+
+
+def scatter_blocks(arrays, z_size, y_size):
+    return [
+        a.reshape(z_size, 2, y_size, 2, a.shape[0] // (4 * z_size * y_size), a.shape[1])
+        for a in arrays
+    ]
+
+
+def scatter_grads(arrays, kinds, z_size, y_size, collective_id):
+    blocks = scatter_blocks(arrays, z_size, y_size)
+    scratch = []
+    for block, kind in zip(blocks, kinds):
+        scratch += scatter_shapes(block, kind)
+    return pl.pallas_call(
+        functools.partial(scatter_kernel, kinds),
+        in_specs=[pl.BlockSpec(memory_space=pl.ANY)] * len(arrays),
+        out_specs=[pl.BlockSpec(memory_space=pltpu.VMEM)] * len(arrays),
+        out_shape=[jax.ShapeDtypeStruct(b.shape[4:], f32) for b in blocks],
+        scratch_shapes=scratch + scatter_sems(len(arrays), z_size, y_size),
+        compiler_params=pltpu.CompilerParams(
+            vmem_limit_bytes=60 << 20, collective_id=collective_id, has_side_effects=True
+        ),
+        name="scatter_grads",
+    )(*blocks)
 
 
 def self_forward_kernel(
@@ -337,11 +556,31 @@
     )(projected, bias)
 
 
-def self_backward_kernel(
-    heads, block, rows_ref, qkv_ref, bias_ref, out_ref, lse_ref, grad_ref,
-    cut, gout, grads, back, queries, keys_h, gouts, delta, grad_q,
-    send_in, take_in, send_out, take_out,
-):
+def spread(steps, first, last):
+    return [(first + k * (last - first) // max(1, len(steps) - 1), s) for k, s in enumerate(steps)]
+
+
+def run_slot(placed, slot):
+    for at, step in placed:
+        pl.when(slot == at)(step)
+
+
+def both_peers():
+    _, _, y, c, _, y_size = scatter_places()
+    peers = [{"seq": peer_at(step)} for step in range(1, lax.axis_size("seq"))]
+    peers += [{"fsdp": 2 * y + 1 - c}]
+    return peers + [{"fsdp": 2 * lax.rem(y + k, y_size) + c} for k in range(1, y_size)]
+
+
+def self_backward_kernel(heads, block, kinds, *refs):
+    count = len(kinds)
+    rows_ref, qkv_ref, bias_ref, out_ref, lse_ref = refs[:5]
+    sources, refs = refs[5 : 5 + count], refs[5 + count :]
+    grad_ref, owned, refs = refs[0], refs[1 : 1 + count], refs[1 + count :]
+    cut, gout, grads, back, queries, keys_h, gouts, delta, grad_q = refs[:9]
+    send_in, take_in, send_out, take_out = refs[9:13]
+    buffers = [refs[13 + 5 * a : 18 + 5 * a] for a in range(count)]
+    scatter = scatter_steps(kinds, sources, owned, buffers, refs[13 + 5 * count :])
     micro, _, length, width = qkv_ref.shape
     seq = lax.axis_size("seq")
     blocks = length // block
@@ -351,7 +590,8 @@
     lane = lax.broadcasted_iota(jnp.int32, (8, width), 1)
     first_lane = lax.broadcasted_iota(jnp.int32, (8, width), 0) * HD
     pick = jnp.where((lane >= first_lane) & (lane < first_lane + HD), 1.0, 0.0)
-    greet([{"seq": peer_at(step)} for step in range(1, seq)])
+    placed = spread(scatter[1:-1], 1, SCATTER_END * micro * blocks // 100)
+    greet(both_peers())
 
     def launch(m, carry):
         cut_heads(rows_ref, m, 1, cut)
@@ -359,6 +599,7 @@
         return carry
 
     lax.fori_loop(0, micro, launch, 0)
+    scatter[0]()
     key_place = lax.broadcasted_iota(jnp.int32, (block, block), 0)
     query_place = lax.broadcasted_iota(jnp.int32, (block, block), 1)
     causal = key_place <= query_place
@@ -388,6 +629,7 @@
         lax.fori_loop(0, blocks, prepare, 0)
 
         def key_block(j, carry):
+            run_slot(placed, m * blocks + j)
             krows = rows_at(j, block)
 
             def pair(i, grad_k, grad_v, diagonal):
@@ -434,21 +676,28 @@
         join_heads(back, m, 3, grad_ref)
         return carry
 
+    scatter[-1]()
     lax.fori_loop(0, micro, finish, 0)
 
 
-def self_backward(grad_attended, qkv, bias, out, lse, seq):
+def self_backward(grad_attended, qkv, bias, out, lse, seq, arrays, kinds, y_size):
     micro, rows, width = grad_attended.shape
     length, part = qkv.shape[2:]
     heads = part // HD
     blocks = length // BLOCK
     whole = pl.BlockSpec(memory_space=pltpu.VMEM)
     sems = pltpu.SemaphoreType.DMA((micro, seq))
+    sources = scatter_blocks(arrays, seq // 2, y_size)
+    count = len(arrays)
+    scratch = []
+    for source, kind in zip(sources, kinds):
+        scratch += scatter_shapes(source, kind)
     return pl.pallas_call(
-        functools.partial(self_backward_kernel, heads, BLOCK),
-        in_specs=[whole] * 5,
-        out_specs=whole,
-        out_shape=jax.ShapeDtypeStruct((micro, rows, 3 * width), bf16),
+        functools.partial(self_backward_kernel, heads, BLOCK, kinds),
+        in_specs=[whole] * 5 + [pl.BlockSpec(memory_space=pl.ANY)] * count,
+        out_specs=[whole] * (1 + count),
+        out_shape=[jax.ShapeDtypeStruct((micro, rows, 3 * width), bf16)]
+        + [jax.ShapeDtypeStruct(b.shape[4:], f32) for b in sources],
         scratch_shapes=[
             pltpu.VMEM((micro, 1, seq, rows, part), bf16),
             pltpu.VMEM((micro, 1, length, part), bf16),
@@ -463,12 +712,14 @@
             sems,
             sems,
             sems,
-        ],
+        ]
+        + scratch
+        + scatter_sems(count, seq // 2, y_size),
         compiler_params=pltpu.CompilerParams(
-            vmem_limit_bytes=50 << 20, collective_id=2, has_side_effects=True
+            vmem_limit_bytes=60 << 20, collective_id=2, has_side_effects=True
         ),
         name="self_backward",
-    )(grad_attended, qkv, bias, out, lse)
+    )(grad_attended, qkv, bias, out, lse, *sources)
 
 
 def cross_forward_kernel(lengths_ref, q_ref, k_ref, v_ref, out_ref, lse_ref):
@@ -679,12 +930,6 @@
     grad_inner = (gelu_parts(pre_active)[1] * dot_nt(branch_third, down_weight)).astype(bf16)
     grad_upward = dot_tn(hidden_second_low, grad_inner).astype(bf16)
 
-    def scatter(full, axis=0):
-        return lax.psum_scatter(full, ALL, scatter_dimension=axis, tiled=True)
-
-    own_down = scatter(grad_down).astype(f32)
-    own_upward = scatter(grad_upward).astype(f32)
-
     grad_hidden_second = residual_weight * grad_third + dot_nt(grad_inner, upward_weight)
     grad_second, gain_second, bias_second = layer_norm_back(
         mixed_second, gain_rows[1], grad_hidden_second
@@ -711,37 +956,55 @@
     branch_first = grad_first.astype(bf16)
     grad_self_output = dot_tn(attended, branch_first).astype(bf16)
     grad_attended = dot_nt(branch_first, self_output).astype(bf16)
-    own_three = scatter(
-        jnp.concatenate([grad_self_output, grad_cross_weight, grad_cross_output], 1)
-    ).astype(f32)
-    grad_projected = self_backward(
-        grad_attended.reshape(micro, row_count, width), qkv, bias, attended_heads, self_lse, seq
-    ).reshape(total_rows, 3 * width)
+    grad_projected, own_upward, own_down = self_backward(
+        grad_attended.reshape(micro, row_count, width),
+        qkv,
+        bias,
+        attended_heads,
+        self_lse,
+        seq,
+        [grad_upward, grad_down],
+        (True, False),
+        lax.axis_size("fsdp") // 2,
+    )
+    grad_projected = grad_projected.reshape(total_rows, 3 * width)
     grad_joint = dot_tn(x, grad_projected).astype(bf16)
     grad_tokens = (residual_weight * grad_first + dot_nt(grad_projected, joint_weight)).astype(bf16)
     grad_pairs_low = own_pairs.reshape(micro * memory_rows, 2 * width)
     grad_pair_weight = dot_tn(memory.reshape(micro * memory_rows, width), grad_pairs_low)
     grad_memory = dot_nt(grad_pairs_low, pair_weight).astype(bf16)
-    own_last = scatter(
-        jnp.concatenate([grad_joint, grad_pair_weight.astype(bf16)], 1)
-    ).astype(f32)
     norm_grads = jnp.stack(
         [gain_first, gain_second, gain_third, bias_first, bias_second, bias_third]
     )
-    own_norms = scatter(norm_grads, 1)
+    devices = seq * lax.axis_size("fsdp")
+    norm_blocks = norm_grads.reshape(6, devices, width // devices).transpose(1, 0, 2)
+    owned = scatter_grads(
+        [
+            grad_joint,
+            grad_self_output,
+            grad_pair_weight.astype(bf16),
+            grad_cross_weight,
+            grad_cross_output,
+            norm_blocks.reshape(6 * devices, width // devices),
+        ],
+        (True, True, False, False, False, False),
+        seq // 2,
+        lax.axis_size("fsdp") // 2,
+        3,
+    )
     return (
         output.reshape(tokens.shape),
         grad_tokens.reshape(tokens.shape),
         grad_memory.reshape(memory.shape),
-        own_last[:, : 3 * width],
-        own_three[:, :width],
-        own_three[:, width : 2 * width],
-        own_last[:, 3 * width :],
-        own_three[:, 2 * width :],
+        owned[0],
+        owned[1],
+        owned[3],
+        owned[2],
+        owned[4],
         own_upward,
         own_down,
-        own_norms[:3],
-        own_norms[3:],
+        owned[5][:3],
+        owned[5][3:],
     )
 
 

time: 1350 us -> 936 us (0.69)
  waiting for transfers between devices: 619 us -> 75 us
  Pallas kernels: 408 us -> 589 us
  local copies, waits for them, and re-layouts: 56.4 us -> 27.2 us
  other arithmetic: 37.8 us -> 18.8 us
    reduce_scatter x2 -> x0, waiting for transfers between devices: 292 us -> none  [scatter(): return lax.psum_scatter(full, ALL, scatter_dimension=axis, tiled=True)]
    unnamed x13 -> x5, waiting for transfers between devices: 252 us -> 1.92 us
    pallas_call x1 -> x2, Pallas kernels: 136 us -> 317 us  [the longest x1 202 us: self_backward(): pl.pallas_call(functools.partial(self_backward_kernel, heads, BLOCK, kind...]
    unnamed x87 -> x107, local copies, waits for them, and re-layouts: 50.9 us -> 20.5 us
    concatenate x2 -> x0, other arithmetic: 21.3 us -> none  [the longest x1 15.3 us: per_device(): jnp.concatenate([grad_joint, grad_pair_weight.astype(bf16)], 1)]
  transfers between devices with their start and end apart: 10 -> 5, of which waited for: 7 -> 3; matrix products, arithmetic and copies ran while one was open for 14% -> 10% of each run, Pallas kernels for 29% -> 49%
where the time goes in v4:
time: 936 us; the launch traced here: 932 us
  Pallas kernels  589 us (63%)
  matrix products  164 us (18%)
  waiting for transfers between devices  75 us (8%)
  blocking collectives  43.6 us (5%)
  local copies, waits for them, and re-layouts  27.2 us (3%)
  other arithmetic  18.8 us (2%)
  between operations  14.7 us (2%)
    pallas_call x1, Pallas kernels, self_forward(): pl.pallas_call(functools.partial(self_forward_kernel, heads, BLOCK), in_s...  230 us
    pallas_call x1, Pallas kernels, self_backward(): pl.pallas_call(functools.partial(self_backward_kernel, heads, BLOCK, kind...  202 us
    pallas_call x1, Pallas kernels, scatter_grads(): pl.pallas_call(functools.partial(scatter_kernel, kinds), in_specs=[pl.Blo...  115 us
    dot_general x7, matrix products, dot_nt(): lax.dot_general(a, b, (((1,), (1,)), ((), ())), preferred_element_type=f32)  59.1 us
    dot_general x7, matrix products, dot_nn(): lax.dot_general(a, b, (((1,), (0,)), ((), ())), preferred_element_type=f32)  55.9 us
    all_gather x3, waiting for transfers between devices, gather(): return lax.all_gather(shard, ALL, axis=axis, tiled=True)  50.3 us
    dot_general x7, matrix products, dot_tn(): lax.dot_general(a, b, (((0,), (0,)), ((), ())), preferred_element_type=f32)  47.4 us
    all_gather x1, blocking collectives, gather(): return lax.all_gather(shard, ALL, axis=axis, tiled=True)  43.6 us
  transfers between devices with their start and end apart: 5, of which 3 were waited for; matrix products, arithmetic and copies ran while one was open for 10% of the time, Pallas kernels for 49%

profile of v4, /device:TPU:0, one launch (start us, length us, event | category | flops | bytes accessed | tf_op | source)
XLA Modules:
  0.0 931.8 jit_solution(13047686116970315811)
XLA Ops:
  7.2 0.7 all-gather.7.cloned.1.call-update
  8.0 0.8 constant_dynamic-update-slice_fusion.4
  8.8 0.8 constant_dynamic-update-slice_fusion.3
  9.7 0.9 constant_dynamic-update-slice_fusion.2
  10.6 0.8 constant_dynamic-update-slice_fusion.1
  11.4 1.0 constant_dynamic-update-slice_fusion
  12.4 0.8 copy-done.31
  13.3 0.7 all-gather.13.cloned.1.call-update
  14.6 0.7 copy.52
  15.3 0.7 copy.51
  16.0 0.7 maximum_bitcast_fusion
  16.7 43.6 %all-gather.1 = bf16[32,32,6]{1,2,0:T(8,128)(2,1)S(1)} all-gather(bf16[1,32,6]{1,2,0:T(8,128)(2,1)S(1)} %maximum_bitcast_fusion), channel_id=1, replica_groups=mesh['seq'=8,'fsdp'=4] {'seq','fsdp'}, dimensions={0}, use_global_device_ids=true | all-gather | bytes 12672 | tf_op jit(solution)/shard_map/all_gather | solution.py:882
  60.4 0.8 convert_reduce_fusion
  61.2 0.7 stack.26
  63.2 1.3 copy.41
  65.4 18.0 %all-gather.7.cloned.1.call-done = bf16[1024,3072]{1,0:T(8,128)(2,1)} async-done(((bf16[32,3072]{1,0:T(8,128)(2,1)}), bf16[1024,3072]{1,0:T(8,128)(2,1)}) %all-gather.7.cloned.1.call-update) | async-done | bytes 6291472 | tf_op jit(solution)/shard_map/all_gather | solution.py:882
  83.3 9.2 convolution_convert_fusion.3
  92.6 229.5 %self_forward.1 = (bf16[3,3,2048,128]{3,2,1,0:T(8,128)(2,1)}, bf16[3,1,2048,128]{3,2,1,0:T(8,128)(2,1)S(1)}, f32[3,8,2,256]{3,2,1,0:T(2,128)S(1)}, bf16[3,256,1024]{2,1,0:T(8,128)(2,1)S(1)}) custom-call(bf16[3,256,3072]{2,1,0:T(8,128)(2,1)} %bitcast.121, f32[3,8,8,2,256]{4,3,2,1,0:T(2,128)S(1)} %reshape.206.bias_ref.refs_2_), custom_call_target="tpu_custom_call" | custom-call | tf_op jit(solution)/shard_map/self_forward/pallas_call | solution.py:532
  322.1 1.1 copy-done.8
  323.8 4.5 fusion.83
  328.8 1.2 copy-done.18
  330.0 4.6 fusion.51
  334.7 22.8 %all-gather.13.cloned.1.call-done = bf16[3,1,256,1024]{3,2,1,0:T(8,128)(2,1)} async-done(((bf16[3,1,32,1024]{3,2,1,0:T(8,128)(2,1)}), bf16[3,1,256,1024]{3,2,1,0:T(8,128)(2,1)}) %all-gather.13.cloned.1.call-update) | async-done | bytes 1572880 | tf_op jit(solution)/shard_map/all_gather | solution.py:888
  357.4 6.2 fusion.18
  363.7 21.5 %cross_forward.1 = (bf16[3,256,1024]{2,1,0:T(8,128)(2,1)S(1)}, f32[3,8,2,256]{3,2,1,0:T(2,128)S(1)}) custom-call(s32[3]{0:T(128)S(1)} %bitcast.111, bf16[3,256,1024]{2,1,0:T(8,128)(2,1)S(1)} %bitcast.106, bf16[3,256,2048]{2,1,0:T(8,128)(2,1)S(1)} %bitcast.102, bf16[3,256,2048]{2,1,0:T(8,128)(2,1)S(1)} %bitcast.103), custom_call_target="tpu_custom_call" | custom-call | tf_op jit(solution)/shard_map/cross_forward/pallas_call | solution.py:753
  385.2 4.2 fusion.84
  389.9 1.2 copy-done.23
  391.2 13.1 %fusion.12 = f32[768,4096]{1,0:T(8,128)} fusion(bf16[1024,9216]{1,0:T(8,128)(2,1)} %all-gather.9.cloned.1.call-done, f32[768,1024]{1,0:T(8,128)S(1)} %get-tuple-element.121, f32[1024]{0:T(1024)S(1)} %bitcast.150, f32[1024]{0:T(1024)S(1)} %bitcast.141, f32[768]{0:T(1024)S(1)} %add_rsqrt_fusion.1, f32[768]{0:T(1024)S(1)} %broadcast_multiply_fusion.7), kind=kOutput, calls=%fused_computation.17 | convolution fusion | flops 6446383104 | bytes 24131584 | tf_op jit(solution)/shard_map/dot_general | solution.py:27
  404.3 32.4 %all-gather.11.cloned.1.call-done = bf16[4096,1024]{1,0:T(8,128)(2,1)} async-done(((bf16[128,1024]{1,0:T(8,128)(2,1)}), bf16[4096,1024]{1,0:T(8,128)(2,1)}) %all-gather.11.cloned.1.call-update) | async-done | bytes 8388624 | tf_op jit(solution)/shard_map/all_gather | solution.py:882
  436.7 14.0 %fusion.85 = (f32[768]{0:T(1024)S(1)}, f32[768,1024]{1,0:T(8,128)S(1)}) fusion(bf16[4096,1024]{1,0:T(8,128)(2,1)} %all-gather.11.cloned.1.call-done, f32[768,4096]{1,0:T(8,128)} %fusion.12, f32[1024]{0:T(1024)S(1)} %bitcast.151, f32[1024]{0:T(1024)S(1)} %bitcast.142, f32[768]{0:T(1024)S(1)} %add_rsqrt_fusion.1, f32[768,1024]{1,0:T(8,128)} %copy-done.23, ...), kind=kOutput, calls=%fused_computation.131 | convolution fusion | flops 6476266496 | bytes 27280384 | tf_op jit(solution)/shard_map/dot_general | solution.py:27
  451.2 2.1 copy-done.17
  453.2 1.1 fusion.27
  454.4 4.7 fusion.24
  459.1 14.0 %convolution_convert_fusion = bf16[4096,1024]{1,0:T(8,128)(2,1)} fusion(f32[768,1024]{1,0:T(8,128)S(1)} %get-tuple-element.108, f32[768,4096]{1,0:T(8,128)} %fusion.12), kind=kOutput, calls=%fused_computation.13 | convolution fusion | flops 6475743232 | bytes 24117248 | tf_op jit(solution)/shard_map/dot_general | solution.py:35
  473.2 18.6 %fusion.9 = bf16[768,4096]{1,0:T(8,128)(2,1)} fusion(f32[768,4096]{1,0:T(8,128)} %fusion.12, bf16[4096,1024]{1,0:T(8,128)(2,1)} %all-gather.11.cloned.1.call-done, f32[768,1024]{1,0:T(8,128)S(1)} %get-tuple-element.108), kind=kOutput, calls=%fused_computation.11 | convolution fusion | flops 6499860480 | bytes 30408704 | tf_op jit(solution)/shard_map/dot_general | solution.py:31
  491.8 13.3 %multiply_reduce_fusion = (f32[1024]{0:T(1024)S(1)}, f32[768]{0:T(1024)S(1)}, f32[768]{0:T(1024)S(1)}, f32[1024]{0:T(1024)S(1)}, f32[768,1024]{1,0:T(8,128)}) fusion(f32[768,1024]{1,0:T(8,128)S(1)} %copy-done.24, f32[768]{0:T(1024)S(1)} %add_rsqrt_fusion.1, f32[768]{0:T(1024)S(1)} %broadcast_multiply_fusion.7, f32[1024]{0:T(1024)S(1)} %bitcast.143, ...), kind=kOutput, calls=%fused_computation.39 | convolution fusion | flops 6451097600 | bytes 24141824 | tf_op jit(solution)/shard_map/dot_general | solution.py:31
  505.3 3.5 subtract_multiply_fusion.1
  508.8 4.6 fusion.54
  513.5 20.8 %cross_backward.1 = (bf16[3,256,1024]{2,1,0:T(8,128)(2,1)S(1)}, bf16[3,256,1024]{2,1,0:T(8,128)(2,1)S(1)}, bf16[3,256,1024]{2,1,0:T(8,128)(2,1)S(1)}) custom-call(s32[3]{0:T(128)S(1)} %bitcast.112, bf16[3,256,1024]{2,1,0:T(8,128)(2,1)S(1)} %bitcast.107, bf16[3,256,2048]{2,1,0:T(8,128)(2,1)S(1)} %bitcast.104, bf16[3,256,2048]{2,1,0:T(8,128)(2,1)S(1)} %bitcast.105, ...), custom_call_target="tpu_custom_call" | custom-call | tf_op jit(solution)/shard_map/cross_backward/pallas_call | solution.py:826
  534.3 7.3 multiply_reduce_fusion.1
  541.8 4.0 pad_maximum_fusion
  545.9 1.9 copy-done.21
  547.7 2.6 subtract_multiply_fusion
  550.3 1.6 copy-done.27
  551.9 4.7 fusion.48
  556.7 9.6 %convolution_convert_fusion.1 = bf16[1024,4096]{1,0:T(8,128)(2,1)} fusion(bf16[768,4096]{1,0:T(8,128)(2,1)S(1)} %bitcast.169, f32[768,1024]{1,0:T(8,128)S(1)} %copy-done.25, f32[1024]{0:T(1024)S(1)} %bitcast.152, f32[1024]{0:T(1024)S(1)} %bitcast.145, f32[768]{0:T(1024)S(1)} %add_rsqrt_fusion.1, f32[768]{0:T(1024)S(1)} %broadcast_multiply_fusion.7), kind=kOutput, calls=%fused_computation.14 | convolution fusion | flops 6450577408 | bytes 17840128 | tf_op jit(solution)/shard_map/dot_general | solution.py:35
  566.3 201.8 %self_backward.1 = (bf16[3,256,3072]{2,1,0:T(8,128)(2,1)}, f32[32,4096]{1,0:T(8,128)}, f32[128,1024]{1,0:T(8,128)}) custom-call(bf16[3,256,1024]{2,1,0:T(8,128)(2,1)} %bitcast.126, bf16[3,3,2048,128]{3,2,1,0:T(8,128)(2,1)} %get-tuple-element.34.refs_1_, f32[3,8,8,2,256]{4,3,2,1,0:T(2,128)} %copy-done.2, bf16[3,1,2048,128]{3,2,1,0:T(8,128)(2,1)} %copy-done.8, ...), custom_call_target="tpu_custom_call" | custom-call | tf_op jit(solution)/shard_map/self_backward/pallas_call | solution.py:695
  768.1 0.8 stack.27
  768.9 5.2 convolution_convert_fusion.5
  774.2 3.2 convolution_convert_fusion.7
  777.4 3.5 convolution_convert_fusion.6
  781.0 6.2 add_convert_fusion
  787.2 7.6 convolution_convert_fusion.2
  794.7 4.3 convolution_convert_fusion.4
  799.0 115.2 %scatter_grads.1 = (f32[32,3072]{1,0:T(8,128)}, f32[32,1024]{1,0:T(8,128)}, f32[32,2048]{1,0:T(8,128)}, f32[32,1024]{1,0:T(8,128)}, f32[32,1024]{1,0:T(8,128)}, /*index=5*/f32[6,32]{1,0:T(8,128)}) custom-call(bf16[4,2,2,2,32,3072]{5,4,3,2,1,0:T(8,128)(2,1)} %bitcast.120, bf16[4,2,2,2,32,1024]{5,4,3,2,1,0:T(8,128)(2,1)} %bitcast.123, ...), custom_call_target="tpu_custom_call" | custom-call | tf_op jit(solution)/shard_map/scatter_grads/pallas_call | solution.py:410
  914.2 1.3 fusion.82
  915.6 4.4 fusion.59
  920.0 0.7 copy.64
  920.7 0.7 copy.65
  921.4 0.7 copy.66
  922.0 0.7 copy.67
  922.8 0.7 copy.68
  923.4 0.8 copy.69
  924.2 0.8 copy.70
  (133 shorter events, 5.7 us)
Async XLA Ops:
  7.2 53.2 %copy-start.16 = (bf16[3,1,256,1024]{3,2,1,0:T(8,128)(2,1)S(1)}, bf16[3,1,256,1024]{3,2,1,0:T(8,128)(2,1)}, u32[]{:S(2)}) copy-start(bf16[3,1,256,1024]{3,2,1,0:T(8,128)(2,1)} %param.17) | copy-start | bytes 4718596
  7.2 76.1 %all-gather.7.cloned.1.call-start = ((), (), s32[]{:S(2)}) async-start(), calls=%async_computation.1 | async-start | bytes 6488064 | tf_op jit(solution)/shard_map/all_gather | solution.py:882
  7.9 315.9 %all-gather.9.cloned.1.call-start = ((), (), s32[]{:S(2)}) async-start(), calls=%async_computation.2 | async-start | bytes 19464192 | tf_op jit(solution)/shard_map/all_gather | solution.py:882
  12.4 0.8 copy-start.31
  13.2 344.2 %all-gather.13.cloned.1.call-start = ((), (), s32[]{:S(2)}) async-start(), calls=%async_computation.5 | async-start | bytes 1769472 | tf_op jit(solution)/shard_map/all_gather | solution.py:888
  14.0 422.7 %all-gather.11.cloned.1.call-start = ((), (), s32[]{:S(2)}) async-start(), calls=%async_computation.3 | async-start | bytes 8650752 | tf_op jit(solution)/shard_map/all_gather | solution.py:882
  14.5 780.2 %reduce-scatter.2.cloned.1.call-start = ((), (), s32[]{:S(2)}) async-start(), calls=%async_computation.4 | async-start | bytes 3538944 | tf_op jit(solution)/shard_map/reduce_scatter | solution.py:949
  65.4 27.2 %copy-start.2 = (f32[3,8,8,2,256]{4,3,2,1,0:T(2,128)}, f32[3,8,8,2,256]{4,3,2,1,0:T(2,128)S(1)}, u32[]{:S(2)}) copy-start(f32[3,8,8,2,256]{4,3,2,1,0:T(2,128)S(1)} %reshape.206.bias_ref.refs_2_) | copy-start | bytes 1179652
  322.1 1.1 copy-start.8
  323.2 0.6 copy-start.9
  323.8 4.5 copy-start.11
  328.3 1.7 copy-start.18
  357.4 6.2 copy-start
  357.4 6.2 copy-start.10
  363.6 21.6 %copy-start.19 = (f32[768,1024]{1,0:T(8,128)S(1)}, f32[768,1024]{1,0:T(8,128)}, u32[]{:S(2)}) copy-start(f32[768,1024]{1,0:T(8,128)} %copy-done.18) | copy-start | bytes 9437188
  385.2 4.2 copy-start.5
  389.5 1.7 copy-start.23
  450.7 3.7 copy-start.15
  450.7 2.5 copy-start.17
  473.2 18.6 %copy-start.24 = (f32[768,1024]{1,0:T(8,128)S(1)}, f32[768,1024]{1,0:T(8,128)}, u32[]{:S(2)}) copy-start(f32[768,1024]{1,0:T(8,128)} %copy-done.23) | copy-start | bytes 9437188
  508.8 25.5 %copy-start.26 = (f32[768,1024]{1,0:T(8,128)}, f32[768,1024]{1,0:T(8,128)S(1)}, u32[]{:S(2)}) copy-start(f32[768,1024]{1,0:T(8,128)S(1)} %subtract_multiply_fusion.1) | copy-start | bytes 9437188
  508.8 4.6 copy-start.1
  508.8 4.6 copy-start.6
  513.4 20.8 %copy-start.20 = (f32[768,1024]{1,0:T(8,128)S(1)}, f32[768,1024]{1,0:T(8,128)}, u32[]{:S(2)}) copy-start(f32[768,1024]{1,0:T(8,128)} %copy-done.18) | copy-start | bytes 9437188
  534.2 7.4 copy-start.3
  534.3 7.4 copy-start.4
  534.3 7.3 copy-start.13
  545.8 1.9 copy-start.21
  547.7 8.9 slice-start.4
  550.3 1.6 copy-start.27
  551.9 4.8 copy-start.25
  551.9 4.8 slice-start.5
  566.3 201.8 %copy-start.39 = (f32[1,32,32]{2,0,1:T(1,128)S(1)}, f32[1,32,32]{2,0,1:T(1,128)}, u32[]{:S(2)}) copy-start(f32[1,32,32]{2,0,1:T(1,128)} %stack.26) | copy-start | bytes 12292
  566.3 202.7 %copy-start.7 = (bf16[3,256,1024]{2,1,0:T(8,128)(2,1)S(1)}, bf16[3,256,1024]{2,1,0:T(8,128)(2,1)}, u32[]{:S(2)}) copy-start(bf16[3,256,1024]{2,1,0:T(8,128)(2,1)} %copy-done.5) | copy-start | bytes 4718596
  768.9 5.2 copy-start.12
  768.9 5.2 copy-start.28
  774.1 3.3 copy-start.14
  774.1 3.3 copy-start.22
  774.1 6.8 slice-start
  774.2 6.8 slice-start.2
  777.4 3.6 slice-start.1
  777.4 3.6 slice-start.3
  781.0 6.2 copy-start.40
  787.2 7.6 copy-start.30
  799.0 116.5 %copy-start.29 = (bf16[3,32,2048]{2,1,0:T(8,128)(2,1)S(1)}, bf16[3,32,2048]{2,1,0:T(8,128)(2,1)}, u32[]{:S(2)}) copy-start(bf16[3,32,2048]{2,1,0:T(8,128)(2,1)} %reduce-scatter.2.cloned.1.call-done) | copy-start | bytes 1179652
  914.2 5.8 copy-start.34
  915.5 5.2 copy-start.38
  915.5 5.9 copy-start.37
  915.5 6.5 copy-start.35
  915.5 7.2 copy-start.36
  915.6 7.9 copy-start.33
  915.6 8.6 copy-start.32
Sparse Core Ops, SparseCore 0:
  10.9 72.3 all-gather.6
  86.8 224.8 all-gather.8
  313.9 43.4 all-gather.12
  360.1 76.4 all-gather.10
  546.0 134.8 reduce-scatter.1

commit v5 on v4

--- a/solution.py
+++ b/solution.py
@@ -11,6 +11,9 @@
 HD = 64
 TILE = 128
 BLOCK = 256
+WINDOW = 4
+GATHER_END = 75
+SPLIT_ELEMENTS = 96 << 10
 SCATTER_END = 75
 
 scale_factor = 0.125
@@ -155,9 +158,11 @@
     to_self(source_ref, target_ref, send, m).start()
 
 
-def take_blocks(source_ref, target_ref, send, receive, m):
+def take_blocks(source_ref, target_ref, send, receive, m, between=None):
     for step in range(1, lax.axis_size("seq")):
         to_peer(source_ref, target_ref, send, receive, m, step).wait_recv()
+        if between is not None:
+            between(step)
     to_self(source_ref, target_ref, send, m).wait()
 
 
@@ -420,38 +425,236 @@
     )(*blocks)
 
 
-def self_forward_kernel(
-    heads, block, rows_ref, bias_ref, qkv_ref, out_ref, lse_ref, attended_ref,
-    cut, back, queries, values_t, send_in, take_in, send_out, take_out,
-):
+def spread(steps, first, last):
+    return [(first + k * (last - first) // max(1, len(steps) - 1), s) for k, s in enumerate(steps)]
+
+
+def run_slot(placed, slot):
+    for at, step in placed:
+        pl.when(slot == at)(step)
+
+
+def both_peers():
+    _, _, y, c, _, y_size = scatter_places()
+    peers = [{"seq": peer_at(step)} for step in range(1, lax.axis_size("seq"))]
+    peers += [{"fsdp": 2 * y + 1 - c}]
+    return peers + [{"fsdp": 2 * lax.rem(y + k, y_size) + c} for k in range(1, y_size)]
+
+
+def gather_parts(shards, kinds, groups):
+    parts, units = [], []
+    for group in groups:
+        pieces = []
+        for a in group:
+            rows, columns = shards[a].shape
+            kind = kinds[a]
+            split = 2 if rows % 32 == 0 and rows * columns >= SPLIT_ELEMENTS else 1
+            for n in range(split):
+                cut = (n * columns // split, columns // split)
+                if kind == "seq" or rows % 32:
+                    piece = [(a, 0, rows) + cut + ("x" if kind == "all" else kind,)]
+                else:
+                    half = rows // 2
+                    piece = [(a, 0, half) + cut + ("x",), (a, half, half) + cut + ("y",)]
+                if n == len(pieces):
+                    pieces.append([])
+                pieces[n] += piece
+        for piece in pieces:
+            units.append(range(len(parts), len(parts) + len(piece)))
+            parts += piece
+    return parts, units
+
+
+def gather_sems(plan, z_size, y_size):
+    count = len(plan[0])
+    z_sem = pltpu.SemaphoreType.DMA((count, z_size))
+    y_sem = pltpu.SemaphoreType.DMA((count, max(1, y_size - 1)))
+    one = pltpu.SemaphoreType.DMA((count, 1))
+    return [z_sem, z_sem, y_sem, y_sem, y_sem, y_sem, one, one]
+
+
+def gather_steps(plan, shards, outs, sems):
+    z, x, y, c, z_size, y_size = scatter_places()
+    z_s, z_r, first_s, first_r, second_s, second_r, core_s, core_r = sems
+    parts, units = plan
+
+    def remote(view, peer, send, receive):
+        return pltpu.make_async_remote_copy(
+            src_ref=view,
+            dst_ref=view,
+            send_sem=send,
+            recv_sem=receive,
+            device_id=peer,
+            device_id_type=MESH,
+        )
+
+    def shard_of(p):
+        a, start, rows, left, columns, _ = parts[p]
+        return shards[a].at[pl.ds(start, rows), pl.ds(left, columns)]
+
+    def place(p, *lead):
+        a, start, rows, left, columns, _ = parts[p]
+        return outs[a].at[lead + (pl.ds(start, rows), pl.ds(left, columns))]
+
+    def own(p):
+        return place(p, z, x) if parts[p][-1] == "seq" else place(p, z, x, y, c)
+
+    def own_copy(p):
+        return pltpu.make_async_copy(shard_of(p), own(p), z_s.at[p, 0])
+
+    def z_copies(p):
+        return [
+            pltpu.make_async_remote_copy(
+                src_ref=shard_of(p),
+                dst_ref=own(p),
+                send_sem=z_s.at[p, k],
+                recv_sem=z_r.at[p, k],
+                device_id={"seq": 2 * lax.rem(z + k, z_size) + x},
+                device_id_type=MESH,
+            )
+            for k in range(1, z_size)
+        ]
+
+    def x_peer():
+        return {"seq": 2 * z + 1 - x}
+
+    def y_peers():
+        return [{"fsdp": 2 * lax.rem(y + k, y_size) + c} for k in range(1, y_size)]
+
+    whole = slice(None)
+
+    def first_copies(p):
+        kind = parts[p][-1]
+        view = place(p, whole, x) if kind == "seq" else place(p, whole, x, y, c)
+        peers = y_peers() if kind == "y" else [x_peer()]
+        return [
+            remote(view, peer, first_s.at[p, k], first_r.at[p, k]) for k, peer in enumerate(peers)
+        ]
+
+    def second_copies(p):
+        kind = parts[p][-1]
+        if kind == "seq":
+            return []
+        view = place(p, whole, whole, y, c) if kind == "x" else place(p, whole, x, whole, c)
+        peers = y_peers() if kind == "x" else [x_peer()]
+        return [
+            remote(view, peer, second_s.at[p, k], second_r.at[p, k]) for k, peer in enumerate(peers)
+        ]
+
+    def core_copies(p):
+        if parts[p][-1] == "seq":
+            return []
+        view = place(p, whole, whole, whole, c)
+        return [remote(view, {"fsdp": 2 * y + 1 - c}, core_s.at[p, 0], core_r.at[p, 0])]
+
+    def step(t):
+        def unit(at):
+            return units[at] if 0 <= at < len(units) else ()
+
+        for p in unit(t - 3):
+            for copy in second_copies(p):
+                copy.wait_recv()
+            for copy in core_copies(p):
+                copy.start()
+        for p in unit(t - 2):
+            for copy in first_copies(p):
+                copy.wait_recv()
+            for copy in second_copies(p):
+                copy.start()
+        for p in unit(t - 1):
+            for copy in z_copies(p):
+                copy.wait_recv()
+            own_copy(p).wait()
+            for copy in first_copies(p):
+                copy.start()
+        for p in unit(t):
+            for copy in z_copies(p):
+                copy.start()
+            own_copy(p).start()
+
+    def final_step():
+        for p in range(len(parts)):
+            for copy in core_copies(p):
+                copy.wait()
+            for copy in z_copies(p) + first_copies(p) + second_copies(p):
+                copy.wait_send()
+
+    return [functools.partial(step, t) for t in range(len(units) + 3)] + [final_step]
+
+
+def gather_out(shard, kind, z_size, y_size):
+    lead = (z_size, 2) if kind == "seq" else (z_size, 2, y_size, 2)
+    return jax.ShapeDtypeStruct(lead + shard.shape, shard.dtype)
+
+
+def gather_kernel(plan, count, *refs):
+    shards, outs, sems = refs[:count], refs[count : 2 * count], refs[2 * count :]
+    greet(scatter_peers())
+    for step in gather_steps(plan, shards, outs, sems):
+        step()
+
+
+def gather_first(shards, kinds, groups, z_size, y_size, collective_id):
+    plan = gather_parts(shards, kinds, groups)
+    return pl.pallas_call(
+        functools.partial(gather_kernel, plan, len(shards)),
+        in_specs=[pl.BlockSpec(memory_space=pl.ANY)] * len(shards),
+        out_specs=[pl.BlockSpec(memory_space=pl.ANY)] * len(shards),
+        out_shape=[gather_out(s, k, z_size, y_size) for s, k in zip(shards, kinds)],
+        scratch_shapes=gather_sems(plan, z_size, y_size),
+        compiler_params=pltpu.CompilerParams(collective_id=collective_id, has_side_effects=True),
+        name="gather_first",
+    )(*shards)
+
+
+def self_forward_kernel(heads, block, plan, count, *refs):
+    rows_ref, bias_ref = refs[:2]
+    shards, refs = refs[2 : 2 + count], refs[2 + count :]
+    qkv_ref, out_ref, lse_ref, attended_ref = refs[:4]
+    whole, refs = refs[4 : 4 + count], refs[4 + count :]
+    cut, back, queries, values_t, send_in, take_in, send_out, take_out = refs[:8]
+    gather = gather_steps(plan, shards, whole, refs[8:])
     micro, _, length, width = qkv_ref.shape
     seq = lax.axis_size("seq")
     blocks = length // block
     per = block // TILE
     place_rows = length // seq
     masks = head_masks((block, width), heads)
-    greet([{"seq": peer_at(step)} for step in range(1, seq)])
+    per_micro = blocks + seq - 1
+    window = min(WINDOW, seq - 1)
+    placed = spread(gather[1:-1], 0, GATHER_END * micro * per_micro // 100)
+    greet(both_peers())
 
     def launch(m, carry):
         cut_heads(rows_ref, m, 3, cut)
 
-        @pl.when(m < 2)
+        @pl.when(m < 1)
         def _():
-            send_blocks(cut, qkv_ref, send_in, take_in, m)
-
+            for step in range(1, window + 1):
+                to_peer(cut, qkv_ref, send_in, take_in, m, step).start()
+
+        to_self(cut, qkv_ref, send_in, m).start()
         return carry
 
     lax.fori_loop(0, micro, launch, 0)
+    gather[0]()
     key_place = lax.broadcasted_iota(jnp.int32, (block, block), 0)
     query_place = lax.broadcasted_iota(jnp.int32, (block, block), 1)
     causal = key_place <= query_place
 
     def one_micro(m, carry):
-        take_blocks(cut, qkv_ref, send_in, take_in, m)
-
-        @pl.when(m + 2 < micro)
-        def _():
-            send_blocks(cut, qkv_ref, send_in, take_in, m + 2)
+        def between(step):
+            run_slot(placed, m * per_micro + step - 1)
+            if step + window < seq:
+                to_peer(cut, qkv_ref, send_in, take_in, m, step + window).start()
+            else:
+
+                @pl.when(m + 1 < micro)
+                def _():
+                    following = step + window + 1 - seq
+                    to_peer(cut, qkv_ref, send_in, take_in, m + 1, following).start()
+
+        take_blocks(cut, qkv_ref, send_in, take_in, m, between)
 
         def prepare(i, carry):
             rows = rows_at(i, block)
@@ -469,6 +672,7 @@
             return (raw.reshape(per, TILE, block) + bias[:, None, :]).reshape(block, block)
 
         def query_block(i, carry):
+            run_slot(placed, m * per_micro + seq - 1 + i)
             state = []
             for h in range(heads):
                 s = jnp.where(causal, scores_of(i, i, h), masked_score)
@@ -519,9 +723,10 @@
         return carry
 
     lax.fori_loop(0, micro, finish, 0)
-
-
-def self_forward(projected, bias, seq):
+    gather[-1]()
+
+
+def self_forward(projected, bias, seq, shards, kinds, groups, y_size):
     micro, rows, width = projected.shape
     part = width // 3 // seq
     heads = part // HD
@@ -529,16 +734,20 @@
     blocks = length // BLOCK
     whole = pl.BlockSpec(memory_space=pltpu.VMEM)
     sems = pltpu.SemaphoreType.DMA((micro, seq))
+    count = len(shards)
+    any_place = [pl.BlockSpec(memory_space=pl.ANY)] * count
+    plan = gather_parts(shards, kinds, groups)
     return pl.pallas_call(
-        functools.partial(self_forward_kernel, heads, BLOCK),
-        in_specs=[whole, whole],
-        out_specs=[whole] * 4,
+        functools.partial(self_forward_kernel, heads, BLOCK, plan, count),
+        in_specs=[whole, whole] + any_place,
+        out_specs=[whole] * 4 + any_place,
         out_shape=[
             jax.ShapeDtypeStruct((micro, 3, length, part), bf16),
             jax.ShapeDtypeStruct((micro, 1, length, part), bf16),
             jax.ShapeDtypeStruct((micro, blocks, heads, BLOCK), f32),
             jax.ShapeDtypeStruct((micro, rows, width // 3), bf16),
-        ],
+        ]
+        + [gather_out(s, k, seq // 2, y_size) for s, k in zip(shards, kinds)],
         scratch_shapes=[
             pltpu.VMEM((micro, 3, seq, rows, part), bf16),
             pltpu.VMEM((micro, 1, seq, rows, part), bf16),
@@ -548,28 +757,13 @@
             sems,
             sems,
             sems,
-        ],
+        ]
+        + gather_sems(plan, seq // 2, y_size),
         compiler_params=pltpu.CompilerParams(
             vmem_limit_bytes=50 << 20, collective_id=1, has_side_effects=True
         ),
         name="self_forward",
-    )(projected, bias)
-
-
-def spread(steps, first, last):
-    return [(first + k * (last - first) // max(1, len(steps) - 1), s) for k, s in enumerate(steps)]
-
-
-def run_slot(placed, slot):
-    for at, step in placed:
-        pl.when(slot == at)(step)
-
-
-def both_peers():
-    _, _, y, c, _, y_size = scatter_places()
-    peers = [{"seq": peer_at(step)} for step in range(1, lax.axis_size("seq"))]
-    peers += [{"fsdp": 2 * y + 1 - c}]
-    return peers + [{"fsdp": 2 * lax.rem(y + k, y_size) + c} for k in range(1, y_size)]
+    )(projected, bias, *shards)
 
 
 def self_backward_kernel(heads, block, kinds, *refs):
@@ -878,21 +1072,13 @@
     total_rows = micro * row_count
     memory_rows = memory.shape[2]
 
-    def gather(shard, axis=0):
-        return lax.all_gather(shard, ALL, axis=axis, tiled=True)
-
-    joint_weight = gather(self_qkv)
-    norms = gather(jnp.concatenate([norm_gain, norm_bias], 0), 1).astype(f32)
-    gain_rows, bias_rows = norms[:3], norms[3:]
-    small = gather(jnp.concatenate([self_out, cross_q, cross_kv, cross_out, ffn_in], 1))
-    memory_full = lax.all_gather(memory[:, 0], "seq", axis=1, tiled=True)
-    down_weight = gather(ffn_out)
-    cuts = [0]
-    for shard in (self_out, cross_q, cross_kv, cross_out, ffn_in):
-        cuts.append(cuts[-1] + shard.shape[1])
-    self_output, cross_weight, pair_weight, cross_output, upward_weight = (
-        small[:, a:b] for a, b in zip(cuts[:-1], cuts[1:])
-    )
+    devices = seq * lax.axis_size("fsdp")
+    z_size, y_size = seq // 2, lax.axis_size("fsdp") // 2
+
+    def flat(blocks):
+        return blocks.reshape(-1, blocks.shape[-1])
+
+    joint_weight = flat(gather_first([self_qkv], ("all",), ((0,),), z_size, y_size, 4)[0])
 
     x = tokens.reshape(total_rows, width)
     x32 = x.astype(f32)
@@ -900,9 +1086,31 @@
     lengths = memory_lengths[:, 0]
 
     projected = dot_nn(x, joint_weight).astype(bf16)
-    qkv, attended_heads, self_lse, attended = self_forward(
-        projected.reshape(micro, row_count, 3 * width), bias, seq
-    )
+    gathered = self_forward(
+        projected.reshape(micro, row_count, 3 * width),
+        bias,
+        seq,
+        [
+            self_out,
+            jnp.concatenate([norm_gain, norm_bias], 0).astype(f32),
+            cross_q,
+            cross_kv,
+            memory.reshape(micro * memory_rows, width),
+            cross_out,
+            ffn_in,
+            ffn_out,
+        ],
+        ("all", "all", "all", "all", "seq", "all", "all", "all"),
+        ((0, 1), (2, 4), (3,), (5,), (6,), (7,)),
+        y_size,
+    )
+    qkv, attended_heads, self_lse, attended = gathered[:4]
+    self_output, cross_weight, pair_weight = (flat(gathered[i]) for i in (4, 6, 7))
+    cross_output, upward_weight, down_weight = (flat(gathered[i]) for i in (9, 10, 11))
+    norms = gathered[5].reshape(devices, 6, width // devices).transpose(1, 0, 2).reshape(6, width)
+    gain_rows, bias_rows = norms[:3], norms[3:]
+    memory_full = gathered[8].reshape(seq, micro, memory_rows, width).transpose(1, 0, 2, 3)
+    memory_full = memory_full.reshape(micro, seq * memory_rows, width)
     attended = attended.reshape(total_rows, width)
 
     mixed_first = residual_weight * x32 + dot_nn(attended, self_output)
@@ -965,7 +1173,7 @@
         seq,
         [grad_upward, grad_down],
         (True, False),
-        lax.axis_size("fsdp") // 2,
+        y_size,
     )
     grad_projected = grad_projected.reshape(total_rows, 3 * width)
     grad_joint = dot_tn(x, grad_projected).astype(bf16)
@@ -976,7 +1184,6 @@
     norm_grads = jnp.stack(
         [gain_first, gain_second, gain_third, bias_first, bias_second, bias_third]
     )
-    devices = seq * lax.axis_size("fsdp")
     norm_blocks = norm_grads.reshape(6, devices, width // devices).transpose(1, 0, 2)
     owned = scatter_grads(
         [
@@ -988,8 +1195,8 @@
             norm_blocks.reshape(6 * devices, width // devices),
         ],
         (True, True, False, False, False, False),
-        seq // 2,
-        lax.axis_size("fsdp") // 2,
+        z_size,
+        y_size,
         3,
     )
     return (

time: 936 us -> 883 us (0.943)
  Pallas kernels: 589 us -> 671 us
  waiting for transfers between devices: 75 us -> 0.04 us
  blocking collectives: 43.6 us -> 0 us
  matrix products: 164 us -> 146 us
    pallas_call x1 -> x2, Pallas kernels: 230 us -> 338 us  [the longest x1 293 us: self_forward(): pl.pallas_call(functools.partial(self_forward_kernel, heads, BLOCK, plan,...]
    all_gather x4 -> x0, waiting for transfers between devices: 73.1 us -> none  [the longest x3 50.3 us: gather(): return lax.all_gather(shard, ALL, axis=axis, tiled=True)]
    all_gather x1 -> x0, blocking collectives: 43.6 us -> none  [gather(): return lax.all_gather(shard, ALL, axis=axis, tiled=True)]
    pallas_call x1, Pallas kernels: 115 us -> 96.7 us  [scatter_grads(): pl.pallas_call(functools.partial(scatter_kernel, kinds), in_specs=[pl.Blo...]
    dot_general x7, matrix products: 55.9 us -> 45.1 us  [dot_nn(): lax.dot_general(a, b, (((1,), (0,)), ((), ())), preferred_element_type=f32)]
    unnamed x107 -> x125, local copies, waits for them, and re-layouts: 20.5 us -> 22.8 us
  transfers between devices with their start and end apart: 5 -> 1, of which waited for: 3 -> 0; matrix products, arithmetic and copies ran while one was open for 10% -> 7% of each run, Pallas kernels for 49% -> 22%
where the time goes in v5:
time: 883 us; the launch traced here: 880 us
  Pallas kernels  671 us (76%)
  matrix products  146 us (17%)
  local copies, waits for them, and re-layouts  29.7 us (3%)
  other arithmetic  18.3 us (2%)
  between operations  15.1 us (2%)
    pallas_call x1, Pallas kernels, self_forward(): pl.pallas_call(functools.partial(self_forward_kernel, heads, BLOCK, plan,...  293 us
    pallas_call x1, Pallas kernels, self_backward(): pl.pallas_call(functools.partial(self_backward_kernel, heads, BLOCK, kind...  194 us
    pallas_call x1, Pallas kernels, scatter_grads(): pl.pallas_call(functools.partial(scatter_kernel, kinds), in_specs=[pl.Blo...  96.7 us
    dot_general x7, matrix products, dot_nt(): lax.dot_general(a, b, (((1,), (1,)), ((), ())), preferred_element_type=f32)  51.8 us
    dot_general x7, matrix products, dot_tn(): lax.dot_general(a, b, (((0,), (0,)), ((), ())), preferred_element_type=f32)  47.5 us
    pallas_call x1, Pallas kernels, gather_first(): pl.pallas_call(functools.partial(gather_kernel, plan, len(shards)), in_sp...  45.5 us
    dot_general x7, matrix products, dot_nn(): lax.dot_general(a, b, (((1,), (0,)), ((), ())), preferred_element_type=f32)  45.1 us
    unnamed x125, local copies, waits for them, and re-layouts  22.8 us
  transfers between devices with their start and end apart: 1, of which 0 were waited for; matrix products, arithmetic and copies ran while one was open for 7% of the time, Pallas kernels for 22%

profile of v5, /device:TPU:0, one launch (start us, length us, event | category | flops | bytes accessed | tf_op | source)
XLA Modules:
  0.0 879.5 jit_solution(7634336616888164000)
XLA Ops:
  7.3 45.5 %gather_first.1 = bf16[4,2,2,2,32,3072]{5,4,3,2,1,0:T(8,128)(2,1)} custom-call(bf16[32,3072]{1,0:T(8,128)(2,1)} %refs_0_.1), custom_call_target="tpu_custom_call" | custom-call | tf_op jit(solution)/shard_map/gather_first/pallas_call | solution.py:599
  52.8 0.2 convolution_minimum_fusion.3
  53.6 0.2 fusion.28
  53.8 0.2 fusion.19
  54.1 1.3 copy.31
  55.4 0.5 broadcast_in_dim.12
  55.9 0.5 reshape.247.refs_1_.refs_2_
  56.5 9.8 %convolution_convert_fusion.3 = bf16[768,3072]{1,0:T(8,128)(2,1)} fusion(bf16[768,1024]{1,0:T(8,128)(2,1)S(1)} %bitcast.170, bf16[1024,3072]{1,0:T(8,128)(2,1)} %bitcast.129), kind=kOutput, calls=%fused_computation.16 | convolution fusion | flops 4834197504 | bytes 12582912 | tf_op jit(solution)/shard_map/dot_general | solution.py:30
  66.4 292.7 %self_forward.1 = (bf16[3,3,2048,128]{3,2,1,0:T(8,128)(2,1)}, bf16[3,1,2048,128]{3,2,1,0:T(8,128)(2,1)S(1)}, f32[3,8,2,256]{3,2,1,0:T(2,128)S(1)}, bf16[3,256,10...) custom-call(bf16[3,256,3072]{2,1,0:T(8,128)(2,1)} %bitcast.134, ...), custom_call_target="tpu_custom_call" | custom-call | tf_op jit(solution)/shard_map/self_forward/pallas_call | solution.py:740
  359.1 1.2 copy-done.6
  360.3 0.3 slice_reduce_fusion.1
  360.6 0.3 copy-done.15
  361.0 3.9 fusion.40
  365.0 0.4 multiply_reduce_fusion.6
  365.5 2.1 copy-done.34
  367.5 1.3 copy.32
  369.0 6.2 convolution_convert_fusion.5
  375.2 1.8 convolution_convert_fusion.11
  377.1 21.5 %cross_forward.1 = (bf16[3,256,1024]{2,1,0:T(8,128)(2,1)S(1)}, f32[3,8,2,256]{3,2,1,0:T(2,128)S(1)}) custom-call(s32[3]{0:T(128)S(1)} %bitcast.122, bf16[3,256,1024]{2,1,0:T(8,128)(2,1)S(1)} %bitcast.114, bf16[3,256,2048]{2,1,0:T(8,128)(2,1)S(1)} %bitcast.110, bf16[3,256,2048]{2,1,0:T(8,128)(2,1)S(1)} %bitcast.111), custom_call_target="tpu_custom_call" | custom-call | tf_op jit(solution)/shard_map/cross_forward/pallas_call | solution.py:947
  398.7 2.1 fusion.41
  400.8 0.4 multiply_reduce_fusion.5
  401.4 2.4 slice-done.3
  403.8 9.6 %fusion.35 = f32[768,4096]{1,0:T(8,128)} fusion(bf16[1024,4096]{1,0:T(8,128)(2,1)S(1)} %bitcast.155, f32[768,1024]{1,0:T(8,128)S(1)} %get-tuple-element.113, f32[1024]{0:T(1024)S(1)} %add.98, f32[1024]{0:T(1024)S(1)} %mul.238, f32[768]{0:T(1024)S(1)} %add_rsqrt_fusion.1, f32[768]{0:T(1024)S(1)} %broadcast_multiply_fusion.7), kind=kOutput, calls=%fused_computation.107 | convolution fusion | flops 6446383104 | bytes 24131584 | tf_op jit(solution)/shard_map/dot_general | solution.py:30
  413.4 11.6 %fusion.42 = (f32[768]{0:T(1024)S(1)}, f32[768,1024]{1,0:T(8,128)S(1)}) fusion(bf16[4096,1024]{1,0:T(8,128)(2,1)S(1)} %bitcast.159, f32[768,4096]{1,0:T(8,128)} %fusion.35, f32[1024]{0:T(1024)S(1)} %add.98, f32[1024]{0:T(1024)S(1)} %mul.238, f32[768]{0:T(1024)S(1)} %add_rsqrt_fusion.1, f32[768,1024]{1,0:T(8,128)S(1)} %get-tuple-element.113, ...), kind=kOutput, calls=%fused_computation.111 | convolution fusion | flops 6476266496 | bytes 27280384 | tf_op jit(solution)/shard_map/dot_general | solution.py:30
  425.1 1.7 copy-done.19
  426.8 0.4 multiply_reduce_fusion.4
  427.3 2.2 convert_reduce_fusion
  429.5 3.4 fusion.16
  433.0 4.7 fusion.13
  437.7 19.6 %fusion.9 = bf16[768,4096]{1,0:T(8,128)(2,1)} fusion(f32[768,4096]{1,0:T(8,128)} %fusion.35, bf16[4096,1024]{1,0:T(8,128)(2,1)} %bitcast.156, f32[768,1024]{1,0:T(8,128)S(1)} %get-tuple-element.106), kind=kOutput, calls=%fused_computation.11 | convolution fusion | flops 6499860480 | bytes 30408704 | tf_op jit(solution)/shard_map/dot_general | solution.py:34
  457.3 12.4 %multiply_reduce_fusion = (f32[1024]{0:T(1024)S(1)}, f32[768]{0:T(1024)S(1)}, f32[768]{0:T(1024)S(1)}, f32[1024]{0:T(1024)S(1)}, f32[768,1024]{1,0:T(8,128)S(1)}) fusion(f32[768,1024]{1,0:T(8,128)S(1)} %copy-done.25, f32[768]{0:T(1024)S(1)} %add_rsqrt_fusion.1, f32[768]{0:T(1024)S(1)} %broadcast_multiply_fusion.7, f32[1024]{0:T(1024)S(1)} %mul.238, ...), kind=kOutput, calls=%fused_computation.31 | convolution fusion | flops 6451097600 | bytes 24141824 | tf_op jit(solution)/shard_map/dot_general | solution.py:34
  469.7 1.1 subtract_multiply_fusion.1
  470.8 0.5 copy-done.45
  471.3 1.9 convolution_convert_fusion.10
  473.2 0.7 copy-done.1
  473.9 0.5 copy-done.4
  474.3 20.8 %cross_backward.1 = (bf16[3,256,1024]{2,1,0:T(8,128)(2,1)S(1)}, bf16[3,256,1024]{2,1,0:T(8,128)(2,1)S(1)}, bf16[3,256,1024]{2,1,0:T(8,128)(2,1)S(1)}) custom-call(s32[3]{0:T(128)S(1)} %bitcast.123, bf16[3,256,1024]{2,1,0:T(8,128)(2,1)S(1)} %bitcast.115, bf16[3,256,2048]{2,1,0:T(8,128)(2,1)S(1)} %bitcast.112, bf16[3,256,2048]{2,1,0:T(8,128)(2,1)S(1)} %bitcast.113, ...), custom_call_target="tpu_custom_call" | custom-call | tf_op jit(solution)/shard_map/cross_backward/pallas_call | solution.py:1020
  495.1 1.1 copy-done.17
  496.3 2.0 pad_maximum_fusion
  498.3 14.7 %convolution_convert_fusion = bf16[4096,1024]{1,0:T(8,128)(2,1)} fusion(f32[768,1024]{1,0:T(8,128)} %copy-done.30, f32[768,4096]{1,0:T(8,128)} %fusion.35), kind=kOutput, calls=%fused_computation.13 | convolution fusion | flops 6475743232 | bytes 24117248 | tf_op jit(solution)/shard_map/dot_general | solution.py:38
  513.0 4.4 multiply_reduce_fusion.1
  518.0 3.5 subtract_multiply_fusion
  521.5 1.7 copy-done.31
  523.2 3.0 convolution_convert_fusion.9
  526.2 9.6 %convolution_convert_fusion.1 = bf16[1024,4096]{1,0:T(8,128)(2,1)} fusion(bf16[768,4096]{1,0:T(8,128)(2,1)S(1)} %bitcast.177, f32[768,1024]{1,0:T(8,128)S(1)} %copy-done.26, f32[1024]{0:T(1024)S(1)} %add.98, f32[1024]{0:T(1024)S(1)} %mul.238, f32[768]{0:T(1024)S(1)} %add_rsqrt_fusion.1, f32[768]{0:T(1024)S(1)} %broadcast_multiply_fusion.7), kind=kOutput, calls=%fused_computation.14 | convolution fusion | flops 6450577408 | bytes 17840128 | tf_op jit(solution)/shard_map/dot_general | solution.py:38
  535.8 193.6 %self_backward.1 = (bf16[3,256,3072]{2,1,0:T(8,128)(2,1)}, f32[32,4096]{1,0:T(8,128)}, f32[128,1024]{1,0:T(8,128)}) custom-call(bf16[3,256,1024]{2,1,0:T(8,128)(2,1)} %bitcast.145, bf16[3,3,2048,128]{3,2,1,0:T(8,128)(2,1)} %get-tuple-element.50.refs_1_, f32[3,8,8,2,256]{4,3,2,1,0:T(2,128)} %copy-done.2, bf16[3,1,2048,128]{3,2,1,0:T(8,128)(2,1)} %copy-done.6, ...), custom_call_target="tpu_custom_call" | custom-call | tf_op jit(solution)/shard_map/self_backward/pallas_call | solution.py:889
  729.4 0.8 stack.27
  730.2 5.7 convolution_convert_fusion.8
  735.9 3.3 convolution_convert_fusion.6
  739.2 3.6 convolution_convert_fusion.7
  742.9 0.4 slice-done.7
  743.3 6.2 add_convert_fusion
  749.4 7.4 convolution_convert_fusion.2
  756.9 4.5 convolution_convert_fusion.12
  761.4 3.3 convolution_convert_fusion.4
  764.7 96.7 %scatter_grads.1 = (f32[32,3072]{1,0:T(8,128)}, f32[32,1024]{1,0:T(8,128)}, f32[32,2048]{1,0:T(8,128)}, f32[32,1024]{1,0:T(8,128)}, f32[32,1024]{1,0:T(8,128)}, /*index=5*/f32[6,32]{1,0:T(8,128)}) custom-call(bf16[4,2,2,2,32,3072]{5,4,3,2,1,0:T(8,128)(2,1)} %bitcast.133, bf16[4,2,2,2,32,1024]{5,4,3,2,1,0:T(8,128)(2,1)} %bitcast.139, ...), custom_call_target="tpu_custom_call" | custom-call | tf_op jit(solution)/shard_map/scatter_grads/pallas_call | solution.py:415
  861.4 1.3 fusion.39
  862.8 1.8 copy.49
  864.5 1.6 copy.50
  866.1 1.6 copy.51
  867.7 1.7 copy.52
  869.3 1.6 copy.53
  870.9 0.8 copy.54
  871.7 0.8 copy.55
  (145 shorter events, 2.2 us)
Async XLA Ops:
  7.2 749.7 %reduce-scatter.2.cloned.1.call-start = ((), (), s32[]{:S(2)}) async-start(), calls=%async_computation.1 | async-start | bytes 3538944 | tf_op jit(solution)/shard_map/reduce_scatter | solution.py:1157
  7.2 45.6 %copy-start.37 = (s32[3,1,13]{2,1,0:T(1,128)S(1)}, s32[3,1,13]{2,1,0:T(1,128)}, u32[]{:S(2)}) copy-start(s32[3,1,13]{2,1,0:T(1,128)} %param.19) | copy-start | bytes 472
  7.2 46.3 %copy-start.38 = (s32[3,1,16]{2,1,0:T(1,128)S(1)}, s32[3,1,16]{2,1,0:T(1,128)}, u32[]{:S(2)}) copy-start(s32[3,1,16]{2,1,0:T(1,128)} %param.18) | copy-start | bytes 580
  7.3 49.1 %copy-start.46 = (bf16[3,1,256,1024]{3,2,1,0:T(8,128)(2,1)S(1)}, bf16[3,1,256,1024]{3,2,1,0:T(8,128)(2,1)}, u32[]{:S(2)}) copy-start(bf16[3,1,256,1024]{3,2,1,0:T(8,128)(2,1)} %param.15) | copy-start | bytes 4718596
  56.3 10.0 %copy-start.2 = (f32[3,8,8,2,256]{4,3,2,1,0:T(2,128)}, f32[3,8,8,2,256]{4,3,2,1,0:T(2,128)S(1)}, u32[]{:S(2)}) copy-start(f32[3,8,8,2,256]{4,3,2,1,0:T(2,128)S(1)} %reshape.247.refs_1_.refs_2_) | copy-start | bytes 1179652
  56.3 9.9 %copy-start.39 = (bf16[3,32]{1,0:T(4,128)(2,1)S(1)}, bf16[3,32]{1,0:T(4,128)(2,1)}, u32[]{:S(2)}) copy-start(bf16[3,32]{1,0:T(4,128)(2,1)} %param.29) | copy-start | bytes 580
  56.4 9.9 %copy-start.40 = (bf16[3,32]{1,0:T(4,128)(2,1)S(1)}, bf16[3,32]{1,0:T(4,128)(2,1)}, u32[]{:S(2)}) copy-start(bf16[3,32]{1,0:T(4,128)(2,1)} %param.28) | copy-start | bytes 580
  56.4 9.9 %copy-start.7 = (bf16[3,1,32,1024]{3,2,1,0:T(8,128)(2,1)S(1)}, bf16[3,1,32,1024]{3,2,1,0:T(8,128)(2,1)}, u32[]{:S(2)}) copy-start(bf16[3,1,32,1024]{3,2,1,0:T(8,128)(2,1)} %param.16) | copy-start | bytes 589828
  56.4 9.9 %copy-start.9 = (bf16[32,4096]{1,0:T(8,128)(2,1)S(1)}, bf16[32,4096]{1,0:T(8,128)(2,1)}, u32[]{:S(2)}) copy-start(bf16[32,4096]{1,0:T(8,128)(2,1)} %refs_8_.1) | copy-start | bytes 786436
  56.4 9.9 %copy-start.10 = (bf16[128,1024]{1,0:T(8,128)(2,1)S(1)}, bf16[128,1024]{1,0:T(8,128)(2,1)}, u32[]{:S(2)}) copy-start(bf16[128,1024]{1,0:T(8,128)(2,1)} %refs_9_.1) | copy-start | bytes 786436
  56.4 9.9 %copy-start.11 = (bf16[32,2048]{1,0:T(8,128)(2,1)S(1)}, bf16[32,2048]{1,0:T(8,128)(2,1)}, u32[]{:S(2)}) copy-start(bf16[32,2048]{1,0:T(8,128)(2,1)} %refs_5_.1) | copy-start | bytes 393220
  56.4 9.9 %copy-start.12 = (bf16[32,1024]{1,0:T(8,128)(2,1)S(1)}, bf16[32,1024]{1,0:T(8,128)(2,1)}, u32[]{:S(2)}) copy-start(bf16[32,1024]{1,0:T(8,128)(2,1)} %refs_2_.1) | copy-start | bytes 196612
  56.4 9.9 %copy-start.13 = (bf16[32,1024]{1,0:T(8,128)(2,1)S(1)}, bf16[32,1024]{1,0:T(8,128)(2,1)}, u32[]{:S(2)}) copy-start(bf16[32,1024]{1,0:T(8,128)(2,1)} %refs_4_.1) | copy-start | bytes 196612
  56.4 9.9 %copy-start.14 = (bf16[32,1024]{1,0:T(8,128)(2,1)S(1)}, bf16[32,1024]{1,0:T(8,128)(2,1)}, u32[]{:S(2)}) copy-start(bf16[32,1024]{1,0:T(8,128)(2,1)} %refs_7_.1) | copy-start | bytes 196612
  359.1 1.2 copy-start.6
  360.3 0.6 copy-start.15
  365.0 3.8 copy-start.20
  365.0 2.5 copy-start.34
  369.0 6.2 copy-start.21
  369.0 6.2 copy-start.42
  375.2 1.9 copy-start.16
  377.1 21.6 %copy-start = (bf16[768,1024]{1,0:T(8,128)(2,1)}, bf16[768,1024]{1,0:T(8,128)(2,1)S(1)}, u32[]{:S(2)}) copy-start(bf16[768,1024]{1,0:T(8,128)(2,1)S(1)} %convolution_convert_fusion.11) | copy-start | bytes 4718596
  377.1 21.6 %copy-start.44 = (bf16[4,2,2,2,32,1024]{5,4,3,2,1,0:T(8,128)(2,1)S(1)}, bf16[4,2,2,2,32,1024]{5,4,3,2,1,0:T(8,128)(2,1)}, u32[]{:S(2)}) copy-start(bf16[4,2,2,2,32,1024]{5,4,3,2,1,0:T(8,128)(2,1)} %get-tuple-element.45) | copy-start | bytes 6291460
  398.7 2.1 copy-start.3
  398.7 2.8 slice-start.2
  398.7 5.1 slice-start.3
  400.8 12.7 %copy-start.24 = (f32[768,1024]{1,0:T(8,128)}, f32[768,1024]{1,0:T(8,128)S(1)}, u32[]{:S(2)}) copy-start(f32[768,1024]{1,0:T(8,128)S(1)} %get-tuple-element.113) | copy-start | bytes 9437188
  400.8 12.6 %slice-start.4 = ((s8[8388608]{0:T(1024)(128)(4,1)}), s8[4194304]{0:T(1024)(128)(4,1)S(1)}, s32[]{:S(2)}) async-start(s8[8388608]{0:T(1024)(128)(4,1)} %bitcast.157), calls=%async_computation.6 | async-start | bytes 8388608
  403.8 9.6 %slice-start.5 = ((s8[8388608]{0:T(1024)(128)(4,1)}), s8[4194304]{0:T(1024)(128)(4,1)S(1)}, s32[]{:S(2)}) async-start(s8[8388608]{0:T(1024)(128)(4,1)} %bitcast.157), calls=%async_computation.7 | async-start | bytes 8388608
  425.0 1.7 copy-start.19
  437.7 19.6 %copy-start.30 = (f32[768,1024]{1,0:T(8,128)}, f32[768,1024]{1,0:T(8,128)S(1)}, u32[]{:S(2)}) copy-start(f32[768,1024]{1,0:T(8,128)S(1)} %get-tuple-element.106) | copy-start | bytes 9437188
  437.7 19.6 %copy-start.25 = (f32[768,1024]{1,0:T(8,128)S(1)}, f32[768,1024]{1,0:T(8,128)}, u32[]{:S(2)}) copy-start(f32[768,1024]{1,0:T(8,128)} %copy-done.24) | copy-start | bytes 9437188
  469.7 1.6 copy-start.45
  471.3 1.9 copy-start.27
  471.3 2.5 copy-start.1
  471.3 3.0 copy-start.4
  495.1 1.1 copy-start.17
  498.3 14.7 %copy-start.18 = (bf16[3,256,1024]{2,1,0:T(8,128)(2,1)S(1)}, bf16[3,256,1024]{2,1,0:T(8,128)(2,1)}, u32[]{:S(2)}) copy-start(bf16[3,256,1024]{2,1,0:T(8,128)(2,1)} %copy-done.17) | copy-start | bytes 4718596
  498.3 14.7 %copy-start.22 = (f32[768,1024]{1,0:T(8,128)S(1)}, f32[768,1024]{1,0:T(8,128)}, u32[]{:S(2)}) copy-start(f32[768,1024]{1,0:T(8,128)} %copy-done.20) | copy-start | bytes 9437188
  498.3 14.7 %copy-start.28 = (f32[768,1024]{1,0:T(8,128)S(1)}, f32[768,1024]{1,0:T(8,128)}, u32[]{:S(2)}) copy-start(f32[768,1024]{1,0:T(8,128)} %copy-done.27) | copy-start | bytes 9437188
  498.3 14.7 %copy-start.43 = (bf16[4,2,2,2,32,1024]{5,4,3,2,1,0:T(8,128)(2,1)S(1)}, bf16[4,2,2,2,32,1024]{5,4,3,2,1,0:T(8,128)(2,1)}, u32[]{:S(2)}) copy-start(bf16[4,2,2,2,32,1024]{5,4,3,2,1,0:T(8,128)(2,1)} %get-tuple-element.41) | copy-start | bytes 6291460
  517.9 5.3 copy-start.41
  517.9 8.2 slice-start.8
  521.5 1.7 copy-start.31
  523.2 3.0 copy-start.26
  523.2 3.0 slice-start.9
  730.2 5.7 copy-start.5
  730.2 5.7 copy-start.29
  735.9 3.3 copy-start.23
  735.9 6.9 slice-start
  735.9 6.8 slice-start.6
  739.2 3.6 slice-start.1
  739.2 3.7 copy-start.32
  739.2 4.1 slice-start.7
  743.3 6.2 copy-start.47
  756.9 4.5 copy-start.8
  756.9 4.5 copy-start.33
  764.7 106.2 %copy-start.36 = (f32[32,4096]{1,0:T(8,128)S(1)}, f32[32,4096]{1,0:T(8,128)}, u32[]{:S(2)}) copy-start(f32[32,4096]{1,0:T(8,128)} %get-tuple-element.140) | copy-start | bytes 1572868
  861.4 10.3 %copy-start.35 = (f32[128,1024]{1,0:T(8,128)S(1)}, f32[128,1024]{1,0:T(8,128)}, u32[]{:S(2)}) copy-start(f32[128,1024]{1,0:T(8,128)} %get-tuple-element.141) | copy-start | bytes 1572868
Sparse Core Ops, SparseCore 0:
  498.4 106.5 reduce-scatter.1

commit v6 on v5

--- a/solution.py
+++ b/solution.py
@@ -222,6 +222,12 @@
 
 
 def scatter_shapes(blocks, x_first):
+    if x_first == "seq":
+        z_size, _, rows, columns = blocks.shape
+        shape = (z_size, rows, columns)
+        return [pltpu.VMEM(shape, blocks.dtype)] * 2 + [
+            pltpu.VMEM((z_size - 1, rows, columns), blocks.dtype)
+        ]
     z_size, _, y_size, _, rows, columns = blocks.shape
     if x_first:
         first, second = (1, y_size), (y_size - 1,)
@@ -265,9 +271,32 @@
             device_id_type=MESH,
         )
 
+    across = [a for a in range(count) if kinds[a] != "seq"]
+    along = [a for a in range(count) if kinds[a] == "seq"]
+
     def own_copy(a, t):
-        return pltpu.make_async_copy(
-            sources[a].at[to_z(t), :, :, c], buffers[a][0].at[t], local.at[a, t]
+        if kinds[a] == "seq":
+            source = sources[a].at[to_z(t), x]
+        else:
+            source = sources[a].at[to_z(t), :, :, c]
+        return pltpu.make_async_copy(source, buffers[a][0].at[t], local.at[a, t])
+
+    def seq_first(a, t):
+        return remote(
+            sources[a].at[to_z(t), 1 - x],
+            buffers[a][1].at[t],
+            core_s.at[a, t],
+            core_r.at[a, t],
+            x_peer(),
+        )
+
+    def seq_last(a, t):
+        return remote(
+            buffers[a][0].at[t],
+            buffers[a][2].at[t],
+            last_s.at[a, t],
+            last_r.at[a, t],
+            {"seq": 2 * to_z(t) + x},
         )
 
     def core_copy(a, t):
@@ -322,11 +351,11 @@
 
     def start_core(t):
         for a in range(count):
-            core_copy(a, t).start()
+            (core_copy if a in across else seq_first)(a, t).start()
             own_copy(a, t).start()
 
     def core_step(t):
-        for a in range(count):
+        for a in across:
             core_copy(a, t).wait_recv()
             own_copy(a, t).wait()
             own, core = buffers[a][:2]
@@ -342,7 +371,7 @@
             start_core(t + 2)
 
     def first_step(t):
-        for a in range(count):
+        for a in across:
             own, _, first, _, _ = buffers[a]
             for k, copy in enumerate(first_copies(a, t)):
                 copy.wait_recv()
@@ -353,7 +382,13 @@
                 copy.start()
 
     def second_step(t):
-        for a in range(count):
+        for a in along:
+            seq_first(a, t).wait_recv()
+            own_copy(a, t).wait()
+            add_into(buffers[a][0].at[t], buffers[a][1].at[t])
+            if t < z_size - 1:
+                seq_last(a, t).start()
+        for a in across:
             own, _, _, second, _ = buffers[a]
             for k, copy in enumerate(second_copies(a, t)):
                 copy.wait_recv()
@@ -362,7 +397,16 @@
                 last_copy(a, t).start()
 
     def final_step():
-        for a in range(count):
+        for a in along:
+            own, _, last = buffers[a]
+            total = own[z_size - 1].astype(f32)
+            for t in range(z_size - 1):
+                seq_last(a, t).wait()
+                total = total + last[t].astype(f32)
+            outs[a][...] = total
+            for t in range(z_size):
+                seq_first(a, t).wait_send()
+        for a in across:
             own, _, _, _, last = buffers[a]
             total = own[z_size - 1, x, y].astype(f32)
             for t in range(z_size - 1):
@@ -391,24 +435,34 @@
     return steps
 
 
+def scatter_buffers(kinds, refs):
+    buffers = []
+    for kind in kinds:
+        size = 3 if kind == "seq" else 5
+        buffers.append(refs[:size])
+        refs = refs[size:]
+    return buffers, refs
+
+
 def scatter_kernel(kinds, *refs):
     count = len(kinds)
     sources, outs, rest = refs[:count], refs[count : 2 * count], refs[2 * count :]
-    buffers = [rest[5 * a : 5 * a + 5] for a in range(count)]
+    buffers, rest = scatter_buffers(kinds, rest)
     greet(scatter_peers())
-    for step in scatter_steps(kinds, sources, outs, buffers, rest[5 * count :]):
+    for step in scatter_steps(kinds, sources, outs, buffers, rest):
         step()
 
 
-def scatter_blocks(arrays, z_size, y_size):
-    return [
-        a.reshape(z_size, 2, y_size, 2, a.shape[0] // (4 * z_size * y_size), a.shape[1])
-        for a in arrays
-    ]
+def scatter_blocks(arrays, kinds, z_size, y_size):
+    blocks = []
+    for a, kind in zip(arrays, kinds):
+        lead = (z_size, 2) if kind == "seq" else (z_size, 2, y_size, 2)
+        blocks.append(a.reshape(lead + (-1, a.shape[1])))
+    return blocks
 
 
 def scatter_grads(arrays, kinds, z_size, y_size, collective_id):
-    blocks = scatter_blocks(arrays, z_size, y_size)
+    blocks = scatter_blocks(arrays, kinds, z_size, y_size)
     scratch = []
     for block, kind in zip(blocks, kinds):
         scratch += scatter_shapes(block, kind)
@@ -416,7 +470,7 @@
         functools.partial(scatter_kernel, kinds),
         in_specs=[pl.BlockSpec(memory_space=pl.ANY)] * len(arrays),
         out_specs=[pl.BlockSpec(memory_space=pltpu.VMEM)] * len(arrays),
-        out_shape=[jax.ShapeDtypeStruct(b.shape[4:], f32) for b in blocks],
+        out_shape=[jax.ShapeDtypeStruct(b.shape[-2:], f32) for b in blocks],
         scratch_shapes=scratch + scatter_sems(len(arrays), z_size, y_size),
         compiler_params=pltpu.CompilerParams(
             vmem_limit_bytes=60 << 20, collective_id=collective_id, has_side_effects=True
@@ -773,8 +827,8 @@
     grad_ref, owned, refs = refs[0], refs[1 : 1 + count], refs[1 + count :]
     cut, gout, grads, back, queries, keys_h, gouts, delta, grad_q = refs[:9]
     send_in, take_in, send_out, take_out = refs[9:13]
-    buffers = [refs[13 + 5 * a : 18 + 5 * a] for a in range(count)]
-    scatter = scatter_steps(kinds, sources, owned, buffers, refs[13 + 5 * count :])
+    buffers, refs = scatter_buffers(kinds, refs[13:])
+    scatter = scatter_steps(kinds, sources, owned, buffers, refs)
     micro, _, length, width = qkv_ref.shape
     seq = lax.axis_size("seq")
     blocks = length // block
@@ -881,7 +935,7 @@
     blocks = length // BLOCK
     whole = pl.BlockSpec(memory_space=pltpu.VMEM)
     sems = pltpu.SemaphoreType.DMA((micro, seq))
-    sources = scatter_blocks(arrays, seq // 2, y_size)
+    sources = scatter_blocks(arrays, kinds, seq // 2, y_size)
     count = len(arrays)
     scratch = []
     for source, kind in zip(sources, kinds):
@@ -891,7 +945,7 @@
         in_specs=[whole] * 5 + [pl.BlockSpec(memory_space=pl.ANY)] * count,
         out_specs=[whole] * (1 + count),
         out_shape=[jax.ShapeDtypeStruct((micro, rows, 3 * width), bf16)]
-        + [jax.ShapeDtypeStruct(b.shape[4:], f32) for b in sources],
+        + [jax.ShapeDtypeStruct(b.shape[-2:], f32) for b in sources],
         scratch_shapes=[
             pltpu.VMEM((micro, 1, seq, rows, part), bf16),
             pltpu.VMEM((micro, 1, length, part), bf16),
@@ -916,28 +970,29 @@
     )(grad_attended, qkv, bias, out, lse, *sources)
 
 
-def cross_forward_kernel(lengths_ref, q_ref, k_ref, v_ref, out_ref, lse_ref):
-    count, width = k_ref.shape[1], k_ref.shape[2]
-    rows = q_ref.shape[1]
-    heads = width // HD
-    masks = head_masks((rows, width), heads)
+def cross_forward_kernel(lengths_ref, q_ref, pairs_ref, out_ref, lse_ref):
+    count, width, rows = pairs_ref.shape[1], q_ref.shape[2], q_ref.shape[1]
+    masks = head_masks((rows, 128), 2)
     valid = (
         lax.broadcasted_iota(jnp.int32, (count, rows), 0) < lengths_ref[pl.program_id(0)]
     )
-    q = q_ref[0].astype(f32) * scale_factor
-    values_t = jnp.transpose(v_ref[0].astype(f32)).astype(bf16)
-    outs, lses = [], []
-    for h in range(heads):
-        s = dot_nt(k_ref[0], keep_head(q, masks[h], heads).astype(bf16))
-        s = jnp.where(valid, s, masked_score)
-        m = jnp.max(s, 0, keepdims=True)
-        p = jnp.exp(s - m)
-        total = jnp.sum(p, 0, keepdims=True)
-        out = dot_nn(values_t[h * HD : (h + 1) * HD], p.astype(bf16))
-        outs.append(out * (1.0 / total))
-        lses.append(m + jnp.log(total))
-    out_ref[0] = jnp.transpose(jnp.concatenate(outs, 0)).astype(bf16)
-    lse_ref[0, 0] = jnp.concatenate(lses, 0)
+    for g in range(width // 128):
+        cut = slice(g * 128, g * 128 + 128)
+        q = q_ref[0, :, cut].astype(f32) * scale_factor
+        values = pairs_ref[0, :, width + g * 128 : width + g * 128 + 128]
+        values_t = jnp.transpose(values.astype(f32)).astype(bf16)
+        outs, lses = [], []
+        for h in range(2):
+            s = dot_nt(pairs_ref[0, :, cut], keep_head(q, masks[h], 2).astype(bf16))
+            s = jnp.where(valid, s, masked_score)
+            m = jnp.max(s, 0, keepdims=True)
+            p = jnp.exp(s - m)
+            total = jnp.sum(p, 0, keepdims=True)
+            out = dot_nn(values_t[h * HD : (h + 1) * HD], p.astype(bf16))
+            outs.append(out * (1.0 / total))
+            lses.append(m + jnp.log(total))
+        out_ref[0, :, cut] = jnp.transpose(jnp.concatenate(outs, 0)).astype(bf16)
+        lse_ref[0, g] = jnp.concatenate(lses, 0)
 
 
 def cross_forward(lengths, queries, pairs):
@@ -946,16 +1001,15 @@
     groups = width // 128
     return pl.pallas_call(
         cross_forward_kernel,
-        grid=(micro, groups),
+        grid=(micro,),
         in_specs=[
             pl.BlockSpec(memory_space=pltpu.SMEM),
-            pl.BlockSpec((1, rows, 128), lambda m, g: (m, 0, g)),
-            pl.BlockSpec((1, count, 128), lambda m, g: (m, 0, g)),
-            pl.BlockSpec((1, count, 128), lambda m, g: (m, 0, g + groups)),
+            pl.BlockSpec((1, rows, width), lambda m: (m, 0, 0)),
+            pl.BlockSpec((1, count, 2 * width), lambda m: (m, 0, 0)),
         ],
         out_specs=[
-            pl.BlockSpec((1, rows, 128), lambda m, g: (m, 0, g)),
-            pl.BlockSpec((1, 1, 2, rows), lambda m, g: (m, g, 0, 0)),
+            pl.BlockSpec((1, rows, width), lambda m: (m, 0, 0)),
+            pl.BlockSpec((1, groups, 2, rows), lambda m: (m, 0, 0, 0)),
         ],
         out_shape=[
             jax.ShapeDtypeStruct((micro, rows, width), bf16),
@@ -963,81 +1017,119 @@
         ],
         compiler_params=pltpu.CompilerParams(vmem_limit_bytes=32 << 20),
         name="cross_forward",
-    )(lengths, queries, pairs, pairs)
+    )(lengths, queries, pairs)
 
 
 def cross_backward_kernel(
-    lengths_ref, q_ref, k_ref, v_ref, out_ref, lse_ref, gout_ref, gq_ref, gk_ref, gv_ref
+    lengths_ref, q_ref, pairs_ref, out_ref, lse_ref, gout_ref, gq_ref, gpairs_ref
 ):
-    count, width = k_ref.shape[1], k_ref.shape[2]
-    rows = q_ref.shape[1]
-    heads = width // HD
-    masks = head_masks((rows, width), heads)
-    key_masks = head_masks((count, width), heads)
+    count, width, rows = pairs_ref.shape[1], q_ref.shape[2], q_ref.shape[1]
+    masks = head_masks((rows, 128), 2)
+    key_masks = head_masks((count, 128), 2)
     valid = (
         lax.broadcasted_iota(jnp.int32, (count, rows), 0) < lengths_ref[pl.program_id(0)]
     )
-    lane = lax.broadcasted_iota(jnp.int32, (8, width), 1)
-    row = lax.broadcasted_iota(jnp.int32, (8, width), 0)
+    lane = lax.broadcasted_iota(jnp.int32, (8, 128), 1)
+    row = lax.broadcasted_iota(jnp.int32, (8, 128), 0)
     pick = jnp.where((lane >= row * HD) & (lane < (row + 1) * HD), 1.0, 0.0)
-    q = q_ref[0].astype(f32) * scale_factor
-    g = gout_ref[0].astype(f32)
-    k = k_ref[0].astype(f32)
-    delta = lax.dot_general(
-        pick,
-        g * out_ref[0].astype(f32),
-        (((1,), (1,)), ((), ())),
-        precision=lax.Precision.HIGHEST,
-        preferred_element_type=f32,
-    )
-    grad_q = jnp.zeros((rows, width), f32)
-    grad_k = jnp.zeros((count, width), f32)
-    grad_v = jnp.zeros((count, width), f32)
-    for h in range(heads):
-        qh = keep_head(q, masks[h], heads).astype(bf16)
-        gh = keep_head(g, masks[h], heads).astype(bf16)
-        kh = keep_head(k, key_masks[h], heads).astype(bf16)
-        s = dot_nt(k_ref[0], qh) - lse_ref[0, 0, h : h + 1, :]
-        p = jnp.exp(jnp.where(valid, s, masked_score))
-        gp = dot_nt(v_ref[0], gh)
-        gs = (p * (gp - delta[h : h + 1, :])).astype(bf16)
-        grad_v += dot_nn(p.astype(bf16), gh)
-        grad_k += dot_nn(gs, qh)
-        grad_q += dot_tn(gs, kh)
-    gq_ref[0] = (grad_q * scale_factor).astype(bf16)
-    gk_ref[0] = grad_k.astype(bf16)
-    gv_ref[0] = grad_v.astype(bf16)
+    for group in range(width // 128):
+        cut = slice(group * 128, group * 128 + 128)
+        value_cut = slice(width + group * 128, width + group * 128 + 128)
+        q = q_ref[0, :, cut].astype(f32) * scale_factor
+        g = gout_ref[0, :, cut].astype(f32)
+        k = pairs_ref[0, :, cut].astype(f32)
+        delta = lax.dot_general(
+            pick,
+            g * out_ref[0, :, cut].astype(f32),
+            (((1,), (1,)), ((), ())),
+            precision=lax.Precision.HIGHEST,
+            preferred_element_type=f32,
+        )
+        grad_q = jnp.zeros((rows, 128), f32)
+        grad_k = jnp.zeros((count, 128), f32)
+        grad_v = jnp.zeros((count, 128), f32)
+        for h in range(2):
+            qh = keep_head(q, masks[h], 2).astype(bf16)
+            gh = keep_head(g, masks[h], 2).astype(bf16)
+            kh = keep_head(k, key_masks[h], 2).astype(bf16)
+            s = dot_nt(pairs_ref[0, :, cut], qh) - lse_ref[0, group, h : h + 1, :]
+            p = jnp.exp(jnp.where(valid, s, masked_score))
+            gp = dot_nt(pairs_ref[0, :, value_cut], gh)
+            gs = (p * (gp - delta[h : h + 1, :])).astype(bf16)
+            grad_v += dot_nn(p.astype(bf16), gh)
+            grad_k += dot_nn(gs, qh)
+            grad_q += dot_tn(gs, kh)
+        gq_ref[0, :, cut] = (grad_q * scale_factor).astype(bf16)
+        gpairs_ref[0, :, cut] = grad_k.astype(bf16)
+        gpairs_ref[0, :, value_cut] = grad_v.astype(bf16)
 
 
 def cross_backward(lengths, queries, pairs, out, lse, gout):
     micro, rows, width = queries.shape
     count = pairs.shape[1]
     groups = width // 128
-    row_spec = pl.BlockSpec((1, rows, 128), lambda m, g: (m, 0, g))
-    key_spec = pl.BlockSpec((1, count, 128), lambda m, g: (m, 0, g))
-    value_spec = pl.BlockSpec((1, count, 128), lambda m, g: (m, 0, g + groups))
-    lse_spec = pl.BlockSpec((1, 1, 2, rows), lambda m, g: (m, g, 0, 0))
+    row_spec = pl.BlockSpec((1, rows, width), lambda m: (m, 0, 0))
+    pair_spec = pl.BlockSpec((1, count, 2 * width), lambda m: (m, 0, 0))
     return pl.pallas_call(
         cross_backward_kernel,
-        grid=(micro, groups),
+        grid=(micro,),
         in_specs=[
             pl.BlockSpec(memory_space=pltpu.SMEM),
             row_spec,
-            key_spec,
-            value_spec,
+            pair_spec,
             row_spec,
-            lse_spec,
+            pl.BlockSpec((1, groups, 2, rows), lambda m: (m, 0, 0, 0)),
             row_spec,
         ],
-        out_specs=[row_spec, key_spec, key_spec],
+        out_specs=[row_spec, pair_spec],
         out_shape=[
             jax.ShapeDtypeStruct((micro, rows, width), bf16),
-            jax.ShapeDtypeStruct((micro, count, width), bf16),
-            jax.ShapeDtypeStruct((micro, count, width), bf16),
+            jax.ShapeDtypeStruct((micro, count, 2 * width), bf16),
         ],
         compiler_params=pltpu.CompilerParams(vmem_limit_bytes=32 << 20),
         name="cross_backward",
-    )(lengths, queries, pairs, pairs, out, lse, gout)
+    )(lengths, queries, pairs, out, lse, gout)
+
+
+def ffn_backward_kernel(
+    branch_ref, hidden_ref, active_ref, slope_ref, down_ref, up_ref,
+    grad_down_ref, grad_up_ref, grad_hidden_ref, hidden_t,
+):
+    @pl.when(pl.program_id(0) == 0)
+    def _():
+        hidden_t[...] = jnp.transpose(hidden_ref[...].astype(f32)).astype(bf16)
+        grad_hidden_ref[...] = jnp.zeros_like(grad_hidden_ref)
+
+    branch = branch_ref[...]
+    grad_active = dot_nt(branch, down_ref[...])
+    grad_inner = (slope_ref[...].astype(f32) * grad_active).astype(bf16)
+    grad_down_ref[...] = dot_tn(active_ref[...], branch).astype(bf16)
+    grad_up_ref[...] = dot_nn(hidden_t[...], grad_inner).astype(bf16)
+    grad_hidden_ref[...] += dot_nt(grad_inner, up_ref[...])
+
+
+def ffn_backward(branch, hidden, active, slope, down_weight, upward_weight):
+    rows, width = branch.shape
+    inner = active.shape[1]
+    piece = 512
+    whole = pl.BlockSpec((rows, width), lambda i: (0, 0))
+    across = pl.BlockSpec((rows, piece), lambda i: (0, i))
+    down = pl.BlockSpec((piece, width), lambda i: (i, 0))
+    up = pl.BlockSpec((width, piece), lambda i: (0, i))
+    return pl.pallas_call(
+        ffn_backward_kernel,
+        grid=(inner // piece,),
+        in_specs=[whole, whole, across, across, down, up],
+        out_specs=[down, up, whole],
+        out_shape=[
+            jax.ShapeDtypeStruct((inner, width), bf16),
+            jax.ShapeDtypeStruct((width, inner), bf16),
+            jax.ShapeDtypeStruct((rows, width), f32),
+        ],
+        scratch_shapes=[pltpu.VMEM((width, rows), bf16)],
+        compiler_params=pltpu.CompilerParams(vmem_limit_bytes=48 << 20),
+        name="ffn_backward",
+    )(branch, hidden, active, slope, down_weight, upward_weight)
 
 
 def gelu_parts(v):
@@ -1127,25 +1219,25 @@
     hidden_second = layer_norm(mixed_second, gain_rows[1], bias_rows[1])
     hidden_second_low = hidden_second.astype(bf16)
     pre_active = dot_nn(hidden_second_low, upward_weight)
-    active = gelu_parts(pre_active)[0].astype(bf16)
+    active, slope = gelu_parts(pre_active)
+    active, slope = lax.optimization_barrier((active.astype(bf16), slope.astype(bf16)))
     mixed_third = residual_weight * hidden_second + dot_nn(active, down_weight)
     output = layer_norm(mixed_third, gain_rows[2], bias_rows[2]).astype(bf16)
 
     upstream = cotangent.reshape(total_rows, width).astype(f32)
     grad_third, gain_third, bias_third = layer_norm_back(mixed_third, gain_rows[2], upstream)
     branch_third = grad_third.astype(bf16)
-    grad_down = dot_tn(active, branch_third).astype(bf16)
-    grad_inner = (gelu_parts(pre_active)[1] * dot_nt(branch_third, down_weight)).astype(bf16)
-    grad_upward = dot_tn(hidden_second_low, grad_inner).astype(bf16)
-
-    grad_hidden_second = residual_weight * grad_third + dot_nt(grad_inner, upward_weight)
+    grad_down, grad_upward, grad_hidden = ffn_backward(
+        branch_third, hidden_second_low, active, slope, down_weight, upward_weight
+    )
+    grad_hidden_second = residual_weight * grad_third + grad_hidden
     grad_second, gain_second, bias_second = layer_norm_back(
         mixed_second, gain_rows[1], grad_hidden_second
     )
     branch_second = grad_second.astype(bf16)
     grad_cross_output = dot_tn(cross_attended, branch_second).astype(bf16)
     grad_cross_attended = dot_nt(branch_second, cross_output).astype(bf16)
-    grad_cross_low, grad_keys, grad_values = cross_backward(
+    grad_cross_low, memory_partial = cross_backward(
         lengths,
         cross_query,
         pairs,
@@ -1153,8 +1245,10 @@
         cross_lse,
         grad_cross_attended.reshape(micro, row_count, width),
     )
-    memory_partial = jnp.concatenate([grad_keys, grad_values], 2)
-    own_pairs = lax.psum_scatter(memory_partial, "seq", scatter_dimension=1, tiled=True)
+    memory_partial = memory_partial.reshape(micro * count, 2 * width)
+    memory_share = dot_nt(memory_partial, pair_weight).astype(bf16)
+    memory_share = memory_share.reshape(micro, seq, memory_rows, width).transpose(1, 0, 2, 3)
+    grad_pair_weight = dot_tn(memory_full.reshape(micro * count, width), memory_partial)
     grad_cross_low = grad_cross_low.reshape(total_rows, width)
     grad_cross_weight = dot_tn(hidden_first_low, grad_cross_low).astype(bf16)
     grad_hidden_first = residual_weight * grad_second + dot_nt(grad_cross_low, cross_weight)
@@ -1164,23 +1258,20 @@
     branch_first = grad_first.astype(bf16)
     grad_self_output = dot_tn(attended, branch_first).astype(bf16)
     grad_attended = dot_nt(branch_first, self_output).astype(bf16)
-    grad_projected, own_upward, own_down = self_backward(
+    grad_projected, own_upward, own_down, grad_memory = self_backward(
         grad_attended.reshape(micro, row_count, width),
         qkv,
         bias,
         attended_heads,
         self_lse,
         seq,
-        [grad_upward, grad_down],
-        (True, False),
+        [grad_upward, grad_down, memory_share.reshape(seq * micro * memory_rows, width)],
+        (True, False, "seq"),
         y_size,
     )
     grad_projected = grad_projected.reshape(total_rows, 3 * width)
     grad_joint = dot_tn(x, grad_projected).astype(bf16)
     grad_tokens = (residual_weight * grad_first + dot_nt(grad_projected, joint_weight)).astype(bf16)
-    grad_pairs_low = own_pairs.reshape(micro * memory_rows, 2 * width)
-    grad_pair_weight = dot_tn(memory.reshape(micro * memory_rows, width), grad_pairs_low)
-    grad_memory = dot_nt(grad_pairs_low, pair_weight).astype(bf16)
     norm_grads = jnp.stack(
         [gain_first, gain_second, gain_third, bias_first, bias_second, bias_third]
     )
@@ -1202,7 +1293,7 @@
     return (
         output.reshape(tokens.shape),
         grad_tokens.reshape(tokens.shape),
-        grad_memory.reshape(memory.shape),
+        grad_memory.astype(bf16).reshape(memory.shape),
         owned[0],
         owned[1],
         owned[3],

time: 883 us -> 855 us (0.968)
  matrix products: 146 us -> 99 us
  Pallas kernels: 671 us -> 708 us
  between operations: 15.1 us -> 1.8 us
  local copies, waits for them, and re-layouts: 29.7 us -> 20.2 us
    dot_general x7 -> x5, matrix products: 51.8 us -> 22.4 us  [dot_nt(): lax.dot_general(a, b, (((1,), (1,)), ((), ())), preferred_element_type=f32)]
    dot_general x7 -> x5, matrix products: 47.5 us -> 26.8 us  [dot_tn(): lax.dot_general(a, b, (((0,), (0,)), ((), ())), preferred_element_type=f32)]
    pallas_call x2 -> x3, Pallas kernels: 42.3 us -> 61.8 us  [the longest x1 32.6 us: ffn_backward(): pl.pallas_call(ffn_backward_kernel, grid=(inner // piece,), in_specs=[who...]
    pallas_call x1, Pallas kernels: 96.7 us -> 109 us  [scatter_grads(): pl.pallas_call(functools.partial(scatter_kernel, kinds), in_specs=[pl.Blo...]
    unnamed x125 -> x133, local copies, waits for them, and re-layouts: 22.8 us -> 13.1 us
  transfers between devices with their start and end apart: 1 -> 0, of which waited for: 0 -> 0; matrix products, arithmetic and copies ran while one was open for 7% -> 0% of each run, Pallas kernels for 22% -> 0%
where the time goes in v6:
time: 855 us; the launch traced here: 851 us
  Pallas kernels  708 us (83%)
  matrix products  99 us (12%)
  other arithmetic  22.1 us (3%)
  local copies, waits for them, and re-layouts  20.2 us (2%)
    pallas_call x1, Pallas kernels, self_forward(): pl.pallas_call(functools.partial(self_forward_kernel, heads, BLOCK, plan,...  293 us
    pallas_call x1, Pallas kernels, self_backward(): pl.pallas_call(functools.partial(self_backward_kernel, heads, BLOCK, kind...  198 us
    pallas_call x1, Pallas kernels, scatter_grads(): pl.pallas_call(functools.partial(scatter_kernel, kinds), in_specs=[pl.Blo...  109 us
    dot_general x7, matrix products, dot_nn(): lax.dot_general(a, b, (((1,), (0,)), ((), ())), preferred_element_type=f32)  48.7 us
    pallas_call x1, Pallas kernels, gather_first(): pl.pallas_call(functools.partial(gather_kernel, plan, len(shards)), in_sp...  45.5 us
    pallas_call x1, Pallas kernels, ffn_backward(): pl.pallas_call(ffn_backward_kernel, grid=(inner // piece,), in_specs=[who...  32.6 us
    dot_general x5, matrix products, dot_tn(): lax.dot_general(a, b, (((0,), (0,)), ((), ())), preferred_element_type=f32)  26.8 us
    dot_general x5, matrix products, dot_nt(): lax.dot_general(a, b, (((1,), (1,)), ((), ())), preferred_element_type=f32)  22.4 us

profile of v6, /device:TPU:0, one launch (start us, length us, event | category | flops | bytes accessed | tf_op | source)
XLA Modules:
  0.0 850.9 jit_solution(12856885253045201146)
XLA Ops:
  0.6 45.5 %gather_first.1 = bf16[4,2,2,2,32,3072]{5,4,3,2,1,0:T(8,128)(2,1)} custom-call(bf16[32,3072]{1,0:T(8,128)(2,1)} %refs_0_.1), custom_call_target="tpu_custom_call" | custom-call | tf_op jit(solution)/shard_map/gather_first/pallas_call | solution.py:653
  46.3 9.1 %convolution_convert_fusion.1 = bf16[768,3072]{1,0:T(8,128)(2,1)} fusion(bf16[768,1024]{1,0:T(8,128)(2,1)} %bitcast.169, bf16[1024,3072]{1,0:T(8,128)(2,1)} %bitcast.138), kind=kOutput, calls=%fused_computation.13 | convolution fusion | flops 4834197504 | bytes 12582912 | tf_op jit(solution)/shard_map/dot_general | solution.py:30
  55.4 0.2 convolution_minimum_fusion.3
  55.7 0.2 convolution_minimum_fusion.2
  55.9 0.2 convolution_minimum_fusion.1
  56.0 0.2 convolution_minimum_fusion
  56.2 0.2 fusion.25
  56.4 0.2 fusion.18
  56.7 1.3 copy.32
  58.0 0.5 broadcast_in_dim.12
  58.5 0.5 reshape.249.refs_1_.refs_2_
  59.1 293.4 %self_forward.1 = (bf16[3,3,2048,128]{3,2,1,0:T(8,128)(2,1)}, bf16[3,1,2048,128]{3,2,1,0:T(8,128)(2,1)S(1)}, f32[3,8,2,256]{3,2,1,0:T(2,128)S(1)}, bf16[3,256,10...) custom-call(bf16[3,256,3072]{2,1,0:T(8,128)(2,1)} %bitcast.142, ...), custom_call_target="tpu_custom_call" | custom-call | tf_op jit(solution)/shard_map/self_forward/pallas_call | solution.py:794
  352.5 4.5 fusion.35
  357.0 0.4 multiply_reduce_fusion.6
  357.5 0.3 slice_reduce_fusion.1
  357.8 1.0 copy-done.27
  358.9 4.5 convolution_convert_fusion.10
  363.7 3.6 convolution_convert_fusion.3
  367.4 15.4 %cross_forward.1 = (bf16[3,256,1024]{2,1,0:T(8,128)(2,1)S(1)}, f32[3,8,2,256]{3,2,1,0:T(2,128)S(1)}) custom-call(s32[3]{0:T(128)S(1)} %bitcast.124, bf16[3,256,1024]{2,1,0:T(8,128)(2,1)S(1)} %bitcast.117, bf16[3,256,2048]{2,1,0:T(8,128)(2,1)S(1)} %bitcast.115), custom_call_target="tpu_custom_call" | custom-call | tf_op jit(solution)/shard_map/cross_forward/pallas_call | solution.py:1002
  382.8 2.1 fusion.36
  385.0 1.6 copy-done.22
  386.6 0.4 multiply_reduce_fusion.5
  387.2 2.6 fusion.17.hidden_ref
  389.9 17.7 %fusion.8 = (bf16[768,4096]{1,0:T(8,128)(2,1)}, bf16[768,4096]{1,0:T(8,128)(2,1)S(1)}) fusion(bf16[768,1024]{1,0:T(8,128)(2,1)S(1)} %fusion.17.hidden_ref, bf16[1024,4096]{1,0:T(8,128)(2,1)} %bitcast.132), kind=kOutput, calls=%fused_computation.10 | convolution fusion | flops 6502219776 | bytes 22544384 | tf_op jit(solution)/shard_map/dot_general | solution.py:30
  407.7 7.0 fusion.37
  414.7 1.6 copy-done.25
  416.4 0.4 multiply_reduce_fusion.4
  416.9 3.6 fusion.15
  420.5 0.8 convert_reduce_fusion
  421.3 3.4 fusion.33.branch_ref
  424.7 32.6 %ffn_backward.1 = (bf16[4096,1024]{1,0:T(8,128)(2,1)}, bf16[1024,4096]{1,0:T(8,128)(2,1)}, f32[768,1024]{1,0:T(8,128)}) custom-call(bf16[768,1024]{1,0:T(8,128)(2,1)S(1)} %fusion.33.branch_ref, bf16[768,1024]{1,0:T(8,128)(2,1)S(1)} %copy-done.1, bf16[768,4096]{1,0:T(8,128)(2,1)} %copy-done.31, bf16[768,4096]{1,0:T(8,128)(2,1)} %get-tuple-element.54.slope_ref, ...), custom_call_target="tpu_custom_call" | custom-call | tf_op jit(solution)/shard_map/ffn_backward/pallas_call | solution.py:1119
  457.4 7.4 multiply_reduce_fusion
  464.9 1.1 subtract_multiply_fusion.1
  465.9 0.5 copy-done.56
  466.4 1.8 convolution_convert_fusion.9
  468.3 0.7 copy-done.3
  469.0 0.5 copy-done.7
  469.5 13.7 %cross_backward.1 = (bf16[3,256,1024]{2,1,0:T(8,128)(2,1)S(1)}, bf16[3,256,2048]{2,1,0:T(8,128)(2,1)S(1)}) custom-call(s32[3]{0:T(128)S(1)} %bitcast.125, bf16[3,256,1024]{2,1,0:T(8,128)(2,1)S(1)} %bitcast.118, bf16[3,256,2048]{2,1,0:T(8,128)(2,1)S(1)} %bitcast.116, bf16[3,256,1024]{2,1,0:T(8,128)(2,1)S(1)} %copy-done.7, ...), custom_call_target="tpu_custom_call" | custom-call | tf_op jit(solution)/shard_map/cross_backward/pallas_call | solution.py:1073
  483.3 4.6 multiply_reduce_fusion.1
  488.4 0.8 stack.27
  489.2 5.2 convolution_convert_fusion.4
  494.4 3.6 convolution_convert_fusion.5
  498.0 5.1 convolution_convert_fusion.2
  503.2 1.2 subtract_multiply_fusion
  504.4 0.2 copy-done.59
  504.6 3.2 convolution_convert_fusion.6
  507.8 0.9 copy-done.52
  508.6 3.4 convolution_convert_fusion.7
  512.1 1.3 copy.34
  513.4 0.8 copy-done.53
  514.2 3.0 convolution_convert_fusion.8
  517.2 198.1 %self_backward.1 = (bf16[3,256,3072]{2,1,0:T(8,128)(2,1)}, f32[32,4096]{1,0:T(8,128)}, f32[128,1024]{1,0:T(8,128)}, f32[96,1024]{1,0:T(8,128)}) custom-call(bf16[3,256,1024]{2,1,0:T(8,128)(2,1)} %bitcast.148, bf16[3,3,2048,128]{3,2,1,0:T(8,128)(2,1)} %get-tuple-element.58.refs_1_, f32[3,8,8,2,256]{4,3,2,1,0:T(2,128)} %copy-done.4, ...), custom_call_target="tpu_custom_call" | custom-call | tf_op jit(solution)/shard_map/self_backward/pallas_call | solution.py:943
  715.3 9.6 %convolution_convert_fusion = bf16[3072,1024]{0,1:T(8,128)(2,1)} fusion(bf16[768,3072]{1,0:T(8,128)(2,1)} %bitcast.159, bf16[768,1024]{1,0:T(8,128)(2,1)S(1)} %bitcast.171), kind=kOutput, calls=%fused_computation.12 | convolution fusion | flops 4834983936 | bytes 12582912 | tf_op jit(solution)/shard_map/dot_general | solution.py:38
  725.0 109.0 %scatter_grads.1 = (f32[32,3072]{1,0:T(8,128)}, f32[32,1024]{1,0:T(8,128)}, f32[32,2048]{1,0:T(8,128)}, f32[32,1024]{1,0:T(8,128)}, f32[32,1024]{1,0:T(8,128)}, /*index=5*/f32[6,32]{1,0:T(8,128)}) custom-call(bf16[4,2,2,2,32,3072]{5,4,3,2,1,0:T(8,128)(2,1)} %bitcast.140, bf16[4,2,2,2,32,1024]{5,4,3,2,1,0:T(8,128)(2,1)} %bitcast.146, ...), custom_call_target="tpu_custom_call" | custom-call | tf_op jit(solution)/shard_map/scatter_grads/pallas_call | solution.py:469
  833.9 1.3 fusion.34
  835.3 9.6 %add_convert_fusion = bf16[768,1024]{1,0:T(8,128)(2,1)} fusion(f32[768,1024]{1,0:T(8,128)S(1)} %copy-done.33, bf16[768,3072]{1,0:T(8,128)(2,1)} %bitcast.160, bf16[1024,3072]{1,0:T(8,128)(2,1)} %bitcast.139), kind=kOutput, calls=%fused_computation.29 | convolution fusion | flops 4834197504 | bytes 15728640 | tf_op jit(solution)/shard_map/dot_general | solution.py:34
  844.9 0.7 convert_element_type.115
  845.6 0.7 copy.51
  846.4 0.7 copy.52
  847.0 0.7 copy.53
  847.7 0.7 copy.54
  848.4 0.7 copy.55
  849.0 0.8 copy.56
  849.8 0.8 copy.57
  (146 shorter events, 1.6 us)
Async XLA Ops:
  46.2 9.3 %copy-start.47 = (s32[3,1,16]{2,1,0:T(1,128)S(1)}, s32[3,1,16]{2,1,0:T(1,128)}, u32[]{:S(2)}) copy-start(s32[3,1,16]{2,1,0:T(1,128)} %param.18) | copy-start | bytes 580
  46.2 9.3 %copy-start.48 = (s32[3,1,13]{2,1,0:T(1,128)S(1)}, s32[3,1,13]{2,1,0:T(1,128)}, u32[]{:S(2)}) copy-start(s32[3,1,13]{2,1,0:T(1,128)} %param.19) | copy-start | bytes 472
  46.2 12.8 %copy-start.49 = (bf16[3,32]{1,0:T(4,128)(2,1)S(1)}, bf16[3,32]{1,0:T(4,128)(2,1)}, u32[]{:S(2)}) copy-start(bf16[3,32]{1,0:T(4,128)(2,1)} %param.29) | copy-start | bytes 580
  46.2 12.8 %copy-start.50 = (bf16[3,32]{1,0:T(4,128)(2,1)S(1)}, bf16[3,32]{1,0:T(4,128)(2,1)}, u32[]{:S(2)}) copy-start(bf16[3,32]{1,0:T(4,128)(2,1)} %param.28) | copy-start | bytes 580
  46.2 12.8 %copy-start.9 = (bf16[32,4096]{1,0:T(8,128)(2,1)S(1)}, bf16[32,4096]{1,0:T(8,128)(2,1)}, u32[]{:S(2)}) copy-start(bf16[32,4096]{1,0:T(8,128)(2,1)} %refs_8_.1) | copy-start | bytes 786436
  46.2 12.8 %copy-start.10 = (bf16[128,1024]{1,0:T(8,128)(2,1)S(1)}, bf16[128,1024]{1,0:T(8,128)(2,1)}, u32[]{:S(2)}) copy-start(bf16[128,1024]{1,0:T(8,128)(2,1)} %refs_9_.1) | copy-start | bytes 786436
  46.2 12.8 %copy-start.11 = (bf16[3,1,32,1024]{3,2,1,0:T(8,128)(2,1)S(1)}, bf16[3,1,32,1024]{3,2,1,0:T(8,128)(2,1)}, u32[]{:S(2)}) copy-start(bf16[3,1,32,1024]{3,2,1,0:T(8,128)(2,1)} %param.16) | copy-start | bytes 589828
  46.2 12.8 %copy-start.12 = (bf16[32,2048]{1,0:T(8,128)(2,1)S(1)}, bf16[32,2048]{1,0:T(8,128)(2,1)}, u32[]{:S(2)}) copy-start(bf16[32,2048]{1,0:T(8,128)(2,1)} %refs_5_.1) | copy-start | bytes 393220
  46.3 12.8 %copy-start.13 = (bf16[32,1024]{1,0:T(8,128)(2,1)S(1)}, bf16[32,1024]{1,0:T(8,128)(2,1)}, u32[]{:S(2)}) copy-start(bf16[32,1024]{1,0:T(8,128)(2,1)} %refs_2_.1) | copy-start | bytes 196612
  46.3 12.8 %copy-start.14 = (bf16[32,1024]{1,0:T(8,128)(2,1)S(1)}, bf16[32,1024]{1,0:T(8,128)(2,1)}, u32[]{:S(2)}) copy-start(bf16[32,1024]{1,0:T(8,128)(2,1)} %refs_4_.1) | copy-start | bytes 196612
  46.3 12.8 %copy-start.15 = (bf16[32,1024]{1,0:T(8,128)(2,1)S(1)}, bf16[32,1024]{1,0:T(8,128)(2,1)}, u32[]{:S(2)}) copy-start(bf16[32,1024]{1,0:T(8,128)(2,1)} %refs_7_.1) | copy-start | bytes 196612
  59.0 298.0 %copy-start.4 = (f32[3,8,8,2,256]{4,3,2,1,0:T(2,128)}, f32[3,8,8,2,256]{4,3,2,1,0:T(2,128)S(1)}, u32[]{:S(2)}) copy-start(f32[3,8,8,2,256]{4,3,2,1,0:T(2,128)S(1)} %reshape.249.refs_1_.refs_2_) | copy-start | bytes 1179652
  59.0 293.5 %copy-start.57 = (bf16[3,1,256,1024]{3,2,1,0:T(8,128)(2,1)S(1)}, bf16[3,1,256,1024]{3,2,1,0:T(8,128)(2,1)}, u32[]{:S(2)}) copy-start(bf16[3,1,256,1024]{3,2,1,0:T(8,128)(2,1)} %param.15) | copy-start | bytes 4718596
  352.4 4.6 copy-start.5
  352.4 4.6 copy-start.16
  357.0 1.7 copy-start.27
  358.9 4.5 copy-start.38
  358.9 4.7 copy-start.51
  363.4 3.9 copy-start.2
  363.6 3.7 copy-start.36
  363.6 3.7 copy-start.17
  363.7 19.1 %copy-start.55 = (bf16[4,2,2,2,32,1024]{5,4,3,2,1,0:T(8,128)(2,1)S(1)}, bf16[4,2,2,2,32,1024]{5,4,3,2,1,0:T(8,128)(2,1)}, u32[]{:S(2)}) copy-start(bf16[4,2,2,2,32,1024]{5,4,3,2,1,0:T(8,128)(2,1)} %get-tuple-element.50) | copy-start | bytes 6291460
  367.3 15.5 %copy-start.28 = (f32[768,1024]{1,0:T(8,128)S(1)}, f32[768,1024]{1,0:T(8,128)}, u32[]{:S(2)}) copy-start(f32[768,1024]{1,0:T(8,128)} %copy-done.27) | copy-start | bytes 9437188
  382.8 2.2 copy-start.6
  385.0 1.7 copy-start.22
  387.2 20.4 %slice-start = ((s8[8388608]{0:T(1024)(128)(4,1)}), s8[4194304]{0:T(1024)(128)(4,1)S(1)}, s32[]{:S(2)}) async-start(s8[8388608]{0:T(1024)(128)(4,1)} %bitcast.135), calls=%async_computation | async-start | bytes 8388608
  389.8 17.8 %copy-start = (bf16[768,1024]{1,0:T(8,128)(2,1)}, bf16[768,1024]{1,0:T(8,128)(2,1)S(1)}, u32[]{:S(2)}) copy-start(bf16[768,1024]{1,0:T(8,128)(2,1)S(1)} %fusion.17.hidden_ref) | copy-start | bytes 4718596
  389.8 17.8 %copy-start.23 = (f32[768,1024]{1,0:T(8,128)S(1)}, f32[768,1024]{1,0:T(8,128)}, u32[]{:S(2)}) copy-start(f32[768,1024]{1,0:T(8,128)} %copy-done.22) | copy-start | bytes 9437188
  389.9 17.8 %slice-start.1 = ((s8[8388608]{0:T(1024)(128)(4,1)}), s8[4194304]{0:T(1024)(128)(4,1)S(1)}, s32[]{:S(2)}) async-start(s8[8388608]{0:T(1024)(128)(4,1)} %bitcast.135), calls=%async_computation.1 | async-start | bytes 8388608
  407.6 7.1 copy-start.31
  414.7 1.6 copy-start.25
  416.9 3.6 copy-start.26
  421.3 3.4 copy-start.1
  457.4 7.4 copy-start.24
  464.8 1.6 copy-start.56
  466.4 16.8 %copy-start.34 = (f32[768,1024]{1,0:T(8,128)}, f32[768,1024]{1,0:T(8,128)S(1)}, u32[]{:S(2)}) copy-start(f32[768,1024]{1,0:T(8,128)S(1)} %subtract_multiply_fusion.1) | copy-start | bytes 9437188
  466.4 2.5 copy-start.3
  466.4 3.0 copy-start.7
  469.5 13.8 %copy-start.29 = (f32[768,1024]{1,0:T(8,128)S(1)}, f32[768,1024]{1,0:T(8,128)}, u32[]{:S(2)}) copy-start(f32[768,1024]{1,0:T(8,128)} %copy-done.27) | copy-start | bytes 9437188
  469.5 13.8 %copy-start.54 = (bf16[4,2,2,2,32,1024]{5,4,3,2,1,0:T(8,128)(2,1)S(1)}, bf16[4,2,2,2,32,1024]{5,4,3,2,1,0:T(8,128)(2,1)}, u32[]{:S(2)}) copy-start(bf16[4,2,2,2,32,1024]{5,4,3,2,1,0:T(8,128)(2,1)} %get-tuple-element.46) | copy-start | bytes 6291460
  483.2 4.6 copy-start.18
  483.2 4.6 copy-start.20
  483.3 5.9 copy-start.8
  489.2 5.2 copy-start.21
  489.2 5.2 copy-start.30
  494.4 3.6 copy-start.19
  494.4 3.6 copy-start.37
  498.0 5.2 copy-start.35
  503.1 1.4 copy-start.59
  504.6 8.8 %copy-start.32 = (f32[768,1024]{1,0:T(8,128)}, f32[768,1024]{1,0:T(8,128)S(1)}, u32[]{:S(2)}) copy-start(f32[768,1024]{1,0:T(8,128)S(1)} %subtract_multiply_fusion) | copy-start | bytes 9437188
  504.6 4.1 copy-start.52
  512.1 2.2 copy-start.53
  517.2 198.1 %copy-start.58 = (bf16[3,1,256,1024]{3,2,1,0:T(8,128)(2,1)S(1)}, bf16[3,1,256,1024]{3,2,1,0:T(8,128)(2,1)}, u32[]{:S(2)}) copy-start(bf16[3,1,256,1024]{3,2,1,0:T(8,128)(2,1)} %param.15) | copy-start | bytes 4718596
  725.0 110.3 %copy-start.33 = (f32[768,1024]{1,0:T(8,128)S(1)}, f32[768,1024]{1,0:T(8,128)}, u32[]{:S(2)}) copy-start(f32[768,1024]{1,0:T(8,128)} %copy-done.32) | copy-start | bytes 9437188
  835.3 9.6 %copy-start.41 = (f32[96,1024]{1,0:T(8,128)S(1)}, f32[96,1024]{1,0:T(8,128)}, u32[]{:S(2)}) copy-start(f32[96,1024]{1,0:T(8,128)} %get-tuple-element.65) | copy-start | bytes 1179652
  835.3 10.3 %copy-start.42 = (f32[32,3072]{1,0:T(8,128)S(1)}, f32[32,3072]{1,0:T(8,128)}, u32[]{:S(2)}) copy-start(f32[32,3072]{1,0:T(8,128)} %get-tuple-element.146) | copy-start | bytes 1179652
  835.3 11.1 %copy-start.46 = (f32[32,1024]{1,0:T(8,128)S(1)}, f32[32,1024]{1,0:T(8,128)}, u32[]{:S(2)}) copy-start(f32[32,1024]{1,0:T(8,128)} %get-tuple-element.147) | copy-start | bytes 393220
  835.3 11.7 %copy-start.45 = (f32[32,1024]{1,0:T(8,128)S(1)}, f32[32,1024]{1,0:T(8,128)}, u32[]{:S(2)}) copy-start(f32[32,1024]{1,0:T(8,128)} %get-tuple-element.148) | copy-start | bytes 393220
  835.3 12.4 %copy-start.43 = (f32[32,2048]{1,0:T(8,128)S(1)}, f32[32,2048]{1,0:T(8,128)}, u32[]{:S(2)}) copy-start(f32[32,2048]{1,0:T(8,128)} %get-tuple-element.149) | copy-start | bytes 786436
  835.3 13.1 %copy-start.44 = (f32[32,1024]{1,0:T(8,128)S(1)}, f32[32,1024]{1,0:T(8,128)}, u32[]{:S(2)}) copy-start(f32[32,1024]{1,0:T(8,128)} %get-tuple-element.150) | copy-start | bytes 393220
  835.3 13.7 %copy-start.40 = (f32[32,4096]{1,0:T(8,128)S(1)}, f32[32,4096]{1,0:T(8,128)}, u32[]{:S(2)}) copy-start(f32[32,4096]{1,0:T(8,128)} %get-tuple-element.151) | copy-start | bytes 1572868
  844.9 4.9 copy-start.39

commit v7 on v6

--- a/solution.py
+++ b/solution.py
@@ -11,10 +11,11 @@
 HD = 64
 TILE = 128
 BLOCK = 256
+FIRST_SPLIT = 3
 WINDOW = 4
-GATHER_END = 75
+GATHER_END = 85
 SPLIT_ELEMENTS = 96 << 10
-SCATTER_END = 75
+SCATTER_END = 95
 
 scale_factor = 0.125
 residual_weight = 36.0**0.25
@@ -495,14 +496,14 @@
     return peers + [{"fsdp": 2 * lax.rem(y + k, y_size) + c} for k in range(1, y_size)]
 
 
-def gather_parts(shards, kinds, groups):
+def gather_parts(shards, kinds, groups, most=2):
     parts, units = [], []
     for group in groups:
         pieces = []
         for a in group:
             rows, columns = shards[a].shape
             kind = kinds[a]
-            split = 2 if rows % 32 == 0 and rows * columns >= SPLIT_ELEMENTS else 1
+            split = most if rows % 32 == 0 and rows * columns >= SPLIT_ELEMENTS else 1
             for n in range(split):
                 cut = (n * columns // split, columns // split)
                 if kind == "seq" or rows % 32:
@@ -649,7 +650,7 @@
 
 
 def gather_first(shards, kinds, groups, z_size, y_size, collective_id):
-    plan = gather_parts(shards, kinds, groups)
+    plan = gather_parts(shards, kinds, groups, FIRST_SPLIT)
     return pl.pallas_call(
         functools.partial(gather_kernel, plan, len(shards)),
         in_specs=[pl.BlockSpec(memory_space=pl.ANY)] * len(shards),
@@ -720,38 +721,44 @@
 
         lax.fori_loop(0, blocks, prepare, 0)
 
-        def scores_of(i, j, h):
-            raw = dot_nt(qkv_ref[m, 1, rows_at(j, block), :], queries[h, rows_at(i, block), :])
-            bias = bias_ref[m, j, i]
-            return (raw.reshape(per, TILE, block) + bias[:, None, :]).reshape(block, block)
+        def scores_of(i, j, count, h):
+            keys = pl.ds(pl.multiple_of(j * block, block), count * block)
+            raw = dot_nt(qkv_ref[m, 1, keys, :], queries[h, rows_at(i, block), :])
+            bias = jnp.concatenate([bias_ref[m, j + k, i] for k in range(count)], 0)
+            raw = raw.reshape(count * per, TILE, block) + bias[:, None, :]
+            return raw.reshape(count * block, block)
+
+        def values_by(j, count, h, p):
+            p = p.astype(bf16)
+            return sum(
+                dot_nn(values_t[j + k][h * HD : (h + 1) * HD], p[k * block : (k + 1) * block])
+                for k in range(count)
+            )
 
         def query_block(i, carry):
             run_slot(placed, m * per_micro + seq - 1 + i)
             state = []
             for h in range(heads):
-                s = jnp.where(causal, scores_of(i, i, h), masked_score)
+                s = jnp.where(causal, scores_of(i, i, 1, h), masked_score)
                 top = jnp.max(s, 0, keepdims=True)
                 p = jnp.exp(s - top)
-                total = jnp.sum(p, 0, keepdims=True)
-                acc = dot_nn(values_t[i][h * HD : (h + 1) * HD], p.astype(bf16))
-                state += [top, total, acc]
-
-            def key_block(j, state):
+                state += [top, jnp.sum(p, 0, keepdims=True), values_by(i, 1, h, p)]
+
+            def key_blocks(j, count, state):
                 fresh = []
                 for h in range(heads):
                     top, total, acc = state[3 * h : 3 * h + 3]
-                    s = scores_of(i, j, h)
+                    s = scores_of(i, j, count, h)
                     higher = jnp.maximum(top, jnp.max(s, 0, keepdims=True))
                     shrink = jnp.exp(top - higher)
                     p = jnp.exp(s - higher)
                     total = total * shrink + jnp.sum(p, 0, keepdims=True)
-                    acc = acc * shrink + dot_nn(
-                        values_t[j][h * HD : (h + 1) * HD], p.astype(bf16)
-                    )
-                    fresh += [higher, total, acc]
+                    fresh += [higher, total, acc * shrink + values_by(j, count, h, p)]
                 return tuple(fresh)
 
-            state = lax.fori_loop(0, i, key_block, tuple(state))
+            pairs = i // 2
+            state = lax.fori_loop(0, pairs, lambda j, s: key_blocks(2 * j, 2, s), tuple(state))
+            state = lax.fori_loop(2 * pairs, i, lambda j, s: key_blocks(j, 1, s), state)
             out = jnp.concatenate(
                 [state[3 * h + 2] * (1.0 / state[3 * h + 1]) for h in range(heads)], 0
             )

time: 855 us -> 849 us (level)
  no operation moved by 1% of the time
where the time goes in v7:
time: 849 us; the launch traced here: 844 us
  Pallas kernels  701 us (83%)
  matrix products  99 us (12%)
  other arithmetic  22.1 us (3%)
  local copies, waits for them, and re-layouts  20.2 us (2%)
    pallas_call x1, Pallas kernels, self_forward(): pl.pallas_call(functools.partial(self_forward_kernel, heads, BLOCK, plan,...  288 us
    pallas_call x1, Pallas kernels, self_backward(): pl.pallas_call(functools.partial(self_backward_kernel, heads, BLOCK, kind...  191 us
    pallas_call x1, Pallas kernels, scatter_grads(): pl.pallas_call(functools.partial(scatter_kernel, kinds), in_specs=[pl.Blo...  116 us
    dot_general x7, matrix products, dot_nn(): lax.dot_general(a, b, (((1,), (0,)), ((), ())), preferred_element_type=f32)  48.7 us
    pallas_call x1, Pallas kernels, gather_first(): pl.pallas_call(functools.partial(gather_kernel, plan, len(shards)), in_sp...  44.6 us
    pallas_call x1, Pallas kernels, ffn_backward(): pl.pallas_call(ffn_backward_kernel, grid=(inner // piece,), in_specs=[who...  32.6 us
    dot_general x5, matrix products, dot_tn(): lax.dot_general(a, b, (((0,), (0,)), ((), ())), preferred_element_type=f32)  26.8 us
    dot_general x5, matrix products, dot_nt(): lax.dot_general(a, b, (((1,), (1,)), ((), ())), preferred_element_type=f32)  22.4 us

profile of v7, /device:TPU:0, one launch (start us, length us, event | category | flops | bytes accessed | tf_op | source)
XLA Modules:
  0.0 844.4 jit_solution(10380050147490470937)
XLA Ops:
  0.6 44.6 %gather_first.1 = bf16[4,2,2,2,32,3072]{5,4,3,2,1,0:T(8,128)(2,1)} custom-call(bf16[32,3072]{1,0:T(8,128)(2,1)} %refs_0_.1), custom_call_target="tpu_custom_call" | custom-call | tf_op jit(solution)/shard_map/gather_first/pallas_call | solution.py:654
  45.4 9.1 %convolution_convert_fusion.1 = bf16[768,3072]{1,0:T(8,128)(2,1)} fusion(bf16[768,1024]{1,0:T(8,128)(2,1)} %bitcast.169, bf16[1024,3072]{1,0:T(8,128)(2,1)} %bitcast.138), kind=kOutput, calls=%fused_computation.13 | convolution fusion | flops 4834197504 | bytes 12582912 | tf_op jit(solution)/shard_map/dot_general | solution.py:31
  54.6 0.2 convolution_minimum_fusion.3
  54.8 0.2 convolution_minimum_fusion.2
  55.0 0.2 convolution_minimum_fusion.1
  55.1 0.2 convolution_minimum_fusion
  55.3 0.2 fusion.25
  55.5 0.2 fusion.18
  55.8 1.3 copy.32
  57.1 0.5 broadcast_in_dim.12
  57.6 0.5 reshape.249.refs_1_.refs_2_
  58.2 288.3 %self_forward.1 = (bf16[3,3,2048,128]{3,2,1,0:T(8,128)(2,1)}, bf16[3,1,2048,128]{3,2,1,0:T(8,128)(2,1)S(1)}, f32[3,8,2,256]{3,2,1,0:T(2,128)S(1)}, bf16[3,256,10...) custom-call(bf16[3,256,3072]{2,1,0:T(8,128)(2,1)} %bitcast.142, ...), custom_call_target="tpu_custom_call" | custom-call | tf_op jit(solution)/shard_map/self_forward/pallas_call | solution.py:801
  346.6 4.5 fusion.35
  351.2 0.4 multiply_reduce_fusion.6
  351.6 0.3 slice_reduce_fusion.1
  351.9 1.0 copy-done.27
  353.0 4.5 convolution_convert_fusion.10
  357.8 3.6 convolution_convert_fusion.3
  361.5 15.4 %cross_forward.1 = (bf16[3,256,1024]{2,1,0:T(8,128)(2,1)S(1)}, f32[3,8,2,256]{3,2,1,0:T(2,128)S(1)}) custom-call(s32[3]{0:T(128)S(1)} %bitcast.124, bf16[3,256,1024]{2,1,0:T(8,128)(2,1)S(1)} %bitcast.117, bf16[3,256,2048]{2,1,0:T(8,128)(2,1)S(1)} %bitcast.115), custom_call_target="tpu_custom_call" | custom-call | tf_op jit(solution)/shard_map/cross_forward/pallas_call | solution.py:1009
  376.9 2.1 fusion.36
  379.1 1.6 copy-done.22
  380.7 0.4 multiply_reduce_fusion.5
  381.3 2.6 fusion.17.hidden_ref
  384.0 17.7 %fusion.8 = (bf16[768,4096]{1,0:T(8,128)(2,1)}, bf16[768,4096]{1,0:T(8,128)(2,1)S(1)}) fusion(bf16[768,1024]{1,0:T(8,128)(2,1)S(1)} %fusion.17.hidden_ref, bf16[1024,4096]{1,0:T(8,128)(2,1)} %bitcast.132), kind=kOutput, calls=%fused_computation.10 | convolution fusion | flops 6502219776 | bytes 22544384 | tf_op jit(solution)/shard_map/dot_general | solution.py:31
  401.8 7.0 fusion.37
  408.9 1.6 copy-done.25
  410.5 0.4 multiply_reduce_fusion.4
  411.0 3.6 fusion.15
  414.6 0.8 convert_reduce_fusion
  415.4 3.4 fusion.33.branch_ref
  418.8 32.6 %ffn_backward.1 = (bf16[4096,1024]{1,0:T(8,128)(2,1)}, bf16[1024,4096]{1,0:T(8,128)(2,1)}, f32[768,1024]{1,0:T(8,128)}) custom-call(bf16[768,1024]{1,0:T(8,128)(2,1)S(1)} %fusion.33.branch_ref, bf16[768,1024]{1,0:T(8,128)(2,1)S(1)} %copy-done.1, bf16[768,4096]{1,0:T(8,128)(2,1)} %copy-done.31, bf16[768,4096]{1,0:T(8,128)(2,1)} %get-tuple-element.54.slope_ref, ...), custom_call_target="tpu_custom_call" | custom-call | tf_op jit(solution)/shard_map/ffn_backward/pallas_call | solution.py:1126
  451.5 7.4 multiply_reduce_fusion
  459.0 1.1 subtract_multiply_fusion.1
  460.0 0.5 copy-done.56
  460.6 1.8 convolution_convert_fusion.9
  462.4 0.7 copy-done.3
  463.1 0.5 copy-done.7
  463.6 13.7 %cross_backward.1 = (bf16[3,256,1024]{2,1,0:T(8,128)(2,1)S(1)}, bf16[3,256,2048]{2,1,0:T(8,128)(2,1)S(1)}) custom-call(s32[3]{0:T(128)S(1)} %bitcast.125, bf16[3,256,1024]{2,1,0:T(8,128)(2,1)S(1)} %bitcast.118, bf16[3,256,2048]{2,1,0:T(8,128)(2,1)S(1)} %bitcast.116, bf16[3,256,1024]{2,1,0:T(8,128)(2,1)S(1)} %copy-done.7, ...), custom_call_target="tpu_custom_call" | custom-call | tf_op jit(solution)/shard_map/cross_backward/pallas_call | solution.py:1080
  477.4 4.6 multiply_reduce_fusion.1
  482.5 0.8 stack.27
  483.3 5.2 convolution_convert_fusion.4
  488.5 3.6 convolution_convert_fusion.5
  492.1 5.1 convolution_convert_fusion.2
  497.3 1.2 subtract_multiply_fusion
  498.5 0.2 copy-done.59
  498.7 3.2 convolution_convert_fusion.6
  501.9 0.9 copy-done.52
  502.8 3.4 convolution_convert_fusion.7
  506.2 1.3 copy.34
  507.5 0.8 copy-done.53
  508.4 3.0 convolution_convert_fusion.8
  511.3 190.5 %self_backward.1 = (bf16[3,256,3072]{2,1,0:T(8,128)(2,1)}, f32[32,4096]{1,0:T(8,128)}, f32[128,1024]{1,0:T(8,128)}, f32[96,1024]{1,0:T(8,128)}) custom-call(bf16[3,256,1024]{2,1,0:T(8,128)(2,1)} %bitcast.148, bf16[3,3,2048,128]{3,2,1,0:T(8,128)(2,1)} %get-tuple-element.58.refs_1_, f32[3,8,8,2,256]{4,3,2,1,0:T(2,128)} %copy-done.4, ...), custom_call_target="tpu_custom_call" | custom-call | tf_op jit(solution)/shard_map/self_backward/pallas_call | solution.py:950
  701.9 9.6 %convolution_convert_fusion = bf16[3072,1024]{0,1:T(8,128)(2,1)} fusion(bf16[768,3072]{1,0:T(8,128)(2,1)} %bitcast.159, bf16[768,1024]{1,0:T(8,128)(2,1)S(1)} %bitcast.171), kind=kOutput, calls=%fused_computation.12 | convolution fusion | flops 4834983936 | bytes 12582912 | tf_op jit(solution)/shard_map/dot_general | solution.py:39
  711.5 115.9 %scatter_grads.1 = (f32[32,3072]{1,0:T(8,128)}, f32[32,1024]{1,0:T(8,128)}, f32[32,2048]{1,0:T(8,128)}, f32[32,1024]{1,0:T(8,128)}, f32[32,1024]{1,0:T(8,128)}, /*index=5*/f32[6,32]{1,0:T(8,128)}) custom-call(bf16[4,2,2,2,32,3072]{5,4,3,2,1,0:T(8,128)(2,1)} %bitcast.140, bf16[4,2,2,2,32,1024]{5,4,3,2,1,0:T(8,128)(2,1)} %bitcast.146, ...), custom_call_target="tpu_custom_call" | custom-call | tf_op jit(solution)/shard_map/scatter_grads/pallas_call | solution.py:470
  827.5 1.3 fusion.34
  828.9 9.6 %add_convert_fusion = bf16[768,1024]{1,0:T(8,128)(2,1)} fusion(f32[768,1024]{1,0:T(8,128)S(1)} %copy-done.33, bf16[768,3072]{1,0:T(8,128)(2,1)} %bitcast.160, bf16[1024,3072]{1,0:T(8,128)(2,1)} %bitcast.139), kind=kOutput, calls=%fused_computation.29 | convolution fusion | flops 4834197504 | bytes 15728640 | tf_op jit(solution)/shard_map/dot_general | solution.py:35
  838.4 0.7 convert_element_type.115
  839.1 0.7 copy.51
  839.9 0.7 copy.52
  840.6 0.7 copy.53
  841.2 0.7 copy.54
  841.9 0.7 copy.55
  842.6 0.8 copy.56
  843.4 0.8 copy.57
  (146 shorter events, 1.6 us)
Async XLA Ops:
  45.3 9.2 %copy-start.47 = (s32[3,1,16]{2,1,0:T(1,128)S(1)}, s32[3,1,16]{2,1,0:T(1,128)}, u32[]{:S(2)}) copy-start(s32[3,1,16]{2,1,0:T(1,128)} %param.18) | copy-start | bytes 580
  45.3 9.2 %copy-start.48 = (s32[3,1,13]{2,1,0:T(1,128)S(1)}, s32[3,1,13]{2,1,0:T(1,128)}, u32[]{:S(2)}) copy-start(s32[3,1,13]{2,1,0:T(1,128)} %param.19) | copy-start | bytes 472
  45.3 12.8 %copy-start.49 = (bf16[3,32]{1,0:T(4,128)(2,1)S(1)}, bf16[3,32]{1,0:T(4,128)(2,1)}, u32[]{:S(2)}) copy-start(bf16[3,32]{1,0:T(4,128)(2,1)} %param.29) | copy-start | bytes 580
  45.3 12.8 %copy-start.50 = (bf16[3,32]{1,0:T(4,128)(2,1)S(1)}, bf16[3,32]{1,0:T(4,128)(2,1)}, u32[]{:S(2)}) copy-start(bf16[3,32]{1,0:T(4,128)(2,1)} %param.28) | copy-start | bytes 580
  45.3 12.8 %copy-start.9 = (bf16[32,4096]{1,0:T(8,128)(2,1)S(1)}, bf16[32,4096]{1,0:T(8,128)(2,1)}, u32[]{:S(2)}) copy-start(bf16[32,4096]{1,0:T(8,128)(2,1)} %refs_8_.1) | copy-start | bytes 786436
  45.3 12.8 %copy-start.10 = (bf16[128,1024]{1,0:T(8,128)(2,1)S(1)}, bf16[128,1024]{1,0:T(8,128)(2,1)}, u32[]{:S(2)}) copy-start(bf16[128,1024]{1,0:T(8,128)(2,1)} %refs_9_.1) | copy-start | bytes 786436
  45.4 12.8 %copy-start.11 = (bf16[3,1,32,1024]{3,2,1,0:T(8,128)(2,1)S(1)}, bf16[3,1,32,1024]{3,2,1,0:T(8,128)(2,1)}, u32[]{:S(2)}) copy-start(bf16[3,1,32,1024]{3,2,1,0:T(8,128)(2,1)} %param.16) | copy-start | bytes 589828
  45.4 12.8 %copy-start.12 = (bf16[32,2048]{1,0:T(8,128)(2,1)S(1)}, bf16[32,2048]{1,0:T(8,128)(2,1)}, u32[]{:S(2)}) copy-start(bf16[32,2048]{1,0:T(8,128)(2,1)} %refs_5_.1) | copy-start | bytes 393220
  45.4 12.8 %copy-start.13 = (bf16[32,1024]{1,0:T(8,128)(2,1)S(1)}, bf16[32,1024]{1,0:T(8,128)(2,1)}, u32[]{:S(2)}) copy-start(bf16[32,1024]{1,0:T(8,128)(2,1)} %refs_2_.1) | copy-start | bytes 196612
  45.4 12.8 %copy-start.14 = (bf16[32,1024]{1,0:T(8,128)(2,1)S(1)}, bf16[32,1024]{1,0:T(8,128)(2,1)}, u32[]{:S(2)}) copy-start(bf16[32,1024]{1,0:T(8,128)(2,1)} %refs_4_.1) | copy-start | bytes 196612
  45.4 12.8 %copy-start.15 = (bf16[32,1024]{1,0:T(8,128)(2,1)S(1)}, bf16[32,1024]{1,0:T(8,128)(2,1)}, u32[]{:S(2)}) copy-start(bf16[32,1024]{1,0:T(8,128)(2,1)} %refs_7_.1) | copy-start | bytes 196612
  58.1 293.0 %copy-start.4 = (f32[3,8,8,2,256]{4,3,2,1,0:T(2,128)}, f32[3,8,8,2,256]{4,3,2,1,0:T(2,128)S(1)}, u32[]{:S(2)}) copy-start(f32[3,8,8,2,256]{4,3,2,1,0:T(2,128)S(1)} %reshape.249.refs_1_.refs_2_) | copy-start | bytes 1179652
  58.1 288.5 %copy-start.57 = (bf16[3,1,256,1024]{3,2,1,0:T(8,128)(2,1)S(1)}, bf16[3,1,256,1024]{3,2,1,0:T(8,128)(2,1)}, u32[]{:S(2)}) copy-start(bf16[3,1,256,1024]{3,2,1,0:T(8,128)(2,1)} %param.15) | copy-start | bytes 4718596
  346.5 4.6 copy-start.5
  346.6 4.6 copy-start.16
  351.1 1.7 copy-start.27
  353.0 4.6 copy-start.38
  353.0 4.7 copy-start.51
  357.6 3.9 copy-start.2
  357.7 3.7 copy-start.36
  357.8 3.7 copy-start.17
  357.8 19.1 %copy-start.55 = (bf16[4,2,2,2,32,1024]{5,4,3,2,1,0:T(8,128)(2,1)S(1)}, bf16[4,2,2,2,32,1024]{5,4,3,2,1,0:T(8,128)(2,1)}, u32[]{:S(2)}) copy-start(bf16[4,2,2,2,32,1024]{5,4,3,2,1,0:T(8,128)(2,1)} %get-tuple-element.50) | copy-start | bytes 6291460
  361.4 15.5 %copy-start.28 = (f32[768,1024]{1,0:T(8,128)S(1)}, f32[768,1024]{1,0:T(8,128)}, u32[]{:S(2)}) copy-start(f32[768,1024]{1,0:T(8,128)} %copy-done.27) | copy-start | bytes 9437188
  376.9 2.2 copy-start.6
  379.1 1.7 copy-start.22
  381.3 20.4 %slice-start = ((s8[8388608]{0:T(1024)(128)(4,1)}), s8[4194304]{0:T(1024)(128)(4,1)S(1)}, s32[]{:S(2)}) async-start(s8[8388608]{0:T(1024)(128)(4,1)} %bitcast.135), calls=%async_computation | async-start | bytes 8388608
  383.9 17.8 %copy-start = (bf16[768,1024]{1,0:T(8,128)(2,1)}, bf16[768,1024]{1,0:T(8,128)(2,1)S(1)}, u32[]{:S(2)}) copy-start(bf16[768,1024]{1,0:T(8,128)(2,1)S(1)} %fusion.17.hidden_ref) | copy-start | bytes 4718596
  384.0 17.8 %copy-start.23 = (f32[768,1024]{1,0:T(8,128)S(1)}, f32[768,1024]{1,0:T(8,128)}, u32[]{:S(2)}) copy-start(f32[768,1024]{1,0:T(8,128)} %copy-done.22) | copy-start | bytes 9437188
  384.0 17.8 %slice-start.1 = ((s8[8388608]{0:T(1024)(128)(4,1)}), s8[4194304]{0:T(1024)(128)(4,1)S(1)}, s32[]{:S(2)}) async-start(s8[8388608]{0:T(1024)(128)(4,1)} %bitcast.135), calls=%async_computation.1 | async-start | bytes 8388608
  401.7 7.1 copy-start.31
  408.8 1.6 copy-start.25
  411.0 3.6 copy-start.26
  415.4 3.4 copy-start.1
  451.5 7.4 copy-start.24
  459.0 1.6 copy-start.56
  460.5 16.8 %copy-start.34 = (f32[768,1024]{1,0:T(8,128)}, f32[768,1024]{1,0:T(8,128)S(1)}, u32[]{:S(2)}) copy-start(f32[768,1024]{1,0:T(8,128)S(1)} %subtract_multiply_fusion.1) | copy-start | bytes 9437188
  460.6 2.5 copy-start.3
  460.6 3.0 copy-start.7
  463.6 13.8 %copy-start.29 = (f32[768,1024]{1,0:T(8,128)S(1)}, f32[768,1024]{1,0:T(8,128)}, u32[]{:S(2)}) copy-start(f32[768,1024]{1,0:T(8,128)} %copy-done.27) | copy-start | bytes 9437188
  463.6 13.8 %copy-start.54 = (bf16[4,2,2,2,32,1024]{5,4,3,2,1,0:T(8,128)(2,1)S(1)}, bf16[4,2,2,2,32,1024]{5,4,3,2,1,0:T(8,128)(2,1)}, u32[]{:S(2)}) copy-start(bf16[4,2,2,2,32,1024]{5,4,3,2,1,0:T(8,128)(2,1)} %get-tuple-element.46) | copy-start | bytes 6291460
  477.3 4.6 copy-start.18
  477.3 4.6 copy-start.20
  477.4 5.9 copy-start.8
  483.3 5.2 copy-start.21
  483.3 5.2 copy-start.30
  488.5 3.6 copy-start.19
  488.5 3.6 copy-start.37
  492.1 5.2 copy-start.35
  497.3 1.4 copy-start.59
  498.7 8.8 %copy-start.32 = (f32[768,1024]{1,0:T(8,128)}, f32[768,1024]{1,0:T(8,128)S(1)}, u32[]{:S(2)}) copy-start(f32[768,1024]{1,0:T(8,128)S(1)} %subtract_multiply_fusion) | copy-start | bytes 9437188
  498.7 4.1 copy-start.52
  506.2 2.2 copy-start.53
  511.3 190.5 %copy-start.58 = (bf16[3,1,256,1024]{3,2,1,0:T(8,128)(2,1)S(1)}, bf16[3,1,256,1024]{3,2,1,0:T(8,128)(2,1)}, u32[]{:S(2)}) copy-start(bf16[3,1,256,1024]{3,2,1,0:T(8,128)(2,1)} %param.15) | copy-start | bytes 4718596
  711.5 117.3 %copy-start.33 = (f32[768,1024]{1,0:T(8,128)S(1)}, f32[768,1024]{1,0:T(8,128)}, u32[]{:S(2)}) copy-start(f32[768,1024]{1,0:T(8,128)} %copy-done.32) | copy-start | bytes 9437188
  828.8 9.6 %copy-start.41 = (f32[96,1024]{1,0:T(8,128)S(1)}, f32[96,1024]{1,0:T(8,128)}, u32[]{:S(2)}) copy-start(f32[96,1024]{1,0:T(8,128)} %get-tuple-element.65) | copy-start | bytes 1179652
  828.8 10.3 %copy-start.42 = (f32[32,3072]{1,0:T(8,128)S(1)}, f32[32,3072]{1,0:T(8,128)}, u32[]{:S(2)}) copy-start(f32[32,3072]{1,0:T(8,128)} %get-tuple-element.146) | copy-start | bytes 1179652
  828.8 11.1 %copy-start.46 = (f32[32,1024]{1,0:T(8,128)S(1)}, f32[32,1024]{1,0:T(8,128)}, u32[]{:S(2)}) copy-start(f32[32,1024]{1,0:T(8,128)} %get-tuple-element.147) | copy-start | bytes 393220
  828.8 11.7 %copy-start.45 = (f32[32,1024]{1,0:T(8,128)S(1)}, f32[32,1024]{1,0:T(8,128)}, u32[]{:S(2)}) copy-start(f32[32,1024]{1,0:T(8,128)} %get-tuple-element.148) | copy-start | bytes 393220
  828.8 12.4 %copy-start.43 = (f32[32,2048]{1,0:T(8,128)S(1)}, f32[32,2048]{1,0:T(8,128)}, u32[]{:S(2)}) copy-start(f32[32,2048]{1,0:T(8,128)} %get-tuple-element.149) | copy-start | bytes 786436
  828.8 13.1 %copy-start.44 = (f32[32,1024]{1,0:T(8,128)S(1)}, f32[32,1024]{1,0:T(8,128)}, u32[]{:S(2)}) copy-start(f32[32,1024]{1,0:T(8,128)} %get-tuple-element.150) | copy-start | bytes 393220
  828.8 13.7 %copy-start.40 = (f32[32,4096]{1,0:T(8,128)S(1)}, f32[32,4096]{1,0:T(8,128)}, u32[]{:S(2)}) copy-start(f32[32,4096]{1,0:T(8,128)} %get-tuple-element.151) | copy-start | bytes 1572868
  838.4 4.9 copy-start.39

commit v8 on v7

--- a/solution.py
+++ b/solution.py
@@ -850,7 +850,11 @@
 
     def launch(m, carry):
         cut_heads(rows_ref, m, 1, cut)
-        send_blocks(cut, gout, send_in, take_in, m)
+
+        @pl.when(m < 1)
+        def _():
+            send_blocks(cut, gout, send_in, take_in, m)
+
         return carry
 
     lax.fori_loop(0, micro, launch, 0)
@@ -861,6 +865,10 @@
 
     def one_micro(m, carry):
         take_blocks(cut, gout, send_in, take_in, m)
+
+        @pl.when(m + 1 < micro)
+        def _():
+            send_blocks(cut, gout, send_in, take_in, m + 1)
 
         def prepare(i, carry):
             rows = rows_at(i, block)

time: 849 us -> 857 us (level)
    pallas_call x1, Pallas kernels: 191 us -> 204 us  [self_backward(): pl.pallas_call(functools.partial(self_backward_kernel, heads, BLOCK, kind...]
where the time goes in v8:
time: 857 us; the launch traced here: 851 us
  Pallas kernels  708 us (83%)
  matrix products  99 us (12%)
  other arithmetic  22.1 us (3%)
  local copies, waits for them, and re-layouts  20.2 us (2%)
    pallas_call x1, Pallas kernels, self_forward(): pl.pallas_call(functools.partial(self_forward_kernel, heads, BLOCK, plan,...  288 us
    pallas_call x1, Pallas kernels, self_backward(): pl.pallas_call(functools.partial(self_backward_kernel, heads, BLOCK, kind...  204 us
    pallas_call x1, Pallas kernels, scatter_grads(): pl.pallas_call(functools.partial(scatter_kernel, kinds), in_specs=[pl.Blo...  110 us
    dot_general x7, matrix products, dot_nn(): lax.dot_general(a, b, (((1,), (0,)), ((), ())), preferred_element_type=f32)  48.7 us
    pallas_call x1, Pallas kernels, gather_first(): pl.pallas_call(functools.partial(gather_kernel, plan, len(shards)), in_sp...  44.6 us
    pallas_call x1, Pallas kernels, ffn_backward(): pl.pallas_call(ffn_backward_kernel, grid=(inner // piece,), in_specs=[who...  32.6 us
    dot_general x5, matrix products, dot_tn(): lax.dot_general(a, b, (((0,), (0,)), ((), ())), preferred_element_type=f32)  26.8 us
    dot_general x5, matrix products, dot_nt(): lax.dot_general(a, b, (((1,), (1,)), ((), ())), preferred_element_type=f32)  22.4 us

profile of v8, /device:TPU:0, one launch (start us, length us, event | category | flops | bytes accessed | tf_op | source)
XLA Modules:
  0.0 851.5 jit_solution(10253792494601399725)
XLA Ops:
  0.6 44.6 %gather_first.1 = bf16[4,2,2,2,32,3072]{5,4,3,2,1,0:T(8,128)(2,1)} custom-call(bf16[32,3072]{1,0:T(8,128)(2,1)} %refs_0_.1), custom_call_target="tpu_custom_call" | custom-call | tf_op jit(solution)/shard_map/gather_first/pallas_call | solution.py:654
  45.4 9.1 %convolution_convert_fusion.1 = bf16[768,3072]{1,0:T(8,128)(2,1)} fusion(bf16[768,1024]{1,0:T(8,128)(2,1)} %bitcast.169, bf16[1024,3072]{1,0:T(8,128)(2,1)} %bitcast.138), kind=kOutput, calls=%fused_computation.13 | convolution fusion | flops 4834197504 | bytes 12582912 | tf_op jit(solution)/shard_map/dot_general | solution.py:31
  54.6 0.2 convolution_minimum_fusion.3
  54.8 0.2 convolution_minimum_fusion.2
  55.0 0.2 convolution_minimum_fusion.1
  55.1 0.2 convolution_minimum_fusion
  55.3 0.2 fusion.25
  55.5 0.2 fusion.18
  55.8 1.3 copy.32
  57.1 0.5 broadcast_in_dim.12
  57.6 0.5 reshape.249.refs_1_.refs_2_
  58.2 288.3 %self_forward.1 = (bf16[3,3,2048,128]{3,2,1,0:T(8,128)(2,1)}, bf16[3,1,2048,128]{3,2,1,0:T(8,128)(2,1)S(1)}, f32[3,8,2,256]{3,2,1,0:T(2,128)S(1)}, bf16[3,256,10...) custom-call(bf16[3,256,3072]{2,1,0:T(8,128)(2,1)} %bitcast.142, ...), custom_call_target="tpu_custom_call" | custom-call | tf_op jit(solution)/shard_map/self_forward/pallas_call | solution.py:801
  346.6 4.5 fusion.35
  351.2 0.4 multiply_reduce_fusion.6
  351.6 0.3 slice_reduce_fusion.1
  351.9 1.0 copy-done.27
  353.0 4.5 convolution_convert_fusion.10
  357.8 3.6 convolution_convert_fusion.3
  361.5 15.4 %cross_forward.1 = (bf16[3,256,1024]{2,1,0:T(8,128)(2,1)S(1)}, f32[3,8,2,256]{3,2,1,0:T(2,128)S(1)}) custom-call(s32[3]{0:T(128)S(1)} %bitcast.124, bf16[3,256,1024]{2,1,0:T(8,128)(2,1)S(1)} %bitcast.117, bf16[3,256,2048]{2,1,0:T(8,128)(2,1)S(1)} %bitcast.115), custom_call_target="tpu_custom_call" | custom-call | tf_op jit(solution)/shard_map/cross_forward/pallas_call | solution.py:1017
  376.9 2.1 fusion.36
  379.1 1.6 copy-done.22
  380.7 0.4 multiply_reduce_fusion.5
  381.3 2.6 fusion.17.hidden_ref
  384.0 17.7 %fusion.8 = (bf16[768,4096]{1,0:T(8,128)(2,1)}, bf16[768,4096]{1,0:T(8,128)(2,1)S(1)}) fusion(bf16[768,1024]{1,0:T(8,128)(2,1)S(1)} %fusion.17.hidden_ref, bf16[1024,4096]{1,0:T(8,128)(2,1)} %bitcast.132), kind=kOutput, calls=%fused_computation.10 | convolution fusion | flops 6502219776 | bytes 22544384 | tf_op jit(solution)/shard_map/dot_general | solution.py:31
  401.8 7.0 fusion.37
  408.9 1.6 copy-done.25
  410.5 0.4 multiply_reduce_fusion.4
  411.0 3.6 fusion.15
  414.6 0.8 convert_reduce_fusion
  415.4 3.4 fusion.33.branch_ref
  418.8 32.6 %ffn_backward.1 = (bf16[4096,1024]{1,0:T(8,128)(2,1)}, bf16[1024,4096]{1,0:T(8,128)(2,1)}, f32[768,1024]{1,0:T(8,128)}) custom-call(bf16[768,1024]{1,0:T(8,128)(2,1)S(1)} %fusion.33.branch_ref, bf16[768,1024]{1,0:T(8,128)(2,1)S(1)} %copy-done.1, bf16[768,4096]{1,0:T(8,128)(2,1)} %copy-done.31, bf16[768,4096]{1,0:T(8,128)(2,1)} %get-tuple-element.54.slope_ref, ...), custom_call_target="tpu_custom_call" | custom-call | tf_op jit(solution)/shard_map/ffn_backward/pallas_call | solution.py:1134
  451.5 7.4 multiply_reduce_fusion
  459.0 1.1 subtract_multiply_fusion.1
  460.0 0.5 copy-done.56
  460.6 1.8 convolution_convert_fusion.9
  462.4 0.7 copy-done.3
  463.1 0.5 copy-done.7
  463.6 13.7 %cross_backward.1 = (bf16[3,256,1024]{2,1,0:T(8,128)(2,1)S(1)}, bf16[3,256,2048]{2,1,0:T(8,128)(2,1)S(1)}) custom-call(s32[3]{0:T(128)S(1)} %bitcast.125, bf16[3,256,1024]{2,1,0:T(8,128)(2,1)S(1)} %bitcast.118, bf16[3,256,2048]{2,1,0:T(8,128)(2,1)S(1)} %bitcast.116, bf16[3,256,1024]{2,1,0:T(8,128)(2,1)S(1)} %copy-done.7, ...), custom_call_target="tpu_custom_call" | custom-call | tf_op jit(solution)/shard_map/cross_backward/pallas_call | solution.py:1088
  477.4 4.6 multiply_reduce_fusion.1
  482.5 0.8 stack.27
  483.3 5.2 convolution_convert_fusion.4
  488.5 3.6 convolution_convert_fusion.5
  492.1 5.1 convolution_convert_fusion.2
  497.3 1.2 subtract_multiply_fusion
  498.5 0.2 copy-done.59
  498.7 3.2 convolution_convert_fusion.6
  501.9 0.9 copy-done.52
  502.8 3.4 convolution_convert_fusion.7
  506.2 1.3 copy.34
  507.5 0.8 copy-done.53
  508.4 3.0 convolution_convert_fusion.8
  511.3 203.9 %self_backward.1 = (bf16[3,256,3072]{2,1,0:T(8,128)(2,1)}, f32[32,4096]{1,0:T(8,128)}, f32[128,1024]{1,0:T(8,128)}, f32[96,1024]{1,0:T(8,128)}) custom-call(bf16[3,256,1024]{2,1,0:T(8,128)(2,1)} %bitcast.148, bf16[3,3,2048,128]{3,2,1,0:T(8,128)(2,1)} %get-tuple-element.58.refs_1_, f32[3,8,8,2,256]{4,3,2,1,0:T(2,128)} %copy-done.4, ...), custom_call_target="tpu_custom_call" | custom-call | tf_op jit(solution)/shard_map/self_backward/pallas_call | solution.py:958
  715.2 9.6 %convolution_convert_fusion = bf16[3072,1024]{0,1:T(8,128)(2,1)} fusion(bf16[768,3072]{1,0:T(8,128)(2,1)} %bitcast.159, bf16[768,1024]{1,0:T(8,128)(2,1)S(1)} %bitcast.171), kind=kOutput, calls=%fused_computation.12 | convolution fusion | flops 4834983936 | bytes 12582912 | tf_op jit(solution)/shard_map/dot_general | solution.py:39
  724.8 109.7 %scatter_grads.1 = (f32[32,3072]{1,0:T(8,128)}, f32[32,1024]{1,0:T(8,128)}, f32[32,2048]{1,0:T(8,128)}, f32[32,1024]{1,0:T(8,128)}, f32[32,1024]{1,0:T(8,128)}, /*index=5*/f32[6,32]{1,0:T(8,128)}) custom-call(bf16[4,2,2,2,32,3072]{5,4,3,2,1,0:T(8,128)(2,1)} %bitcast.140, bf16[4,2,2,2,32,1024]{5,4,3,2,1,0:T(8,128)(2,1)} %bitcast.146, ...), custom_call_target="tpu_custom_call" | custom-call | tf_op jit(solution)/shard_map/scatter_grads/pallas_call | solution.py:470
  834.5 1.3 fusion.34
  835.9 9.6 %add_convert_fusion = bf16[768,1024]{1,0:T(8,128)(2,1)} fusion(f32[768,1024]{1,0:T(8,128)S(1)} %copy-done.33, bf16[768,3072]{1,0:T(8,128)(2,1)} %bitcast.160, bf16[1024,3072]{1,0:T(8,128)(2,1)} %bitcast.139), kind=kOutput, calls=%fused_computation.29 | convolution fusion | flops 4834197504 | bytes 15728640 | tf_op jit(solution)/shard_map/dot_general | solution.py:35
  845.5 0.7 convert_element_type.115
  846.2 0.7 copy.51
  847.0 0.7 copy.52
  847.6 0.7 copy.53
  848.3 0.7 copy.54
  849.0 0.7 copy.55
  849.6 0.8 copy.56
  850.4 0.8 copy.57
  (146 shorter events, 1.6 us)
Async XLA Ops:
  45.3 9.2 %copy-start.47 = (s32[3,1,16]{2,1,0:T(1,128)S(1)}, s32[3,1,16]{2,1,0:T(1,128)}, u32[]{:S(2)}) copy-start(s32[3,1,16]{2,1,0:T(1,128)} %param.18) | copy-start | bytes 580
  45.3 9.2 %copy-start.48 = (s32[3,1,13]{2,1,0:T(1,128)S(1)}, s32[3,1,13]{2,1,0:T(1,128)}, u32[]{:S(2)}) copy-start(s32[3,1,13]{2,1,0:T(1,128)} %param.19) | copy-start | bytes 472
  45.3 12.8 %copy-start.49 = (bf16[3,32]{1,0:T(4,128)(2,1)S(1)}, bf16[3,32]{1,0:T(4,128)(2,1)}, u32[]{:S(2)}) copy-start(bf16[3,32]{1,0:T(4,128)(2,1)} %param.29) | copy-start | bytes 580
  45.3 12.8 %copy-start.50 = (bf16[3,32]{1,0:T(4,128)(2,1)S(1)}, bf16[3,32]{1,0:T(4,128)(2,1)}, u32[]{:S(2)}) copy-start(bf16[3,32]{1,0:T(4,128)(2,1)} %param.28) | copy-start | bytes 580
  45.3 12.8 %copy-start.9 = (bf16[32,4096]{1,0:T(8,128)(2,1)S(1)}, bf16[32,4096]{1,0:T(8,128)(2,1)}, u32[]{:S(2)}) copy-start(bf16[32,4096]{1,0:T(8,128)(2,1)} %refs_8_.1) | copy-start | bytes 786436
  45.3 12.8 %copy-start.10 = (bf16[128,1024]{1,0:T(8,128)(2,1)S(1)}, bf16[128,1024]{1,0:T(8,128)(2,1)}, u32[]{:S(2)}) copy-start(bf16[128,1024]{1,0:T(8,128)(2,1)} %refs_9_.1) | copy-start | bytes 786436
  45.4 12.8 %copy-start.11 = (bf16[3,1,32,1024]{3,2,1,0:T(8,128)(2,1)S(1)}, bf16[3,1,32,1024]{3,2,1,0:T(8,128)(2,1)}, u32[]{:S(2)}) copy-start(bf16[3,1,32,1024]{3,2,1,0:T(8,128)(2,1)} %param.16) | copy-start | bytes 589828
  45.4 12.8 %copy-start.12 = (bf16[32,2048]{1,0:T(8,128)(2,1)S(1)}, bf16[32,2048]{1,0:T(8,128)(2,1)}, u32[]{:S(2)}) copy-start(bf16[32,2048]{1,0:T(8,128)(2,1)} %refs_5_.1) | copy-start | bytes 393220
  45.4 12.8 %copy-start.13 = (bf16[32,1024]{1,0:T(8,128)(2,1)S(1)}, bf16[32,1024]{1,0:T(8,128)(2,1)}, u32[]{:S(2)}) copy-start(bf16[32,1024]{1,0:T(8,128)(2,1)} %refs_2_.1) | copy-start | bytes 196612
  45.4 12.8 %copy-start.14 = (bf16[32,1024]{1,0:T(8,128)(2,1)S(1)}, bf16[32,1024]{1,0:T(8,128)(2,1)}, u32[]{:S(2)}) copy-start(bf16[32,1024]{1,0:T(8,128)(2,1)} %refs_4_.1) | copy-start | bytes 196612
  45.4 12.8 %copy-start.15 = (bf16[32,1024]{1,0:T(8,128)(2,1)S(1)}, bf16[32,1024]{1,0:T(8,128)(2,1)}, u32[]{:S(2)}) copy-start(bf16[32,1024]{1,0:T(8,128)(2,1)} %refs_7_.1) | copy-start | bytes 196612
  58.1 293.0 %copy-start.4 = (f32[3,8,8,2,256]{4,3,2,1,0:T(2,128)}, f32[3,8,8,2,256]{4,3,2,1,0:T(2,128)S(1)}, u32[]{:S(2)}) copy-start(f32[3,8,8,2,256]{4,3,2,1,0:T(2,128)S(1)} %reshape.249.refs_1_.refs_2_) | copy-start | bytes 1179652
  58.1 288.5 %copy-start.57 = (bf16[3,1,256,1024]{3,2,1,0:T(8,128)(2,1)S(1)}, bf16[3,1,256,1024]{3,2,1,0:T(8,128)(2,1)}, u32[]{:S(2)}) copy-start(bf16[3,1,256,1024]{3,2,1,0:T(8,128)(2,1)} %param.15) | copy-start | bytes 4718596
  346.5 4.6 copy-start.5
  346.6 4.6 copy-start.16
  351.1 1.7 copy-start.27
  353.0 4.6 copy-start.38
  353.0 4.7 copy-start.51
  357.6 3.9 copy-start.2
  357.7 3.7 copy-start.36
  357.8 3.7 copy-start.17
  357.8 19.1 %copy-start.55 = (bf16[4,2,2,2,32,1024]{5,4,3,2,1,0:T(8,128)(2,1)S(1)}, bf16[4,2,2,2,32,1024]{5,4,3,2,1,0:T(8,128)(2,1)}, u32[]{:S(2)}) copy-start(bf16[4,2,2,2,32,1024]{5,4,3,2,1,0:T(8,128)(2,1)} %get-tuple-element.50) | copy-start | bytes 6291460
  361.4 15.5 %copy-start.28 = (f32[768,1024]{1,0:T(8,128)S(1)}, f32[768,1024]{1,0:T(8,128)}, u32[]{:S(2)}) copy-start(f32[768,1024]{1,0:T(8,128)} %copy-done.27) | copy-start | bytes 9437188
  376.9 2.2 copy-start.6
  379.1 1.7 copy-start.22
  381.3 20.4 %slice-start = ((s8[8388608]{0:T(1024)(128)(4,1)}), s8[4194304]{0:T(1024)(128)(4,1)S(1)}, s32[]{:S(2)}) async-start(s8[8388608]{0:T(1024)(128)(4,1)} %bitcast.135), calls=%async_computation | async-start | bytes 8388608
  383.9 17.8 %copy-start = (bf16[768,1024]{1,0:T(8,128)(2,1)}, bf16[768,1024]{1,0:T(8,128)(2,1)S(1)}, u32[]{:S(2)}) copy-start(bf16[768,1024]{1,0:T(8,128)(2,1)S(1)} %fusion.17.hidden_ref) | copy-start | bytes 4718596
  384.0 17.8 %copy-start.23 = (f32[768,1024]{1,0:T(8,128)S(1)}, f32[768,1024]{1,0:T(8,128)}, u32[]{:S(2)}) copy-start(f32[768,1024]{1,0:T(8,128)} %copy-done.22) | copy-start | bytes 9437188
  384.0 17.8 %slice-start.1 = ((s8[8388608]{0:T(1024)(128)(4,1)}), s8[4194304]{0:T(1024)(128)(4,1)S(1)}, s32[]{:S(2)}) async-start(s8[8388608]{0:T(1024)(128)(4,1)} %bitcast.135), calls=%async_computation.1 | async-start | bytes 8388608
  401.7 7.1 copy-start.31
  408.8 1.6 copy-start.25
  411.0 3.6 copy-start.26
  415.4 3.4 copy-start.1
  451.5 7.4 copy-start.24
  459.0 1.6 copy-start.56
  460.5 16.8 %copy-start.34 = (f32[768,1024]{1,0:T(8,128)}, f32[768,1024]{1,0:T(8,128)S(1)}, u32[]{:S(2)}) copy-start(f32[768,1024]{1,0:T(8,128)S(1)} %subtract_multiply_fusion.1) | copy-start | bytes 9437188
  460.6 2.5 copy-start.3
  460.6 3.0 copy-start.7
  463.6 13.8 %copy-start.29 = (f32[768,1024]{1,0:T(8,128)S(1)}, f32[768,1024]{1,0:T(8,128)}, u32[]{:S(2)}) copy-start(f32[768,1024]{1,0:T(8,128)} %copy-done.27) | copy-start | bytes 9437188
  463.6 13.8 %copy-start.54 = (bf16[4,2,2,2,32,1024]{5,4,3,2,1,0:T(8,128)(2,1)S(1)}, bf16[4,2,2,2,32,1024]{5,4,3,2,1,0:T(8,128)(2,1)}, u32[]{:S(2)}) copy-start(bf16[4,2,2,2,32,1024]{5,4,3,2,1,0:T(8,128)(2,1)} %get-tuple-element.46) | copy-start | bytes 6291460
  477.3 4.6 copy-start.18
  477.3 4.6 copy-start.20
  477.4 5.9 copy-start.8
  483.3 5.2 copy-start.21
  483.3 5.2 copy-start.30
  488.5 3.6 copy-start.19
  488.5 3.6 copy-start.37
  492.1 5.2 copy-start.35
  497.3 1.4 copy-start.59
  498.7 8.8 %copy-start.32 = (f32[768,1024]{1,0:T(8,128)}, f32[768,1024]{1,0:T(8,128)S(1)}, u32[]{:S(2)}) copy-start(f32[768,1024]{1,0:T(8,128)S(1)} %subtract_multiply_fusion) | copy-start | bytes 9437188
  498.7 4.1 copy-start.52
  506.2 2.2 copy-start.53
  511.3 203.9 %copy-start.58 = (bf16[3,1,256,1024]{3,2,1,0:T(8,128)(2,1)S(1)}, bf16[3,1,256,1024]{3,2,1,0:T(8,128)(2,1)}, u32[]{:S(2)}) copy-start(bf16[3,1,256,1024]{3,2,1,0:T(8,128)(2,1)} %param.15) | copy-start | bytes 4718596
  724.8 111.0 %copy-start.33 = (f32[768,1024]{1,0:T(8,128)S(1)}, f32[768,1024]{1,0:T(8,128)}, u32[]{:S(2)}) copy-start(f32[768,1024]{1,0:T(8,128)} %copy-done.32) | copy-start | bytes 9437188
  835.9 9.6 %copy-start.41 = (f32[96,1024]{1,0:T(8,128)S(1)}, f32[96,1024]{1,0:T(8,128)}, u32[]{:S(2)}) copy-start(f32[96,1024]{1,0:T(8,128)} %get-tuple-element.65) | copy-start | bytes 1179652
  835.9 10.3 %copy-start.42 = (f32[32,3072]{1,0:T(8,128)S(1)}, f32[32,3072]{1,0:T(8,128)}, u32[]{:S(2)}) copy-start(f32[32,3072]{1,0:T(8,128)} %get-tuple-element.146) | copy-start | bytes 1179652
  835.9 11.1 %copy-start.46 = (f32[32,1024]{1,0:T(8,128)S(1)}, f32[32,1024]{1,0:T(8,128)}, u32[]{:S(2)}) copy-start(f32[32,1024]{1,0:T(8,128)} %get-tuple-element.147) | copy-start | bytes 393220
  835.9 11.7 %copy-start.45 = (f32[32,1024]{1,0:T(8,128)S(1)}, f32[32,1024]{1,0:T(8,128)}, u32[]{:S(2)}) copy-start(f32[32,1024]{1,0:T(8,128)} %get-tuple-element.148) | copy-start | bytes 393220
  835.9 12.4 %copy-start.43 = (f32[32,2048]{1,0:T(8,128)S(1)}, f32[32,2048]{1,0:T(8,128)}, u32[]{:S(2)}) copy-start(f32[32,2048]{1,0:T(8,128)} %get-tuple-element.149) | copy-start | bytes 786436
  835.9 13.1 %copy-start.44 = (f32[32,1024]{1,0:T(8,128)S(1)}, f32[32,1024]{1,0:T(8,128)}, u32[]{:S(2)}) copy-start(f32[32,1024]{1,0:T(8,128)} %get-tuple-element.150) | copy-start | bytes 393220
  835.9 13.7 %copy-start.40 = (f32[32,4096]{1,0:T(8,128)S(1)}, f32[32,4096]{1,0:T(8,128)}, u32[]{:S(2)}) copy-start(f32[32,4096]{1,0:T(8,128)} %get-tuple-element.151) | copy-start | bytes 1572868
  845.5 4.9 copy-start.39
